TPU v7x, 512 devices: a whole 4x8x8 slice. The times are simulated.
512 devices in a mesh: blk: 64 (over y_lo, z, core), rows: 8 (over x, y_hi).
Axes of the slice: x: 4, y: 8 (y_hi: 2, y_lo: 4; y = y_hi * 4 + y_lo), z: 8, core: 2. Of those that a mesh axis runs over, the one named last changes fastest.
Arguments:
- points: float32 [32, 131072], P(None, ('blk', 'rows')), may hold values from -6 to 6
- lengthscale: float32 [32], replicated, may hold values from 4 to 12
- noise_var: float32 [131072], P(('blk', 'rows')), may hold values from 0.5 to 2
- targets: float32 [64, 131072], P(None, ('blk', 'rows')), may hold values from -6 to 6
Outputs:
- solution: float32 [64, 131072], P(None, ('blk', 'rows'))
- residual: float32 [64, 131072], P(None, ('blk', 'rows'))
All inputs are finite; a program needn't handle non-finite values.
Results may differ from a plain program's by a relative error of at most 0.011.
Values may be sent and summed in bfloat16 or wider, within the bound.
No kernel may reach another device: no remote copies, remote signals or barrier semaphores. Data moves between devices by JAX's collectives and lax.ppermute only.
A program may use at most 64 MiB of HBM per device.

v0:
```python
import math

import jax
import jax.numpy as jnp
from jax import lax
from jax.sharding import PartitionSpec as P

BAND = 4
ITERS = 2


ROOT_FIVE = math.sqrt(5.0)


def passed_along(block, axis, distance):
    devices = range(lax.axis_size(axis))
    route = [((i - distance) % len(devices), i) for i in devices]
    return lax.ppermute(block, axis, route)


def matern_block(row_points, row_squares, col_points, col_squares, tapering):
    inner_prod = lax.dot_general(
        row_points,
        col_points,
        (((0,), (0,)), ((), ())),
        precision=lax.Precision.HIGHEST,
        preferred_element_type=jnp.float32,
    )
    dist_sq = row_squares[:, None] + col_squares[None, :] - 2.0 * inner_prod
    scaled = ROOT_FIVE * jnp.sqrt(jnp.maximum(dist_sq, 0.0))
    values = (1.0 + scaled + scaled * scaled / 3.0) * jnp.exp(-scaled) * tapering
    return values.astype(jnp.bfloat16)


def forward(vectors, kernel_tile):
    return lax.dot_general(
        vectors, kernel_tile, (((1,), (1,)), ((), ())), preferred_element_type=jnp.float32
    )


def tile_apply(row_points, row_squares, col_points, col_squares, col_dir, tapering):
    columns = col_points.shape[1]
    width = math.gcd(columns, 512)
    pieces = columns // width
    piece_points = col_points.reshape(col_points.shape[0], pieces, width).transpose(1, 0, 2)
    piece_squares = col_squares.reshape(pieces, width)
    piece_dir = col_dir.reshape(col_dir.shape[0], pieces, width).transpose(1, 0, 2)
    start = jnp.zeros((col_dir.shape[0], row_points.shape[1]), jnp.float32)

    def one_piece(total, inputs):
        some_points, some_squares, some_dir = inputs
        kernel_tile = matern_block(row_points, row_squares, some_points, some_squares, tapering)
        total = total + forward(some_dir, kernel_tile)
        return (total, None)

    total, owed = lax.scan(one_piece, start, (piece_points, piece_squares, piece_dir))
    return (total, None)


def body(points, lengthscale, noise_var, targets):
    scaled = points / lengthscale[:, None]
    squares = jnp.sum(scaled * scaled, axis=0)
    group_points = lax.all_gather(scaled, "rows", axis=1, tiled=True)
    group_squares = jnp.sum(group_points * group_points, axis=0)
    ahead_points = []
    behind_points = []
    for distance in range(1, BAND):
        moved = passed_along(group_points, "blk", -distance)
        ahead_points.append((moved, jnp.sum(moved * moved, axis=0)))
        moved_back = passed_along(group_points, "blk", distance)
        behind_points.append((moved_back, jnp.sum(moved_back * moved_back, axis=0)))
    solution = jnp.zeros_like(targets)
    residual = targets
    direction = targets
    norm_now = lax.psum(jnp.sum(residual * residual, axis=1), ("blk", "rows"))
    for iteration in range(ITERS):
        rounded = direction.astype(jnp.bfloat16)
        group_dir = lax.all_gather(rounded, "rows", axis=1, tiled=True)
        summed = noise_var[None, :] * direction
        own_part, unused = tile_apply(scaled, squares, group_points, group_squares, group_dir, 1.0)
        summed = summed + own_part
        for apply_distance in range(1, BAND):
            tapering = (BAND - apply_distance) / BAND
            far_points, far_squares = ahead_points[apply_distance - 1]
            far_dir = passed_along(group_dir, "blk", -apply_distance)
            ahead_part, unused = tile_apply(
                scaled, squares, far_points, far_squares, far_dir, tapering
            )
            summed = summed + ahead_part
            back_points, back_squares = behind_points[apply_distance - 1]
            back_dir = passed_along(group_dir, "blk", apply_distance)
            back_part, unused = tile_apply(
                scaled, squares, back_points, back_squares, back_dir, tapering
            )
            summed = summed + back_part
        curvature = lax.psum(jnp.sum(direction * summed, axis=1), ("blk", "rows"))
        step_size = norm_now / curvature
        solution = solution + step_size[:, None] * direction
        residual = residual - step_size[:, None] * summed
        norm_next = lax.psum(jnp.sum(residual * residual, axis=1), ("blk", "rows"))
        direction = residual + (norm_next / norm_now)[:, None] * direction
        norm_now = norm_next
    return (solution, residual)


def solution(mesh):
    placed = (P(None, ("blk", "rows")), P(), P(("blk", "rows")), P(None, ("blk", "rows")))
    return jax.shard_map(
        body,
        mesh=mesh,
        in_specs=placed,
        out_specs=(P(None, ("blk", "rows")), P(None, ("blk", "rows"))),
        check_vma=False,
    )
```

profile of v0, /device:TPU:1, one launch (start us, length us, event | category | flops | bytes accessed | tf_op | source)
XLA Modules:
  0.0 589.6 jit_solution(8534332552060348260)
XLA Ops:
  1.5 40.0 %all_gather.10 = f32[32,2048]{1,0:T(8,128)S(1)} all-gather(f32[32,256]{1,0:T(8,128)S(1)} %get-tuple-element.2087), channel_id=1, replica_groups=mesh['blk'=64,'rows'=8] {'rows'}, dimensions={1}, use_global_device_ids=true | all-gather | bytes 294912 | tf_op jit(solution)/shard_map/all_gather | solution.py:63
  41.4 13.5 %collective-permute-start.1 = (f32[32,2048]{1,0:T(8,128)S(1)}, f32[32,2048]{1,0:T(8,128)S(1)}, u32[]{:S(2)}, u32[]{:S(2)}) collective-permute-start(f32[32,2048]{1,0:T(8,128)S(1)} %all_gather.10), channel_id=1, source_target_pairs={{8,0},{16,8},{24,16},{32,24},{40,32},{48,40},{56,48},{64,56},{72,6... | collective-permute-start | bytes 786440 | tf_op jit(solution)/shard_map/ppermute | solution.py:18
  56.9 38.7 %all_gather.9 = bf16[64,2048]{1,0:T(8,128)(2,1)S(1)} all-gather(bf16[64,256]{1,0:T(8,128)(2,1)S(1)} %convert_element_type.48), channel_id=1, replica_groups=mesh['blk'=64,'rows'=8] {'rows'}, dimensions={1}, use_global_device_ids=true | all-gather | bytes 294912 | tf_op jit(solution)/shard_map/all_gather | solution.py:78
  95.7 8.2 %collective-permute-start = (bf16[64,2048]{1,0:T(8,128)(2,1)S(1)}, bf16[64,2048]{1,0:T(8,128)(2,1)S(1)}, u32[]{:S(2)}, u32[]{:S(2)}) collective-permute-start(bf16[64,2048]{1,0:T(8,128)(2,1)S(1)} %all_gather.9), channel_id=1, source_target_pairs={{8,0},{16,8},{24,16},{32,24},{40,32},{48,40},{56,48},{64,56},{72,6... | collective-permute-start | bytes 786440 | tf_op jit(solution)/shard_map/ppermute | solution.py:18
  105.8 8.0 %collective-permute-start.5 = (f32[32,2048]{1,0:T(8,128)S(1)}, f32[32,2048]{1,0:T(8,128)S(1)}, u32[]{:S(2)}, u32[]{:S(2)}) collective-permute-start(f32[32,2048]{1,0:T(8,128)S(1)} %all_gather.10), channel_id=1, source_target_pairs={{16,0},{24,8},{32,16},{40,24},{48,32},{56,40},{64,48},{72,56},{80,... | collective-permute-start | bytes 786440 | tf_op jit(solution)/shard_map/ppermute | solution.py:18
  124.6 4.7 while.155
  132.0 8.8 %collective-permute-start.9 = (f32[32,2048]{1,0:T(8,128)S(1)}, f32[32,2048]{1,0:T(8,128)S(1)}, u32[]{:S(2)}, u32[]{:S(2)}) collective-permute-start(f32[32,2048]{1,0:T(8,128)S(1)} %all_gather.10), channel_id=1, source_target_pairs={{24,0},{32,8},{40,16},{48,24},{56,32},{64,40},{72,48},{80,56},{88,... | collective-permute-start | bytes 786440 | tf_op jit(solution)/shard_map/ppermute | solution.py:18
  142.0 8.1 %while.156 = (s32[]{:T(128)}, f32[64,256]{1,0:T(8,128)S(1)}, bf16[4,64,512]{2,1,0:T(8,128)(2,1)S(1)}, f32[256]{0:T(256)S(1)}, f32[4,512]{1,0:T(4,128)S(1)}, /*in...) while((s32[]{:T(128)}, f32[64,256]{1,0:T(8,128)S(1)}, ...), condition=%wide.region_11.12_spmd.clone, body=%wide.region_10.11_spmd.clone.sunk | while | flops 68845568 | bytes 826991 | solution.py:56
  158.5 8.1 %while.157 = (s32[]{:T(128)}, f32[64,256]{1,0:T(8,128)S(1)}, bf16[4,64,512]{2,1,0:T(8,128)(2,1)S(1)}, f32[256]{0:T(256)S(1)}, f32[4,512]{1,0:T(4,128)S(1)}, /*in...) while((s32[]{:T(128)}, f32[64,256]{1,0:T(8,128)S(1)}, ...), condition=%wide.region_14.15_spmd.clone, body=%wide.region_13.14_spmd.clone.sunk | while | flops 68845568 | bytes 826991 | solution.py:56
  169.8 4.7 while.158
  175.8 4.7 while.159
  183.5 4.7 while.160
  189.1 96.5 %all-reduce = (f32[64]{0:T(128)S(1)}, f32[64]{0:T(128)S(1)}) all-reduce(f32[64]{0:T(128)S(1)} %get-tuple-element.920, f32[64]{0:T(128)S(1)} %get-tuple-element.919), channel_id=1, replica_groups=mesh['blk'=64,'rows'=8] {'blk','rows'}, use_global_device_ids=true, to_apply=%region_1.0 | all-reduce | flops 128 | bytes 1024 | tf_op jit(solution)/shard_map/psum | solution.py:75
  285.8 93.8 %psum.30 = f32[64]{0:T(128)S(1)} all-reduce(f32[64]{0:T(128)S(1)} %multiply_reduce_fusion.8), channel_id=1, replica_groups=mesh['blk'=64,'rows'=8] {'blk','rows'}, use_global_device_ids=true, to_apply=%region_27.28 | all-reduce | flops 64 | bytes 512 | tf_op jit(solution)/shard_map/psum | solution.py:100
  379.6 39.1 %all_gather.11 = bf16[64,2048]{1,0:T(8,128)(2,1)S(1)} all-gather(bf16[64,256]{1,0:T(8,128)(2,1)S(1)} %get-tuple-element.1121), channel_id=1, replica_groups=mesh['blk'=64,'rows'=8] {'rows'}, dimensions={1}, use_global_device_ids=true | all-gather | bytes 294912 | tf_op jit(solution)/shard_map/all_gather | solution.py:78
  418.7 8.6 %collective-permute-start.12 = (bf16[64,2048]{1,0:T(8,128)(2,1)S(1)}, bf16[64,2048]{1,0:T(8,128)(2,1)}, u32[]{:S(2)}, u32[]{:S(2)}) collective-permute-start(bf16[64,2048]{1,0:T(8,128)(2,1)S(1)} %all_gather.11), channel_id=1, source_target_pairs={{8,0},{16,8},{24,16},{32,24},{40,32},{48,40},{56,48},{64,56},{72,6... | collective-permute-start | bytes 786440 | tf_op jit(solution)/shard_map/ppermute | solution.py:18
  430.0 6.5 %collective-permute-start.14 = (bf16[64,2048]{1,0:T(8,128)(2,1)S(1)}, bf16[64,2048]{1,0:T(8,128)(2,1)}, u32[]{:S(2)}, u32[]{:S(2)}) collective-permute-start(bf16[64,2048]{1,0:T(8,128)(2,1)S(1)} %all_gather.11), channel_id=1, source_target_pairs={{16,0},{24,8},{32,16},{40,24},{48,32},{56,40},{64,48},{72,56},{80,... | collective-permute-start | bytes 786440 | tf_op jit(solution)/shard_map/ppermute | solution.py:18
  450.5 4.7 while.162
  456.2 8.1 %while.163 = (s32[]{:T(128)}, f32[64,256]{1,0:T(8,128)S(1)}, bf16[4,64,512]{2,1,0:T(8,128)(2,1)S(1)}, f32[256]{0:T(256)S(1)}, f32[4,512]{1,0:T(4,128)S(1)}, /*in...) while((s32[]{:T(128)}, f32[64,256]{1,0:T(8,128)S(1)}, ...), condition=%wide.region_33.34_spmd.clone, body=%wide.region_32.33_spmd.clone.sunk | while | flops 68845568 | bytes 826991 | solution.py:56
  465.3 8.1 %while.164 = (s32[]{:T(128)}, f32[64,256]{1,0:T(8,128)S(1)}, bf16[4,64,512]{2,1,0:T(8,128)(2,1)S(1)}, f32[256]{0:T(256)S(1)}, f32[4,512]{1,0:T(4,128)S(1)}, /*in...) while((s32[]{:T(128)}, f32[64,256]{1,0:T(8,128)S(1)}, ...), condition=%wide.region_35.36_spmd.clone, body=%wide.region_34.35_spmd.clone.sunk | while | flops 68845568 | bytes 826991 | solution.py:56
  473.4 4.7 while.165
  478.2 4.7 while.166
  482.9 4.7 while.167
  487.8 101.1 %psum.31 = f32[64]{0:T(128)S(1)} all-reduce(f32[64]{0:T(128)S(1)} %get-tuple-element.1119), channel_id=1, replica_groups=mesh['blk'=64,'rows'=8] {'blk','rows'}, use_global_device_ids=true, to_apply=%region_43.44 | all-reduce | flops 64 | bytes 512 | tf_op jit(solution)/shard_map/psum | solution.py:96
  (270 shorter events, 132.5 us)
Async XLA Ops:
  1.5 55.4 %copy-start = (f32[64,256]{1,0:T(8,128)S(1)}, f32[64,256]{1,0:T(8,128)}, u32[]{:S(2)}) copy-start(f32[64,256]{1,0:T(8,128)} %param.35) | copy-start | bytes 196612
  41.4 77.5 %collective-permute-start.1 = (f32[32,2048]{1,0:T(8,128)S(1)}, f32[32,2048]{1,0:T(8,128)S(1)}, u32[]{:S(2)}, u32[]{:S(2)}) collective-permute-start(f32[32,2048]{1,0:T(8,128)S(1)} %all_gather.10), channel_id=1, source_target_pairs={{8,0},{16,8},{24,16},{32,24},{40,32},{48,40},{56,48},{64,56},{72,6... | collective-permute-start | bytes 786440 | tf_op jit(solution)/shard_map/ppermute | solution.py:18
  55.0 74.3 %collective-permute-start.3 = (f32[32,2048]{1,0:T(8,128)S(1)}, f32[32,2048]{1,0:T(8,128)S(1)}, u32[]{:S(2)}, u32[]{:S(2)}) collective-permute-start(f32[32,2048]{1,0:T(8,128)S(1)} %all_gather.10), channel_id=1, source_target_pairs={{504,0},{0,8},{8,16},{16,24},{24,32},{32,40},{40,48},{48,56},{56,6... | collective-permute-start | bytes 786440 | tf_op jit(solution)/shard_map/ppermute | solution.py:18
  95.7 26.6 %collective-permute-start = (bf16[64,2048]{1,0:T(8,128)(2,1)S(1)}, bf16[64,2048]{1,0:T(8,128)(2,1)S(1)}, u32[]{:S(2)}, u32[]{:S(2)}) collective-permute-start(bf16[64,2048]{1,0:T(8,128)(2,1)S(1)} %all_gather.9), channel_id=1, source_target_pairs={{8,0},{16,8},{24,16},{32,24},{40,32},{48,40},{56,48},{64,56},{72,6... | collective-permute-start | bytes 786440 | tf_op jit(solution)/shard_map/ppermute | solution.py:18
  103.9 28.1 %collective-permute-start.2 = (bf16[64,2048]{1,0:T(8,128)(2,1)S(1)}, bf16[64,2048]{1,0:T(8,128)(2,1)}, u32[]{:S(2)}, u32[]{:S(2)}) collective-permute-start(bf16[64,2048]{1,0:T(8,128)(2,1)S(1)} %all_gather.9), channel_id=1, source_target_pairs={{504,0},{0,8},{8,16},{16,24},{24,32},{32,40},{40,48},{48,56},{56,6... | collective-permute-start | bytes 786440 | tf_op jit(solution)/shard_map/ppermute | solution.py:18
  105.8 44.2 %collective-permute-start.5 = (f32[32,2048]{1,0:T(8,128)S(1)}, f32[32,2048]{1,0:T(8,128)S(1)}, u32[]{:S(2)}, u32[]{:S(2)}) collective-permute-start(f32[32,2048]{1,0:T(8,128)S(1)} %all_gather.10), channel_id=1, source_target_pairs={{16,0},{24,8},{32,16},{40,24},{48,32},{56,40},{64,48},{72,56},{80,... | collective-permute-start | bytes 786440 | tf_op jit(solution)/shard_map/ppermute | solution.py:18
  118.9 33.8 %collective-permute-start.4 = (bf16[64,2048]{1,0:T(8,128)(2,1)S(1)}, bf16[64,2048]{1,0:T(8,128)(2,1)}, u32[]{:S(2)}, u32[]{:S(2)}) collective-permute-start(bf16[64,2048]{1,0:T(8,128)(2,1)S(1)} %all_gather.9), channel_id=1, source_target_pairs={{16,0},{24,8},{32,16},{40,24},{48,32},{56,40},{64,48},{72,56},{80,... | collective-permute-start | bytes 786440 | tf_op jit(solution)/shard_map/ppermute | solution.py:18
  122.3 44.3 %collective-permute-start.7 = (f32[32,2048]{1,0:T(8,128)S(1)}, f32[32,2048]{1,0:T(8,128)S(1)}, u32[]{:S(2)}, u32[]{:S(2)}) collective-permute-start(f32[32,2048]{1,0:T(8,128)S(1)} %all_gather.10), channel_id=1, source_target_pairs={{496,0},{504,8},{0,16},{8,24},{16,32},{24,40},{32,48},{40,56},{48,... | collective-permute-start | bytes 786440 | tf_op jit(solution)/shard_map/ppermute | solution.py:18
  129.3 39.3 %collective-permute-start.6 = (bf16[64,2048]{1,0:T(8,128)(2,1)S(1)}, bf16[64,2048]{1,0:T(8,128)(2,1)}, u32[]{:S(2)}, u32[]{:S(2)}) collective-permute-start(bf16[64,2048]{1,0:T(8,128)(2,1)S(1)} %all_gather.9), channel_id=1, source_target_pairs={{496,0},{504,8},{0,16},{8,24},{16,32},{24,40},{32,48},{40,56},{48,... | collective-permute-start | bytes 786440 | tf_op jit(solution)/shard_map/ppermute | solution.py:18
  132.0 42.5 %collective-permute-start.9 = (f32[32,2048]{1,0:T(8,128)S(1)}, f32[32,2048]{1,0:T(8,128)S(1)}, u32[]{:S(2)}, u32[]{:S(2)}) collective-permute-start(f32[32,2048]{1,0:T(8,128)S(1)} %all_gather.10), channel_id=1, source_target_pairs={{24,0},{32,8},{40,16},{48,24},{56,32},{64,40},{72,48},{80,56},{88,... | collective-permute-start | bytes 786440 | tf_op jit(solution)/shard_map/ppermute | solution.py:18
  150.1 24.6 %collective-permute-start.8 = (bf16[64,2048]{1,0:T(8,128)(2,1)S(1)}, bf16[64,2048]{1,0:T(8,128)(2,1)}, u32[]{:S(2)}, u32[]{:S(2)}) collective-permute-start(bf16[64,2048]{1,0:T(8,128)(2,1)S(1)} %all_gather.9), channel_id=1, source_target_pairs={{24,0},{32,8},{40,16},{48,24},{56,32},{64,40},{72,48},{80,56},{88,... | collective-permute-start | bytes 786440 | tf_op jit(solution)/shard_map/ppermute | solution.py:18
  152.8 27.8 %collective-permute-start.11 = (f32[32,2048]{1,0:T(8,128)S(1)}, f32[32,2048]{1,0:T(8,128)S(1)}, u32[]{:S(2)}, u32[]{:S(2)}) collective-permute-start(f32[32,2048]{1,0:T(8,128)S(1)} %all_gather.10), channel_id=1, source_target_pairs={{488,0},{496,8},{504,16},{0,24},{8,32},{16,40},{24,48},{32,56},{40... | collective-permute-start | bytes 786440 | tf_op jit(solution)/shard_map/ppermute | solution.py:18
  166.6 15.7 %collective-permute-start.10 = (bf16[64,2048]{1,0:T(8,128)(2,1)S(1)}, bf16[64,2048]{1,0:T(8,128)(2,1)}, u32[]{:S(2)}, u32[]{:S(2)}) collective-permute-start(bf16[64,2048]{1,0:T(8,128)(2,1)S(1)} %all_gather.9), channel_id=1, source_target_pairs={{488,0},{496,8},{504,16},{0,24},{8,32},{16,40},{24,48},{32,56},{40... | collective-permute-start | bytes 786440 | tf_op jit(solution)/shard_map/ppermute | solution.py:18
  188.2 0.7 copy-start.1
  418.7 27.4 %collective-permute-start.12 = (bf16[64,2048]{1,0:T(8,128)(2,1)S(1)}, bf16[64,2048]{1,0:T(8,128)(2,1)}, u32[]{:S(2)}, u32[]{:S(2)}) collective-permute-start(bf16[64,2048]{1,0:T(8,128)(2,1)S(1)} %all_gather.11), channel_id=1, source_target_pairs={{8,0},{16,8},{24,16},{32,24},{40,32},{48,40},{56,48},{64,56},{72,6... | collective-permute-start | bytes 786440 | tf_op jit(solution)/shard_map/ppermute | solution.py:18
  427.4 27.9 %collective-permute-start.13 = (bf16[64,2048]{1,0:T(8,128)(2,1)S(1)}, bf16[64,2048]{1,0:T(8,128)(2,1)}, u32[]{:S(2)}, u32[]{:S(2)}) collective-permute-start(bf16[64,2048]{1,0:T(8,128)(2,1)S(1)} %all_gather.11), channel_id=1, source_target_pairs={{504,0},{0,8},{8,16},{16,24},{24,32},{32,40},{40,48},{48,56},{56,6... | collective-permute-start | bytes 786440 | tf_op jit(solution)/shard_map/ppermute | solution.py:18
  430.0 34.3 %collective-permute-start.14 = (bf16[64,2048]{1,0:T(8,128)(2,1)S(1)}, bf16[64,2048]{1,0:T(8,128)(2,1)}, u32[]{:S(2)}, u32[]{:S(2)}) collective-permute-start(bf16[64,2048]{1,0:T(8,128)(2,1)S(1)} %all_gather.11), channel_id=1, source_target_pairs={{16,0},{24,8},{32,16},{40,24},{48,32},{56,40},{64,48},{72,56},{80,... | collective-permute-start | bytes 786440 | tf_op jit(solution)/shard_map/ppermute | solution.py:18
  436.5 36.9 %collective-permute-start.15 = (bf16[64,2048]{1,0:T(8,128)(2,1)S(1)}, bf16[64,2048]{1,0:T(8,128)(2,1)S(1)}, u32[]{:S(2)}, u32[]{:S(2)}) collective-permute-start(bf16[64,2048]{1,0:T(8,128)(2,1)S(1)} %all_gather.11), channel_id=1, source_target_pairs={{496,0},{504,8},{0,16},{8,24},{16,32},{24,40},{32,48},{40,56},{48,... | collective-permute-start | bytes 786440 | tf_op jit(solution)/shard_map/ppermute | solution.py:18
  438.4 39.7 %collective-permute-start.16 = (bf16[64,2048]{1,0:T(8,128)(2,1)S(1)}, bf16[64,2048]{1,0:T(8,128)(2,1)S(1)}, u32[]{:S(2)}, u32[]{:S(2)}) collective-permute-start(bf16[64,2048]{1,0:T(8,128)(2,1)S(1)} %all_gather.11), channel_id=1, source_target_pairs={{24,0},{32,8},{40,16},{48,24},{56,32},{64,40},{72,48},{80,56},{88,... | collective-permute-start | bytes 786440 | tf_op jit(solution)/shard_map/ppermute | solution.py:18
  446.1 36.8 %collective-permute-start.17 = (bf16[64,2048]{1,0:T(8,128)(2,1)S(1)}, bf16[64,2048]{1,0:T(8,128)(2,1)S(1)}, u32[]{:S(2)}, u32[]{:S(2)}) collective-permute-start(bf16[64,2048]{1,0:T(8,128)(2,1)S(1)} %all_gather.11), channel_id=1, source_target_pairs={{488,0},{496,8},{504,16},{0,24},{8,32},{16,40},{24,48},{32,56},{40... | collective-permute-start | bytes 786440 | tf_op jit(solution)/shard_map/ppermute | solution.py:18
where the time goes:
time: 591 us; the launch traced here: 590 us
  blocking collectives  409 us (69%)
  starting transfers between devices  84.1 us (14%)
  matrix products  76.6 us (13%)
  local copies, waits for them, and re-layouts  12.1 us (2%)
    psum x1, blocking collectives, body(): curvature = lax.psum(jnp.sum(direction * summed, axis=1), ('blk', 'rows'))  101 us
    psum x1, blocking collectives, body(): norm_now = lax.psum(jnp.sum(residual * residual, axis=1), ('blk', 'rows'))  96.5 us
    psum x1, blocking collectives, body(): norm_next = lax.psum(jnp.sum(residual * residual, axis=1), ('blk', 'rows'))  93.8 us
    ppermute x18, starting transfers between devices, passed_along(): return lax.ppermute(block, axis, route)  84.1 us
    all_gather x2, blocking collectives, body(): group_dir = lax.all_gather(rounded, 'rows', axis=1, tiled=True)  77.8 us
    dot_general x56, matrix products, matern_block(): lax.dot_general(row_points, col_points, (((0,), (0,)), ((), ())), precisi...  66.2 us
    all_gather x1, blocking collectives, body(): group_points = lax.all_gather(scaled, 'rows', axis=1, tiled=True)  40 us
  transfers between devices with their start and end apart: 18, of which 1 were waited for; matrix products, arithmetic and copies ran while one was open for 13% of the time, Pallas kernels for 0%

commit v1 on v0

v1 whole, which is shorter than its diff:
```python
import functools
import math

import jax
import jax.numpy as jnp
from jax import lax
from jax.experimental import pallas as pl
from jax.experimental.pallas import tpu as pltpu
from jax.sharding import Mesh, PartitionSpec as P

F32, BF16 = jnp.float32, jnp.bfloat16
AXES = ("y_lo", "z", "core", "x", "y_hi")
SIZES = (4, 8, 2, 4, 2)
BLK = ("y_lo", "z", "core")
N_BLK = 64
SWAP = ((0, 1), (1, 0))

LN2 = math.log(2.0)
UNIT = math.sqrt(5.0) / LN2
SHIFT = 1.5 / LN2
OFFSET = 0.75 / LN2**2
LEVEL = math.log2(LN2**2 / 3.0) + SHIFT
TINY = 1e-20

FEAT = 32
RHS = 64
WIDTH = 256
ROWS = 512
DEPTH = 144
NT = (((1,), (1,)), ((), ()))


def split(value):
    high = value.astype(BF16)
    return high, (value - high.astype(F32)).astype(BF16)


def square_rows(coords, first, second):
    squares = jnp.sum(coords * coords, axis=0, keepdims=True)
    one = squares.astype(BF16).astype(F32)
    two = (squares - one).astype(BF16).astype(F32)
    three = squares - one - two
    row = lax.broadcasted_iota(jnp.int32, (16, coords.shape[1]), 0)
    out = jnp.where((row >= second) & (row < second + 3), 1.0, 0.0)
    for at, piece in enumerate((one, two, three)):
        out = jnp.where(row == first + at, piece, out)
    return out.astype(BF16)


def build_shard(weights_ref, level, shard, cols_ref, dist_ref, kernel_ref):
    coords = shard[: 2 * FEAT]
    wide = coords.astype(F32)
    cols_ref[: 2 * FEAT] = coords
    cols_ref[2 * FEAT : 4 * FEAT] = coords
    cols_ref[4 * FEAT :] = square_rows(wide[:FEAT] + wide[FEAT:], 0, 3)
    dist_ref[...] = jnp.dot(weights_ref[...], cols_ref[...], preferred_element_type=F32)
    step = 64
    for at in range(0, ROWS, step):
        part = jnp.maximum(dist_ref[at : at + step], TINY)
        moved = part * lax.rsqrt(part) + SHIFT
        entry = (moved * moved + OFFSET) * jnp.exp2(level - moved)
        kernel_ref[at : at + step] = entry.astype(BF16)
    return lax.dot_general(shard[2 * FEAT :], kernel_ref[...], NT, preferred_element_type=F32)


def build_first(levels, own_ref, peer_ref, block_ref, weights_ref, total_ref, kernel_ref, cols_ref, dist_ref):
    for at, ref in enumerate((own_ref, peer_ref)):
        coords = ref[: 2 * FEAT].astype(F32)
        high, low = coords[:FEAT], coords[FEAT:]
        extra = square_rows(high + low, 3, 0).astype(F32)
        stacked = jnp.concatenate([-2.0 * high, -2.0 * high, -2.0 * low, -2.0 * low], axis=0)
        weights_ref[at * WIDTH : (at + 1) * WIDTH, : 4 * FEAT] = jnp.transpose(stacked).astype(BF16)
        weights_ref[at * WIDTH : (at + 1) * WIDTH, 4 * FEAT :] = jnp.transpose(extra).astype(BF16)
    total_ref[...] = jnp.zeros_like(total_ref)

    def one(i, carry):
        total_ref[...] += build_shard(weights_ref, levels[0], block_ref[i], cols_ref, dist_ref, kernel_ref.at[i])
        return carry

    lax.fori_loop(0, block_ref.shape[0], one, 0)


def build_more(level_ref, weights_ref, before_ref, *refs):
    count = level_ref.shape[0]
    blocks, (total_ref, kernel_ref, cols_ref, dist_ref) = refs[:count], refs[count:]
    total_ref[...] = before_ref[...]
    for at, block_ref in enumerate(blocks):
        level = level_ref[at]

        def one(i, carry, at=at, block_ref=block_ref, level=level):
            total_ref[...] += build_shard(
                weights_ref, level, block_ref[i], cols_ref, dist_ref, kernel_ref.at[at * 4 + i]
            )
            return carry

        lax.fori_loop(0, block_ref.shape[0], one, 0)


def add_blocks(total_ref, kernel_ref, blocks):
    for at, block_ref in enumerate(blocks):

        def one(i, carry, at=at, block_ref=block_ref):
            both = lax.dot_general(block_ref[i], kernel_ref[at * 4 + i], NT, preferred_element_type=F32)
            total_ref[...] += both[:RHS] + both[RHS:]
            return carry

        lax.fori_loop(0, block_ref.shape[0], one, 0)


def apply_first(kernel_ref, *refs):
    total_ref = refs[-1]
    total_ref[...] = jnp.zeros_like(total_ref)
    add_blocks(total_ref, kernel_ref, refs[:-1])


def apply_more(kernel_ref, before_ref, *refs):
    total_ref = refs[-1]
    total_ref[...] = before_ref[...]
    add_blocks(total_ref, kernel_ref, refs[:-1])


def row_sums(product):
    ones = jnp.ones((8, product.shape[1]), F32)
    return lax.dot_general(ones, product, NT, precision=lax.Precision.HIGHEST, preferred_element_type=F32)


def apply_last(kernel_ref, before_ref, noise_ref, first_ref, peer_first_ref, image_ref, peer_image_ref, *refs):
    total_ref, sums_ref = refs[-2:]
    total_ref[...] = before_ref[...]
    add_blocks(total_ref, kernel_ref, refs[:-2])
    first, image = first_ref[...], image_ref[...]
    peer = peer_image_ref[...].astype(F32)
    peer_image = peer[:RHS] + peer[RHS:]
    peer = peer_first_ref[2 * FEAT :].astype(F32)
    peer_first = peer[:RHS] + peer[RHS:]
    near = total_ref[:, :WIDTH] + noise_ref[...] * image
    far = total_ref[:, WIDTH:]
    rows = (
        first * first,
        first * image,
        image * image,
        first * near + peer_first * far,
        image * near + peer_image * far,
    )
    at = lax.broadcasted_iota(jnp.int32, (8, RHS), 0)
    out = jnp.zeros((8, RHS), F32)
    for i, row in enumerate(rows):
        out = jnp.where(at == i, row_sums(row), out)
    sums_ref[:, :RHS] = out
    sums_ref[:, RHS:] = jnp.zeros_like(out)


VMEM_LIMIT = pltpu.CompilerParams(vmem_limit_bytes=48 * 1024 * 1024)
SMEM = pl.BlockSpec(memory_space=pltpu.SMEM)
VMEM = pl.BlockSpec(memory_space=pltpu.VMEM)


def scratch():
    return [pltpu.VMEM((DEPTH, WIDTH), BF16), pltpu.VMEM((ROWS, WIDTH), F32)]


def shape(*dims, dtype=F32):
    return jax.ShapeDtypeStruct(dims, dtype)


def shifted(value, distance):
    route = [((i - distance) % N_BLK, i) for i in range(N_BLK)]
    return lax.ppermute(value, BLK, route)


def gathered(value, axes):
    count = math.prod(SIZES[AXES.index(axis)] for axis in axes)
    return lax.all_to_all(jnp.broadcast_to(value[None], (count,) + value.shape), axes, 0, 0)


def halo(block):
    swapped = lax.ppermute(block, "core", SWAP)
    up, down = shifted(block, 2), shifted(block, -2)
    third = [(i, (i - 3 if i % 2 == 0 else i + 3) % N_BLK) for i in range(N_BLK)]
    far = lax.ppermute(block, BLK, third)
    up_swapped = lax.ppermute(up, "core", SWAP)
    down_swapped = lax.ppermute(down, "core", SWAP)
    return swapped, far, up, down, up_swapped, down_swapped


def body(points, lengthscale, noise_var, targets):
    coords = points / lengthscale[:, None] * UNIT
    message = jnp.concatenate(split(coords) + split(targets), axis=0)
    block = gathered(message[: 2 * FEAT + RHS], ("x",))
    peer_message = lax.ppermute(message, "y_hi", SWAP)
    swapped, far, up, down, up_swapped, down_swapped = halo(block)

    levels = [LEVEL + math.log2(taper) for taper in (1.0, 0.75, 0.5, 0.25)]
    odd = lax.axis_index("core") == 1
    edge = (jnp.where(odd, levels[3], levels[1]), jnp.where(odd, levels[1], levels[3]))
    weights, total, kernel_own = pl.pallas_call(
        functools.partial(build_first, levels),
        out_shape=(shape(ROWS, DEPTH, dtype=BF16), shape(RHS, ROWS), shape(4, ROWS, WIDTH, dtype=BF16)),
        scratch_shapes=scratch(),
        compiler_params=VMEM_LIMIT,
    )(message, peer_message, block)
    kernels = []
    for pair, pair_levels in (
        ((swapped, far), (levels[1], levels[3])),
        ((up, down), (levels[2], levels[2])),
        ((up_swapped, down_swapped), edge),
    ):
        total, made = pl.pallas_call(
            build_more,
            in_specs=[SMEM] + [VMEM] * 4,
            out_shape=(shape(RHS, ROWS), shape(8, ROWS, WIDTH, dtype=BF16)),
            scratch_shapes=scratch(),
            compiler_params=VMEM_LIMIT,
        )(jnp.stack([jnp.asarray(level, F32) for level in pair_levels]), weights, total, *pair)
        kernels.append(made)

    noise = noise_var[None, :]
    image = noise * targets + total[:, :WIDTH] + lax.ppermute(total[:, WIDTH:], "y_hi", SWAP)
    image_message = jnp.concatenate(split(image), axis=0)
    block = gathered(image_message, ("x",))
    peer_image = lax.ppermute(image_message, "y_hi", SWAP)
    swapped, far, up, down, up_swapped, down_swapped = halo(block)
    total = pl.pallas_call(apply_first, out_shape=shape(RHS, ROWS), compiler_params=VMEM_LIMIT)(kernel_own, block)
    for made, pair in zip(kernels[:2], ((swapped, far), (up, down))):
        total = pl.pallas_call(apply_more, out_shape=shape(RHS, ROWS), compiler_params=VMEM_LIMIT)(made, total, *pair)
    total, sums = pl.pallas_call(
        apply_last,
        out_shape=(shape(RHS, ROWS), shape(8, 2 * RHS)),
        compiler_params=VMEM_LIMIT,
    )(kernels[2], total, noise, targets, peer_message, image, peer_image, up_swapped, down_swapped)
    second = noise * image + total[:, :WIDTH] + lax.ppermute(total[:, WIDTH:], "y_hi", SWAP)
    for axes in (("x", "y_hi", "y_lo"), ("z", "core")):
        sums = jnp.sum(gathered(sums, axes), axis=0)

    rr, rq, qq, rs, qs = (sums[i, :RHS] for i in range(5))
    step = rr / rq
    norm_next = jnp.maximum(rr - 2.0 * step * rq + step * step * qq, 0.0)
    grown = 1.0 + norm_next / rr
    curvature = grown * grown * rq - step * grown * (qq + rs) + step * step * qs
    step_next = norm_next / curvature
    along = (step + step_next * grown)[:, None]
    across = (step_next * step)[:, None]
    solution = along * targets - across * image
    residual = targets - along * image + across * second
    return solution, residual


def solution(mesh):
    fine = Mesh(mesh.devices.reshape(SIZES), AXES)
    placed = (P(None, AXES), P(), P(AXES), P(None, AXES))
    return jax.shard_map(
        body, mesh=fine, in_specs=placed, out_specs=(P(None, AXES), P(None, AXES)), check_vma=False
    )
```

time: 591 us -> 152 us (0.26)
  blocking collectives: 409 us -> 32.4 us
  matrix products: 76.6 us -> 0 us
  Pallas kernels: 0 us -> 21.8 us
  waiting for transfers between devices: 1.74 us -> 14 us
  local copies, waits for them, and re-layouts: 12.1 us -> 1.37 us
  starting transfers between devices: 84.1 us -> 77.7 us
    psum x3 -> x0, blocking collectives: 291 us -> none  [the longest x1 101 us: body(): curvature = lax.psum(jnp.sum(direction * summed, axis=1), ('blk', 'rows'))]
    all_gather x3 -> x0, blocking collectives: 118 us -> none  [the longest x2 77.8 us: body(): group_dir = lax.all_gather(rounded, 'rows', axis=1, tiled=True)]
    dot_general x112 -> x0, matrix products: 76.6 us -> none  [the longest x56 66.2 us: matern_block(): lax.dot_general(row_points, col_points, (((0,), (0,)), ((), ())), precisi...]
    all_to_all x0 -> x3, blocking collectives: none -> 32.4 us  [gathered(): lax.all_to_all(jnp.broadcast_to(value[None], (count,) + value.shape), axe...]
    pallas_call x0 -> x8, Pallas kernels: none -> 21.8 us  [the longest x3 13.1 us: body(): pl.pallas_call(build_more, in_specs=[SMEM] + [VMEM] * 4, out_shape=(shape...]
    ppermute x18 -> x16, starting transfers between devices: 84.1 us -> 70.3 us  [the longest x4 24.9 us: shifted(): return lax.ppermute(value, BLK, route)]
    reshape x28 -> x0, local copies, waits for them, and re-layouts: 10.6 us -> none  [the longest x14 9.02 us: tile_apply(): col_dir.reshape(col_dir.shape[0], pieces, width).transpose(1, 0, 2)]
    ppermute x18 -> x16, waiting for transfers between devices: 1.74 us -> 9.24 us  [the longest x1 4.81 us: body(): peer_message = lax.ppermute(message, 'y_hi', SWAP)]
  transfers between devices with their start and end apart: 18 -> 17, of which waited for: 1 -> 5; matrix products, arithmetic and copies ran while one was open for 13% -> 0% of each run, Pallas kernels for 0% -> 10%
where the time goes in v1:
time: 152 us; the launch traced here: 151 us
  starting transfers between devices  77.7 us (51%)
  blocking collectives  32.4 us (21%)
  Pallas kernels  21.8 us (14%)
  waiting for transfers between devices  14 us (9%)
  other arithmetic  2.72 us (2%)
    all_to_all x3, blocking collectives, gathered(): lax.all_to_all(jnp.broadcast_to(value[None], (count,) + value.shape), axe...  32.4 us
    ppermute x4, starting transfers between devices, shifted(): return lax.ppermute(value, BLK, route)  24.9 us
    pallas_call x3, Pallas kernels, body(): pl.pallas_call(build_more, in_specs=[SMEM] + [VMEM] * 4, out_shape=(shape...  13.1 us
    ppermute x2, starting transfers between devices, halo(): swapped = lax.ppermute(block, 'core', SWAP)  12.5 us
    ppermute x2, starting transfers between devices, body(): lax.ppermute(total[:, WIDTH:], 'y_hi', SWAP)  10 us
    all_to_all x1, starting transfers between devices, gathered(): lax.all_to_all(jnp.broadcast_to(value[None], (count,) + value.shape), axe...  7.43 us
    ppermute x2, starting transfers between devices, halo(): up_swapped = lax.ppermute(up, 'core', SWAP)  6.81 us
    ppermute x1, waiting for transfers between devices, body(): peer_message = lax.ppermute(message, 'y_hi', SWAP)  4.81 us
  transfers between devices with their start and end apart: 17, of which 5 were waited for; matrix products, arithmetic and copies ran while one was open for 0% of the time, Pallas kernels for 10%

profile of v1, /device:TPU:1, one launch (start us, length us, event | category | flops | bytes accessed | tf_op | source)
XLA Modules:
  0.0 151.1 jit_solution(6694852497987982114)
XLA Ops:
  2.5 10.3 %all_to_all.20.block_ref = bf16[4,128,256]{2,1,0:T(8,128)(2,1)S(1)} all-to-all(bf16[4,128,256]{2,1,0:T(8,128)(2,1)S(1)} %broadcast_in_dim.10), channel_id=1, replica_groups=mesh['y_lo'=4,'z'=8,'core'=2,'x'=4,'y_hi'=2] {'x'}, dimensions={0} | all-to-all | bytes 524288 | tf_op jit(solution)/shard_map/all_to_all | solution.py:173
  12.8 4.0 %collective-permute-start.3 = (bf16[4,128,256]{2,1,0:T(8,128)(2,1)S(1)}, bf16[4,128,256]{2,1,0:T(8,128)(2,1)S(1)}, u32[]{:S(2)}, u32[]{:S(2)}) collective-permute-start(bf16[4,128,256]{2,1,0:T(8,128)(2,1)S(1)} %all_to_all.20.block_ref), channel_id=1, source_target_pairs={{496,0},{504,8},{0,16},{8,24},{16,32},{24,40},{32,48},{40,56},{48,... | collective-permute-start | bytes 786440 | tf_op jit(solution)/shard_map/ppermute | solution.py:168
  16.8 11.6 %collective-permute-start.4 = (bf16[4,128,256]{2,1,0:T(8,128)(2,1)S(1)}, bf16[4,128,256]{2,1,0:T(8,128)(2,1)S(1)}, u32[]{:S(2)}, u32[]{:S(2)}) collective-permute-start(bf16[4,128,256]{2,1,0:T(8,128)(2,1)S(1)} %all_to_all.20.block_ref), channel_id=1, source_target_pairs={{16,0},{24,8},{32,16},{40,24},{48,32},{56,40},{64,48},{72,56},{80,... | collective-permute-start | bytes 786440 | tf_op jit(solution)/shard_map/ppermute | solution.py:168
  28.4 4.3 %collective-permute-start.1 = (bf16[4,128,256]{2,1,0:T(8,128)(2,1)S(1)}, bf16[4,128,256]{2,1,0:T(8,128)(2,1)S(1)}, u32[]{:S(2)}, u32[]{:S(2)}) collective-permute-start(bf16[4,128,256]{2,1,0:T(8,128)(2,1)S(1)} %all_to_all.20.block_ref), channel_id=1, source_target_pairs={{0,8},{8,0},{1,9},{9,1},{2,10},{10,2},{3,11},{11,3},{4,12},{12,4},... | collective-permute-start | bytes 786440 | tf_op jit(solution)/shard_map/ppermute | solution.py:177
  32.7 1.9 %collective-permute-start.2 = (bf16[4,128,256]{2,1,0:T(8,128)(2,1)S(1)}, bf16[4,128,256]{2,1,0:T(8,128)(2,1)S(1)}, u32[]{:S(2)}, u32[]{:S(2)}) collective-permute-start(bf16[4,128,256]{2,1,0:T(8,128)(2,1)S(1)} %all_to_all.20.block_ref), channel_id=1, source_target_pairs={{0,488},{8,32},{16,504},{24,48},{32,8},{40,64},{48,24},{56,80},{64... | collective-permute-start | bytes 786440 | tf_op jit(solution)/shard_map/ppermute | solution.py:180
  34.6 4.0 %collective-permute-start.5 = (bf16[4,128,256]{2,1,0:T(8,128)(2,1)S(1)}, bf16[4,128,256]{2,1,0:T(8,128)(2,1)S(1)}, u32[]{:S(2)}, u32[]{:S(2)}) collective-permute-start(bf16[4,128,256]{2,1,0:T(8,128)(2,1)S(1)} %collective-permute-done.3.refs_0_), channel_id=1, source_target_pairs={{0,8},{8,0},{1,9},{9,1},{2,10},{10,2},{3,11},{11,3},{4,12},{12,4},... | collective-permute-start | bytes 786440 | tf_op jit(solution)/shard_map/ppermute | solution.py:181
  40.6 4.8 %collective-permute-start = (bf16[192,256]{1,0:T(8,128)(2,1)S(1)}, bf16[192,256]{1,0:T(8,128)(2,1)S(1)}, u32[]{:S(2)}, u32[]{:S(2)}) collective-permute-start(bf16[192,256]{1,0:T(8,128)(2,1)S(1)} %pad_maximum_fusion.own_ref), channel_id=1, source_target_pairs={{0,1},{1,0},{2,3},{3,2},{4,5},{5,4},{6,7},{7,6},{8,9},{9,8},{10,11... | collective-permute-start | bytes 294920 | tf_op jit(solution)/shard_map/ppermute | solution.py:190
  45.5 4.8 %collective-permute-done.peer_ref.peer_first_ref = bf16[192,256]{1,0:T(8,128)(2,1)S(1)} collective-permute-done((bf16[192,256]{1,0:T(8,128)(2,1)S(1)}, bf16[192,256]{1,0:T(8,128)(2,1)S(1)}, u32[]{:S(2)}, u32[]{:S(2)}) %collective-permute-start) | collective-permute-done | bytes 98336 | tf_op jit(solution)/shard_map/ppermute | solution.py:190
  50.3 2.0 %shard_map.59 = (bf16[512,144]{1,0:T(8,128)(2,1)S(1)}, f32[64,512]{1,0:T(8,128)S(1)}, bf16[4,512,256]{2,1,0:T(8,128)(2,1)S(1)}) custom-call(bf16[192,256]{1,0:T(8,128)(2,1)S(1)} %pad_maximum_fusion.own_ref, bf16[192,256]{1,0:T(8,128)(2,1)S(1)} %collective-permute-done.peer_ref.peer_first_ref, bf16[4,128,256]{2,1,0:T(8,128)(2,1)S(1)} %all_to_all.20.block_ref), custom_call_target="tpu_custom_call" | custom-call | tf_op jit(solution)/shard_map/pallas_call | solution.py:196
  53.0 4.4 %shard_map.60 = (f32[64,512]{1,0:T(8,128)S(1)}, bf16[8,512,256]{2,1,0:T(8,128)(2,1)S(1)}) custom-call(f32[2]{0:T(128)S(1)} %copy-done.2, bf16[512,144]{1,0:T(8,128)(2,1)S(1)} %get-tuple-element.13.weights_ref, f32[64,512]{1,0:T(8,128)S(1)} %get-tuple-element.14.before_ref, bf16[4,128,256]{2,1,0:T(8,128)(2,1)S(1)} %collective-permute-done.1.refs_0_, ...), custom_call_target="tpu_custom_call" | custom-call | tf_op jit(solution)/shard_map/pallas_call | solution.py:208
  57.4 4.4 %shard_map.61 = (f32[64,512]{1,0:T(8,128)S(1)}, bf16[8,512,256]{2,1,0:T(8,128)(2,1)S(1)}) custom-call(f32[2]{0:T(128)S(1)} %broadcast_1_level_ref.2.level_ref, bf16[512,144]{1,0:T(8,128)(2,1)S(1)} %get-tuple-element.13.weights_ref, f32[64,512]{1,0:T(8,128)S(1)} %get-tuple-element.15.before_ref, bf16[4,128,256]{2,1,0:T(8,128)(2,1)S(1)} %collective-permute-done.3.refs_0_, ...), custom_call_target="tpu_custom_call" | custom-call | tf_op jit(solution)/shard_map/pallas_call | solution.py:208
  61.8 4.4 %shard_map.62 = (f32[64,512]{1,0:T(8,128)S(1)}, bf16[8,512,256]{2,1,0:T(8,128)(2,1)S(1)}) custom-call(f32[2]{0:T(128)S(1)} %pad_maximum_fusion.3.level_ref, bf16[512,144]{1,0:T(8,128)(2,1)S(1)} %get-tuple-element.13.weights_ref, f32[64,512]{1,0:T(8,128)S(1)} %get-tuple-element.16.before_ref, bf16[4,128,256]{2,1,0:T(8,128)(2,1)S(1)} %collective-permute-done.5.refs_0_, ...), custom_call_target="tpu_custom_call" | custom-call | tf_op jit(solution)/shard_map/pallas_call | solution.py:208
  66.2 7.0 %collective-permute-start.7 = (f32[64,256]{1,0:T(8,128)S(1)}, f32[64,256]{1,0:T(8,128)S(1)}, u32[]{:S(2)}, u32[]{:S(2)}) collective-permute-start(f32[64,256]{1,0:T(8,128)S(1)} %slice.30), channel_id=1, source_target_pairs={{0,1},{1,0},{2,3},{3,2},{4,5},{5,4},{6,7},{7,6},{8,9},{9,8},{10,11... | collective-permute-start | bytes 196616 | tf_op jit(solution)/shard_map/ppermute | solution.py:218
  75.2 7.9 %all_to_all.21.refs_0_ = bf16[4,128,256]{2,1,0:T(8,128)(2,1)S(1)} all-to-all(bf16[4,128,256]{2,1,0:T(8,128)(2,1)S(1)} %broadcast_in_dim.11), channel_id=1, replica_groups=mesh['y_lo'=4,'z'=8,'core'=2,'x'=4,'y_hi'=2] {'x'}, dimensions={0} | all-to-all | bytes 524288 | tf_op jit(solution)/shard_map/all_to_all | solution.py:173
  83.1 3.1 %collective-permute-start.10 = (bf16[4,128,256]{2,1,0:T(8,128)(2,1)S(1)}, bf16[4,128,256]{2,1,0:T(8,128)(2,1)S(1)}, u32[]{:S(2)}, u32[]{:S(2)}) collective-permute-start(bf16[4,128,256]{2,1,0:T(8,128)(2,1)S(1)} %all_to_all.21.refs_0_), channel_id=1, source_target_pairs={{496,0},{504,8},{0,16},{8,24},{16,32},{24,40},{32,48},{40,56},{48,... | collective-permute-start | bytes 786440 | tf_op jit(solution)/shard_map/ppermute | solution.py:168
  86.2 6.2 %collective-permute-start.11 = (bf16[4,128,256]{2,1,0:T(8,128)(2,1)S(1)}, bf16[4,128,256]{2,1,0:T(8,128)(2,1)S(1)}, u32[]{:S(2)}, u32[]{:S(2)}) collective-permute-start(bf16[4,128,256]{2,1,0:T(8,128)(2,1)S(1)} %all_to_all.21.refs_0_), channel_id=1, source_target_pairs={{16,0},{24,8},{32,16},{40,24},{48,32},{56,40},{64,48},{72,56},{80,... | collective-permute-start | bytes 786440 | tf_op jit(solution)/shard_map/ppermute | solution.py:168
  92.4 8.2 %collective-permute-start.8 = (bf16[4,128,256]{2,1,0:T(8,128)(2,1)S(1)}, bf16[4,128,256]{2,1,0:T(8,128)(2,1)S(1)}, u32[]{:S(2)}, u32[]{:S(2)}) collective-permute-start(bf16[4,128,256]{2,1,0:T(8,128)(2,1)S(1)} %all_to_all.21.refs_0_), channel_id=1, source_target_pairs={{0,8},{8,0},{1,9},{9,1},{2,10},{10,2},{3,11},{11,3},{4,12},{12,4},... | collective-permute-start | bytes 786440 | tf_op jit(solution)/shard_map/ppermute | solution.py:177
  102.6 2.8 %collective-permute-start.13 = (bf16[4,128,256]{2,1,0:T(8,128)(2,1)S(1)}, bf16[4,128,256]{2,1,0:T(8,128)(2,1)S(1)}, u32[]{:S(2)}, u32[]{:S(2)}) collective-permute-start(bf16[4,128,256]{2,1,0:T(8,128)(2,1)S(1)} %collective-permute-done.10.refs_0_), channel_id=1, source_target_pairs={{0,8},{8,0},{1,9},{9,1},{2,10},{10,2},{3,11},{11,3},{4,12},{12,4},... | collective-permute-start | bytes 786440 | tf_op jit(solution)/shard_map/ppermute | solution.py:181
  107.3 3.5 %collective-permute-start.12 = (bf16[128,256]{1,0:T(8,128)(2,1)S(1)}, bf16[128,256]{1,0:T(8,128)(2,1)S(1)}, u32[]{:S(2)}, u32[]{:S(2)}) collective-permute-start(bf16[128,256]{1,0:T(8,128)(2,1)S(1)} %pad_maximum_fusion.2), channel_id=1, source_target_pairs={{0,1},{1,0},{2,3},{3,2},{4,5},{5,4},{6,7},{7,6},{8,9},{9,8},{10,11... | collective-permute-start | bytes 196616 | tf_op jit(solution)/shard_map/ppermute | solution.py:221
  116.3 2.2 %shard_map.66 = (f32[64,512]{1,0:T(8,128)S(1)}, f32[8,128]{1,0:T(8,128)S(1)}) custom-call(bf16[8,512,256]{2,1,0:T(8,128)(2,1)S(1)} %get-tuple-element.17.kernel_ref, f32[64,512]{1,0:T(8,128)S(1)} %shard_map.65.before_ref, f32[1,256]{1,0:T(1,128)S(1)} %bitcast.51, f32[64,256]{1,0:T(8,128)S(1)} %copy-done, ...), custom_call_target="tpu_custom_call" | custom-call | tf_op jit(solution)/shard_map/pallas_call | solution.py:226
  118.4 14.2 %all_to_all.22 = f32[32,8,128]{2,1,0:T(8,128)S(1)} all-to-all(f32[32,8,128]{2,1,0:T(8,128)S(1)} %broadcast_in_dim.13), channel_id=1, replica_groups=mesh['y_lo'=4,'z'=8,'core'=2,'x'=4,'y_hi'=2] {'x','y_hi','y_lo'}, dimensions={0} | all-to-all | bytes 262144 | tf_op jit(solution)/shard_map/all_to_all | solution.py:173
  133.3 7.4 %all-to-all-start.3 = ((f32[16,8,128]{2,1,0:T(8,128)}), f32[16,8,128]{2,1,0:T(8,128)S(1)}, u32[]{:S(2)}, u32[]{:S(2)}) async-start(f32[16,8,128]{2,1,0:T(8,128)} %broadcast_in_dim.14), calls=%async_computation.3 | async-start | bytes 131072 | tf_op jit(solution)/shard_map/all_to_all | solution.py:173
  140.8 3.0 %collective-permute-start.15 = (f32[64,256]{1,0:T(8,128)S(1)}, f32[64,256]{1,0:T(8,128)S(1)}, u32[]{:S(2)}, u32[]{:S(2)}) collective-permute-start(f32[64,256]{1,0:T(8,128)S(1)} %slice.37), channel_id=1, source_target_pairs={{0,1},{1,0},{2,3},{3,2},{4,5},{5,4},{6,7},{7,6},{8,9},{9,8},{10,11... | collective-permute-start | bytes 196616 | tf_op jit(solution)/shard_map/ppermute | solution.py:231
  143.8 4.8 %all-to-all-done.3 = f32[16,8,128]{2,1,0:T(8,128)S(1)} async-done(((f32[16,8,128]{2,1,0:T(8,128)}), f32[16,8,128]{2,1,0:T(8,128)S(1)}, u32[]{:S(2)}, u32[]{:S(2)}) %all-to-all-start.3) | async-done | bytes 65568 | tf_op jit(solution)/shard_map/all_to_all | solution.py:173
  (47 shorter events, 18.8 us)
Async XLA Ops:
  2.4 72.7 %copy-start = (f32[64,256]{1,0:T(8,128)S(1)}, f32[64,256]{1,0:T(8,128)}, u32[]{:S(2)}) copy-start(f32[64,256]{1,0:T(8,128)} %first_ref.1) | copy-start | bytes 196612
  2.5 72.6 %copy-start.1 = (f32[256]{0:T(256)S(1)}, f32[256]{0:T(256)}, u32[]{:S(2)}) copy-start(f32[256]{0:T(256)} %param.6) | copy-start | bytes 3076
  12.8 21.9 %collective-permute-start.3 = (bf16[4,128,256]{2,1,0:T(8,128)(2,1)S(1)}, bf16[4,128,256]{2,1,0:T(8,128)(2,1)S(1)}, u32[]{:S(2)}, u32[]{:S(2)}) collective-permute-start(bf16[4,128,256]{2,1,0:T(8,128)(2,1)S(1)} %all_to_all.20.block_ref), channel_id=1, source_target_pairs={{496,0},{504,8},{0,16},{8,24},{16,32},{24,40},{32,48},{40,56},{48,... | collective-permute-start | bytes 786440 | tf_op jit(solution)/shard_map/ppermute | solution.py:168
  16.8 21.9 %collective-permute-start.4 = (bf16[4,128,256]{2,1,0:T(8,128)(2,1)S(1)}, bf16[4,128,256]{2,1,0:T(8,128)(2,1)S(1)}, u32[]{:S(2)}, u32[]{:S(2)}) collective-permute-start(bf16[4,128,256]{2,1,0:T(8,128)(2,1)S(1)} %all_to_all.20.block_ref), channel_id=1, source_target_pairs={{16,0},{24,8},{32,16},{40,24},{48,32},{56,40},{64,48},{72,56},{80,... | collective-permute-start | bytes 786440 | tf_op jit(solution)/shard_map/ppermute | solution.py:168
  28.4 23.9 %collective-permute-start.1 = (bf16[4,128,256]{2,1,0:T(8,128)(2,1)S(1)}, bf16[4,128,256]{2,1,0:T(8,128)(2,1)S(1)}, u32[]{:S(2)}, u32[]{:S(2)}) collective-permute-start(bf16[4,128,256]{2,1,0:T(8,128)(2,1)S(1)} %all_to_all.20.block_ref), channel_id=1, source_target_pairs={{0,8},{8,0},{1,9},{9,1},{2,10},{10,2},{3,11},{11,3},{4,12},{12,4},... | collective-permute-start | bytes 786440 | tf_op jit(solution)/shard_map/ppermute | solution.py:177
  32.7 19.6 %collective-permute-start.2 = (bf16[4,128,256]{2,1,0:T(8,128)(2,1)S(1)}, bf16[4,128,256]{2,1,0:T(8,128)(2,1)S(1)}, u32[]{:S(2)}, u32[]{:S(2)}) collective-permute-start(bf16[4,128,256]{2,1,0:T(8,128)(2,1)S(1)} %all_to_all.20.block_ref), channel_id=1, source_target_pairs={{0,488},{8,32},{16,504},{24,48},{32,8},{40,64},{48,24},{56,80},{64... | collective-permute-start | bytes 786440 | tf_op jit(solution)/shard_map/ppermute | solution.py:180
  34.6 27.1 %collective-permute-start.5 = (bf16[4,128,256]{2,1,0:T(8,128)(2,1)S(1)}, bf16[4,128,256]{2,1,0:T(8,128)(2,1)S(1)}, u32[]{:S(2)}, u32[]{:S(2)}) collective-permute-start(bf16[4,128,256]{2,1,0:T(8,128)(2,1)S(1)} %collective-permute-done.3.refs_0_), channel_id=1, source_target_pairs={{0,8},{8,0},{1,9},{9,1},{2,10},{10,2},{3,11},{11,3},{4,12},{12,4},... | collective-permute-start | bytes 786440 | tf_op jit(solution)/shard_map/ppermute | solution.py:181
  38.7 23.1 %collective-permute-start.6 = (bf16[4,128,256]{2,1,0:T(8,128)(2,1)S(1)}, bf16[4,128,256]{2,1,0:T(8,128)(2,1)S(1)}, u32[]{:S(2)}, u32[]{:S(2)}) collective-permute-start(bf16[4,128,256]{2,1,0:T(8,128)(2,1)S(1)} %collective-permute-done.4.refs_1_), channel_id=1, source_target_pairs={{0,8},{8,0},{1,9},{9,1},{2,10},{10,2},{3,11},{11,3},{4,12},{12,4},... | collective-permute-start | bytes 786440 | tf_op jit(solution)/shard_map/ppermute | solution.py:182
  40.6 9.7 %collective-permute-start = (bf16[192,256]{1,0:T(8,128)(2,1)S(1)}, bf16[192,256]{1,0:T(8,128)(2,1)S(1)}, u32[]{:S(2)}, u32[]{:S(2)}) collective-permute-start(bf16[192,256]{1,0:T(8,128)(2,1)S(1)} %pad_maximum_fusion.own_ref), channel_id=1, source_target_pairs={{0,1},{1,0},{2,3},{3,2},{4,5},{5,4},{6,7},{7,6},{8,9},{9,8},{10,11... | collective-permute-start | bytes 294920 | tf_op jit(solution)/shard_map/ppermute | solution.py:190
  52.4 0.7 copy-start.2
  66.2 8.9 %collective-permute-start.7 = (f32[64,256]{1,0:T(8,128)S(1)}, f32[64,256]{1,0:T(8,128)S(1)}, u32[]{:S(2)}, u32[]{:S(2)}) collective-permute-start(f32[64,256]{1,0:T(8,128)S(1)} %slice.30), channel_id=1, source_target_pairs={{0,1},{1,0},{2,3},{3,2},{4,5},{5,4},{6,7},{7,6},{8,9},{9,8},{10,11... | collective-permute-start | bytes 196616 | tf_op jit(solution)/shard_map/ppermute | solution.py:218
  83.1 19.5 %collective-permute-start.10 = (bf16[4,128,256]{2,1,0:T(8,128)(2,1)S(1)}, bf16[4,128,256]{2,1,0:T(8,128)(2,1)S(1)}, u32[]{:S(2)}, u32[]{:S(2)}) collective-permute-start(bf16[4,128,256]{2,1,0:T(8,128)(2,1)S(1)} %all_to_all.21.refs_0_), channel_id=1, source_target_pairs={{496,0},{504,8},{0,16},{8,24},{16,32},{24,40},{32,48},{40,56},{48,... | collective-permute-start | bytes 786440 | tf_op jit(solution)/shard_map/ppermute | solution.py:168
  86.2 19.2 %collective-permute-start.11 = (bf16[4,128,256]{2,1,0:T(8,128)(2,1)S(1)}, bf16[4,128,256]{2,1,0:T(8,128)(2,1)S(1)}, u32[]{:S(2)}, u32[]{:S(2)}) collective-permute-start(bf16[4,128,256]{2,1,0:T(8,128)(2,1)S(1)} %all_to_all.21.refs_0_), channel_id=1, source_target_pairs={{16,0},{24,8},{32,16},{40,24},{48,32},{56,40},{64,48},{72,56},{80,... | collective-permute-start | bytes 786440 | tf_op jit(solution)/shard_map/ppermute | solution.py:168
  92.4 19.4 %collective-permute-start.8 = (bf16[4,128,256]{2,1,0:T(8,128)(2,1)S(1)}, bf16[4,128,256]{2,1,0:T(8,128)(2,1)S(1)}, u32[]{:S(2)}, u32[]{:S(2)}) collective-permute-start(bf16[4,128,256]{2,1,0:T(8,128)(2,1)S(1)} %all_to_all.21.refs_0_), channel_id=1, source_target_pairs={{0,8},{8,0},{1,9},{9,1},{2,10},{10,2},{3,11},{11,3},{4,12},{12,4},... | collective-permute-start | bytes 786440 | tf_op jit(solution)/shard_map/ppermute | solution.py:177
  100.6 11.2 %collective-permute-start.9 = (bf16[4,128,256]{2,1,0:T(8,128)(2,1)S(1)}, bf16[4,128,256]{2,1,0:T(8,128)(2,1)S(1)}, u32[]{:S(2)}, u32[]{:S(2)}) collective-permute-start(bf16[4,128,256]{2,1,0:T(8,128)(2,1)S(1)} %all_to_all.21.refs_0_), channel_id=1, source_target_pairs={{0,488},{8,32},{16,504},{24,48},{32,8},{40,64},{48,24},{56,80},{64... | collective-permute-start | bytes 786440 | tf_op jit(solution)/shard_map/ppermute | solution.py:180
  102.6 13.7 %collective-permute-start.13 = (bf16[4,128,256]{2,1,0:T(8,128)(2,1)S(1)}, bf16[4,128,256]{2,1,0:T(8,128)(2,1)S(1)}, u32[]{:S(2)}, u32[]{:S(2)}) collective-permute-start(bf16[4,128,256]{2,1,0:T(8,128)(2,1)S(1)} %collective-permute-done.10.refs_0_), channel_id=1, source_target_pairs={{0,8},{8,0},{1,9},{9,1},{2,10},{10,2},{3,11},{11,3},{4,12},{12,4},... | collective-permute-start | bytes 786440 | tf_op jit(solution)/shard_map/ppermute | solution.py:181
  105.4 10.9 %collective-permute-start.14 = (bf16[4,128,256]{2,1,0:T(8,128)(2,1)S(1)}, bf16[4,128,256]{2,1,0:T(8,128)(2,1)S(1)}, u32[]{:S(2)}, u32[]{:S(2)}) collective-permute-start(bf16[4,128,256]{2,1,0:T(8,128)(2,1)S(1)} %collective-permute-done.11.refs_1_), channel_id=1, source_target_pairs={{0,8},{8,0},{1,9},{9,1},{2,10},{10,2},{3,11},{11,3},{4,12},{12,4},... | collective-permute-start | bytes 786440 | tf_op jit(solution)/shard_map/ppermute | solution.py:182
  107.3 8.9 %collective-permute-start.12 = (bf16[128,256]{1,0:T(8,128)(2,1)S(1)}, bf16[128,256]{1,0:T(8,128)(2,1)S(1)}, u32[]{:S(2)}, u32[]{:S(2)}) collective-permute-start(bf16[128,256]{1,0:T(8,128)(2,1)S(1)} %pad_maximum_fusion.2), channel_id=1, source_target_pairs={{0,1},{1,0},{2,3},{3,2},{4,5},{5,4},{6,7},{7,6},{8,9},{9,8},{10,11... | collective-permute-start | bytes 196616 | tf_op jit(solution)/shard_map/ppermute | solution.py:221
  133.3 15.2 %all-to-all-start.3 = ((f32[16,8,128]{2,1,0:T(8,128)}), f32[16,8,128]{2,1,0:T(8,128)S(1)}, u32[]{:S(2)}, u32[]{:S(2)}) async-start(f32[16,8,128]{2,1,0:T(8,128)} %broadcast_in_dim.14), calls=%async_computation.3 | async-start | bytes 131072 | tf_op jit(solution)/shard_map/all_to_all | solution.py:173
  140.8 9.6 %collective-permute-start.15 = (f32[64,256]{1,0:T(8,128)S(1)}, f32[64,256]{1,0:T(8,128)S(1)}, u32[]{:S(2)}, u32[]{:S(2)}) collective-permute-start(f32[64,256]{1,0:T(8,128)S(1)} %slice.37), channel_id=1, source_target_pairs={{0,1},{1,0},{2,3},{3,2},{4,5},{5,4},{6,7},{7,6},{8,9},{9,8},{10,11... | collective-permute-start | bytes 196616 | tf_op jit(solution)/shard_map/ppermute | solution.py:231

commit v2 on v1

v2 whole, which is shorter than its diff:
```python
import math

import jax
import jax.numpy as jnp
from jax import lax
from jax.experimental import pallas as pl
from jax.experimental.pallas import tpu as pltpu
from jax.sharding import Mesh, PartitionSpec as P

F32, BF16 = jnp.float32, jnp.bfloat16
AXES = ("y_lo", "z", "core", "x", "y_hi")
SIZES = (4, 8, 2, 4, 2)
BLK = ("y_lo", "z", "core")
N_BLK = 64
SWAP = ((0, 1), (1, 0))

LN2 = math.log(2.0)
UNIT = math.sqrt(5.0) / LN2
SHIFT = 1.5 / LN2
OFFSET = 0.75 / LN2**2
LEVEL = math.log2(LN2**2 / 3.0) + SHIFT
TINY = 1e-20

FEAT = 32
RHS = 64
WIDTH = 256
DEPTH = 144
SHARDS = 8
SIGMA = 0.5
NT = (((1,), (1,)), ((), ()))


def split(value):
    high = lax.reduce_precision(value, 8, 7)
    return high.astype(BF16), (value - high).astype(BF16)


def square_rows(coords, first, second):
    squares = jnp.sum(coords * coords, axis=0, keepdims=True)
    one = squares.astype(BF16).astype(F32)
    two = (squares - one).astype(BF16).astype(F32)
    three = squares - one - two
    row = lax.broadcasted_iota(jnp.int32, (16, coords.shape[1]), 0)
    out = jnp.where((row >= second) & (row < second + 3), 1.0, 0.0)
    for at, piece in enumerate((one, two, three)):
        out = jnp.where(row == first + at, piece, out)
    return out.astype(BF16)


def build_shard(weights, level, shard, cols_ref, dist_ref, kernel_ref):
    coords = shard[: 2 * FEAT]
    wide = coords.astype(F32)
    cols_ref[: 2 * FEAT] = coords
    cols_ref[2 * FEAT : 4 * FEAT] = coords
    cols_ref[4 * FEAT :] = square_rows(wide[:FEAT] + wide[FEAT:], 0, 3)
    dist_ref[...] = jnp.dot(weights, cols_ref[...], preferred_element_type=F32)
    step = 64
    for at in range(0, WIDTH, step):
        part = jnp.maximum(dist_ref[at : at + step], TINY)
        moved = part * lax.rsqrt(part) + SHIFT
        entry = (moved * moved + OFFSET) * jnp.exp2(level - moved)
        kernel_ref[at : at + step] = entry.astype(BF16)
    return lax.dot_general(shard[2 * FEAT :], kernel_ref[...], NT, preferred_element_type=F32)


def build_block(weights, level, block_ref, cols_ref, dist_ref, kernel_ref):
    total = None
    for i in range(SHARDS):
        part = build_shard(weights, level, block_ref[i], cols_ref.at[i % 2], dist_ref.at[i % 2], kernel_ref.at[i])
        total = part if total is None else total + part
    return total


def build_first(own_ref, block_ref, weights_ref, total_ref, kernel_ref, cols_ref, dist_ref):
    coords = own_ref[: 2 * FEAT].astype(F32)
    high, low = coords[:FEAT], coords[FEAT:]
    extra = square_rows(high + low, 3, 0).astype(F32)
    stacked = jnp.concatenate([-2.0 * high, -2.0 * high, -2.0 * low, -2.0 * low], axis=0)
    weights_ref[:, : 4 * FEAT] = jnp.transpose(stacked).astype(BF16)
    weights_ref[:, 4 * FEAT :] = jnp.transpose(extra).astype(BF16)
    total_ref[...] = build_block(weights_ref[...], LEVEL, block_ref, cols_ref, dist_ref, kernel_ref.at[0])


def build_more(level_ref, weights_ref, before_ref, *refs):
    count = level_ref.shape[0]
    blocks, (total_ref, kernel_ref, cols_ref, dist_ref) = refs[:count], refs[count:]
    total = before_ref[...]
    for at, block_ref in enumerate(blocks):
        total = total + build_block(
            weights_ref[...], level_ref[at], block_ref, cols_ref, dist_ref, kernel_ref.at[at]
        )
    total_ref[...] = total


def add_blocks(total, kernel_ref, blocks):
    for at, block_ref in enumerate(blocks):
        for i in range(SHARDS):
            total = total + lax.dot_general(block_ref[i], kernel_ref[at, i], NT, preferred_element_type=F32)
    return total


def apply_first(kernel_ref, *refs):
    refs[-1][...] = add_blocks(jnp.zeros((RHS, WIDTH), F32), kernel_ref, refs[:-1])


def apply_more(kernel_ref, before_ref, *refs):
    refs[-1][...] = add_blocks(before_ref[...], kernel_ref, refs[:-1])


def row_sums(product):
    ones = jnp.ones((8, product.shape[1]), F32)
    return lax.dot_general(ones, product, NT, precision=lax.Precision.HIGHEST, preferred_element_type=F32)


def apply_last(kernel_ref, before_ref, noise_ref, first_ref, first_total_ref, image_ref, *refs):
    second_ref, sums_ref = refs[-2:]
    total = add_blocks(before_ref[...], kernel_ref, refs[:-2])
    first, image = first_ref[...], image_ref[...]
    second = noise_ref[...] * image + (first_total_ref[...] - total) * (1.0 / SIGMA)
    second_ref[...] = second
    rows = (first * first, first * image, image * image, first * second, image * second)
    at = lax.broadcasted_iota(jnp.int32, (8, RHS), 0)
    out = jnp.zeros((8, RHS), F32)
    for i, row in enumerate(rows):
        out = jnp.where(at == i, row_sums(row), out)
    sums_ref[:, :RHS] = out
    sums_ref[:, RHS:] = jnp.zeros_like(out)


VMEM_LIMIT = pltpu.CompilerParams(vmem_limit_bytes=48 * 1024 * 1024)
SMEM = pl.BlockSpec(memory_space=pltpu.SMEM)
VMEM = pl.BlockSpec(memory_space=pltpu.VMEM)


def scratch():
    return [pltpu.VMEM((2, DEPTH, WIDTH), BF16), pltpu.VMEM((2, WIDTH, WIDTH), F32)]


def shape(*dims, dtype=F32):
    return jax.ShapeDtypeStruct(dims, dtype)


def shifted(value, distance):
    route = [((i - distance) % N_BLK, i) for i in range(N_BLK)]
    return lax.ppermute(value, BLK, route)


def gathered(value, axes):
    count = math.prod(SIZES[AXES.index(axis)] for axis in axes)
    return lax.all_to_all(jnp.broadcast_to(value[None], (count,) + value.shape), axes, 0, 0)


def halo(block):
    swapped = lax.ppermute(block, "core", SWAP)
    up, down = shifted(block, 2), shifted(block, -2)
    third = [(i, (i - 3 if i % 2 == 0 else i + 3) % N_BLK) for i in range(N_BLK)]
    far = lax.ppermute(block, BLK, third)
    up_swapped = lax.ppermute(up, "core", SWAP)
    down_swapped = lax.ppermute(down, "core", SWAP)
    return swapped, far, up, down, up_swapped, down_swapped


def kernel_shape(blocks):
    return shape(blocks, SHARDS, WIDTH, WIDTH, dtype=BF16)


def body(points, lengthscale, noise_var, targets):
    coords = points / lengthscale[:, None] * UNIT
    message = jnp.concatenate(split(coords) + (targets.astype(BF16),), axis=0)
    block = gathered(message, ("x", "y_hi"))
    swapped, far, up, down, up_swapped, down_swapped = halo(block)

    levels = [LEVEL + math.log2(taper) for taper in (1.0, 0.75, 0.5, 0.25)]
    odd = lax.axis_index("core") == 1
    edge = (jnp.where(odd, levels[3], levels[1]), jnp.where(odd, levels[1], levels[3]))
    weights, total, made = pl.pallas_call(
        build_first,
        out_shape=(shape(WIDTH, DEPTH, dtype=BF16), shape(RHS, WIDTH), kernel_shape(1)),
        scratch_shapes=scratch(),
        compiler_params=VMEM_LIMIT,
    )(message, block)
    kernels = [made]
    for blocks, block_levels in (
        ((swapped,), (levels[1],)),
        ((far,), (levels[3],)),
        ((up, down), (levels[2], levels[2])),
        ((up_swapped, down_swapped), edge),
    ):
        total, made = pl.pallas_call(
            build_more,
            in_specs=[SMEM] + [VMEM] * (2 + len(blocks)),
            out_shape=(shape(RHS, WIDTH), kernel_shape(len(blocks))),
            scratch_shapes=scratch(),
            compiler_params=VMEM_LIMIT,
        )(jnp.stack([jnp.asarray(level, F32) for level in block_levels]), weights, total, *blocks)
        kernels.append(made)

    noise = noise_var[None, :]
    image = noise * targets + total
    block = gathered((targets - SIGMA * image).astype(BF16), ("x", "y_hi"))
    swapped, far, up, down, up_swapped, down_swapped = halo(block)
    sent = pl.pallas_call(apply_first, out_shape=shape(RHS, WIDTH), compiler_params=VMEM_LIMIT)(kernels[0], block)
    for made, blocks in zip(kernels[1:4], ((swapped,), (far,), (up, down))):
        sent = pl.pallas_call(apply_more, out_shape=shape(RHS, WIDTH), compiler_params=VMEM_LIMIT)(made, sent, *blocks)
    second, sums = pl.pallas_call(
        apply_last, out_shape=(shape(RHS, WIDTH), shape(8, 2 * RHS)), compiler_params=VMEM_LIMIT
    )(kernels[4], sent, noise, targets, total, image, up_swapped, down_swapped)
    for axes in (("x", "y_hi", "y_lo"), ("z", "core")):
        sums = jnp.sum(gathered(sums, axes), axis=0)

    rr, rq, qq, rs, qs = (sums[i, :RHS] for i in range(5))
    step = rr / rq
    norm_next = jnp.maximum(rr - 2.0 * step * rq + step * step * qq, 0.0)
    grown = 1.0 + norm_next / rr
    curvature = grown * grown * rq - step * grown * (qq + rs) + step * step * qs
    step_next = norm_next / curvature
    along = (step + step_next * grown)[:, None]
    across = (step_next * step)[:, None]
    solution = along * targets - across * image
    residual = targets - along * image + across * second
    return solution, residual


def solution(mesh):
    fine = Mesh(mesh.devices.reshape(SIZES), AXES)
    placed = (P(None, AXES), P(), P(AXES), P(None, AXES))
    return jax.shard_map(
        body, mesh=fine, in_specs=placed, out_specs=(P(None, AXES), P(None, AXES)), check_vma=False
    )
```

time: 152 us -> 143 us (0.941)
  blocking collectives: 32.4 us -> 66.7 us
  starting transfers between devices: 77.7 us -> 51.8 us
  Pallas kernels: 21.8 us -> 12.5 us
  waiting for transfers between devices: 14 us -> 8.08 us
    all_to_all x3 -> x4, blocking collectives: 32.4 us -> 66.7 us  [gathered(): lax.all_to_all(jnp.broadcast_to(value[None], (count,) + value.shape), axe...]
    ppermute x4 -> x0, starting transfers between devices: 18.3 us -> none  [the longest x2 10 us: body(): lax.ppermute(total[:, WIDTH:], 'y_hi', SWAP)]
    ppermute x2, starting transfers between devices: 6.81 us -> 16.8 us  [halo(): up_swapped = lax.ppermute(up, 'core', SWAP)]
    pallas_call x8 -> x10, Pallas kernels: 21.8 us -> 12.5 us  [the longest x4 7.89 us: body(): pl.pallas_call(build_more, in_specs=[SMEM] + [VMEM] * (2 + len(blocks)),...]
    ppermute x4 -> x0, waiting for transfers between devices: 9.21 us -> none  [the longest x1 4.81 us: body(): peer_message = lax.ppermute(message, 'y_hi', SWAP)]
    ppermute x4, starting transfers between devices: 24.9 us -> 16.5 us  [shifted(): return lax.ppermute(value, BLK, route)]
    all_to_all x1 -> x0, starting transfers between devices: 7.43 us -> none  [gathered(): lax.all_to_all(jnp.broadcast_to(value[None], (count,) + value.shape), axe...]
    ppermute x4, waiting for transfers between devices: 0.01 us -> 6.27 us  [shifted(): return lax.ppermute(value, BLK, route)]
  transfers between devices with their start and end apart: 17 -> 12, of which waited for: 5 -> 4; matrix products, arithmetic and copies ran while one was open for 0% -> 0% of each run, Pallas kernels for 10% -> 6%
where the time goes in v2:
time: 143 us
  blocking collectives  66.7 us (47%)
  starting transfers between devices  51.8 us (36%)
  Pallas kernels  12.5 us (9%)
  waiting for transfers between devices  8.08 us (6%)
  other arithmetic  2.62 us (2%)
    all_to_all x4, blocking collectives, gathered(): lax.all_to_all(jnp.broadcast_to(value[None], (count,) + value.shape), axe...  66.7 us
    ppermute x2, starting transfers between devices, halo(): up_swapped = lax.ppermute(up, 'core', SWAP)  16.8 us
    ppermute x4, starting transfers between devices, shifted(): return lax.ppermute(value, BLK, route)  16.5 us
    ppermute x2, starting transfers between devices, halo(): swapped = lax.ppermute(block, 'core', SWAP)  7.91 us
    pallas_call x4, Pallas kernels, body(): pl.pallas_call(build_more, in_specs=[SMEM] + [VMEM] * (2 + len(blocks)),...  7.89 us
    ppermute x2, starting transfers between devices, halo(): down_swapped = lax.ppermute(down, 'core', SWAP)  6.85 us
    ppermute x4, waiting for transfers between devices, shifted(): return lax.ppermute(value, BLK, route)  6.27 us
    ppermute x2, starting transfers between devices, halo(): far = lax.ppermute(block, BLK, third)  3.84 us
  transfers between devices with their start and end apart: 12, of which 4 were waited for; matrix products, arithmetic and copies ran while one was open for 0% of the time, Pallas kernels for 6%

profile of v2, /device:TPU:1, one launch (start us, length us, event | category | flops | bytes accessed | tf_op | source)
XLA Modules:
  0.0 142.8 jit_solution(2735797591348907680)
XLA Ops:
  2.4 24.8 %all_to_all.20.block_ref = bf16[8,128,256]{2,1,0:T(8,128)(2,1)S(1)} all-to-all(bf16[8,128,256]{2,1,0:T(8,128)(2,1)S(1)} %broadcast_in_dim.10), channel_id=1, replica_groups=mesh['y_lo'=4,'z'=8,'core'=2,'x'=4,'y_hi'=2] {'x','y_hi'}, dimensions={0} | all-to-all | bytes 1048576 | tf_op jit(solution)/shard_map/all_to_all | solution.py:150
  27.2 9.3 %collective-permute-start.3 = (bf16[8,128,256]{2,1,0:T(8,128)(2,1)S(1)}, bf16[8,128,256]{2,1,0:T(8,128)(2,1)S(1)}, u32[]{:S(2)}, u32[]{:S(2)}) collective-permute-start(bf16[8,128,256]{2,1,0:T(8,128)(2,1)S(1)} %all_to_all.20.block_ref), channel_id=1, source_target_pairs={{16,0},{24,8},{32,16},{40,24},{48,32},{56,40},{64,48},{72,56},{80,... | collective-permute-start | bytes 1572872 | tf_op jit(solution)/shard_map/ppermute | solution.py:145
  36.5 1.9 %collective-permute-start.2 = (bf16[8,128,256]{2,1,0:T(8,128)(2,1)S(1)}, bf16[8,128,256]{2,1,0:T(8,128)(2,1)S(1)}, u32[]{:S(2)}, u32[]{:S(2)}) collective-permute-start(bf16[8,128,256]{2,1,0:T(8,128)(2,1)S(1)} %all_to_all.20.block_ref), channel_id=1, source_target_pairs={{496,0},{504,8},{0,16},{8,24},{16,32},{24,40},{32,48},{40,56},{48,... | collective-permute-start | bytes 1572872 | tf_op jit(solution)/shard_map/ppermute | solution.py:145
  38.4 4.3 %collective-permute-start = (bf16[8,128,256]{2,1,0:T(8,128)(2,1)S(1)}, bf16[8,128,256]{2,1,0:T(8,128)(2,1)S(1)}, u32[]{:S(2)}, u32[]{:S(2)}) collective-permute-start(bf16[8,128,256]{2,1,0:T(8,128)(2,1)S(1)} %all_to_all.20.block_ref), channel_id=1, source_target_pairs={{0,8},{8,0},{1,9},{9,1},{2,10},{10,2},{3,11},{11,3},{4,12},{12,4},... | collective-permute-start | bytes 1572872 | tf_op jit(solution)/shard_map/ppermute | solution.py:154
  42.7 1.9 %collective-permute-start.1 = (bf16[8,128,256]{2,1,0:T(8,128)(2,1)S(1)}, bf16[8,128,256]{2,1,0:T(8,128)(2,1)S(1)}, u32[]{:S(2)}, u32[]{:S(2)}) collective-permute-start(bf16[8,128,256]{2,1,0:T(8,128)(2,1)S(1)} %all_to_all.20.block_ref), channel_id=1, source_target_pairs={{0,488},{8,32},{16,504},{24,48},{32,8},{40,64},{48,24},{56,80},{64... | collective-permute-start | bytes 1572872 | tf_op jit(solution)/shard_map/ppermute | solution.py:157
  45.6 4.9 %collective-permute-start.5 = (bf16[8,128,256]{2,1,0:T(8,128)(2,1)S(1)}, bf16[8,128,256]{2,1,0:T(8,128)(2,1)S(1)}, u32[]{:S(2)}, u32[]{:S(2)}) collective-permute-start(bf16[8,128,256]{2,1,0:T(8,128)(2,1)S(1)} %collective-permute-done.3.refs_1_), channel_id=1, source_target_pairs={{0,8},{8,0},{1,9},{9,1},{2,10},{10,2},{3,11},{11,3},{4,12},{12,4},... | collective-permute-start | bytes 1572872 | tf_op jit(solution)/shard_map/ppermute | solution.py:159
  50.5 3.8 %collective-permute-done.2.refs_0_ = bf16[8,128,256]{2,1,0:T(8,128)(2,1)S(1)} collective-permute-done((bf16[8,128,256]{2,1,0:T(8,128)(2,1)S(1)}, bf16[8,128,256]{2,1,0:T(8,128)(2,1)S(1)}, u32[]{:S(2)}, u32[]{:S(2)}) %collective-permute-start.2) | collective-permute-done | bytes 524320 | tf_op jit(solution)/shard_map/ppermute | solution.py:145
  54.3 12.8 %collective-permute-start.4 = (bf16[8,128,256]{2,1,0:T(8,128)(2,1)S(1)}, bf16[8,128,256]{2,1,0:T(8,128)(2,1)}, u32[]{:S(2)}, u32[]{:S(2)}) collective-permute-start(bf16[8,128,256]{2,1,0:T(8,128)(2,1)S(1)} %collective-permute-done.2.refs_0_), channel_id=1, source_target_pairs={{0,8},{8,0},{1,9},{9,1},{2,10},{10,2},{3,11},{11,3},{4,12},{12,4},... | collective-permute-start | bytes 1572872 | tf_op jit(solution)/shard_map/ppermute | solution.py:158
  67.2 1.2 shard_map.59
  69.6 1.1 shard_map.61
  70.7 2.6 %shard_map.62 = (f32[64,256]{1,0:T(8,128)S(1)}, bf16[2,8,256,256]{3,2,1,0:T(8,128)(2,1)S(1)}) custom-call(f32[2]{0:T(128)S(1)} %broadcast_1_level_ref.2.level_ref, bf16[256,144]{1,0:T(8,128)(2,1)S(1)} %get-tuple-element.15.weights_ref, f32[64,256]{1,0:T(8,128)S(1)} %get-tuple-element.18.before_ref, bf16[8,128,256]{2,1,0:T(8,128)(2,1)S(1)} %collective-permute-done.2.refs_0_, ...), custom_call_target="tpu_custom_call" | custom-call | tf_op jit(solution)/shard_map/pallas_call | solution.py:189
  73.3 3.1 %shard_map.63 = (f32[64,256]{1,0:T(8,128)S(1)}, bf16[2,8,256,256]{3,2,1,0:T(8,128)(2,1)S(1)}) custom-call(f32[2]{0:T(128)S(1)} %pad_maximum_fusion.1.level_ref, bf16[256,144]{1,0:T(8,128)(2,1)S(1)} %get-tuple-element.15.weights_ref, f32[64,256]{1,0:T(8,128)S(1)} %get-tuple-element.19.before_ref, bf16[8,128,256]{2,1,0:T(8,128)(2,1)} %collective-permute-done.4.refs_0_, ...), custom_call_target="tpu_custom_call" | custom-call | tf_op jit(solution)/shard_map/pallas_call | solution.py:189
  76.5 13.5 %all_to_all.21.refs_0_ = bf16[8,64,256]{2,1,0:T(8,128)(2,1)S(1)} all-to-all(bf16[8,64,256]{2,1,0:T(8,128)(2,1)S(1)} %broadcast_in_dim.11), channel_id=1, replica_groups=mesh['y_lo'=4,'z'=8,'core'=2,'x'=4,'y_hi'=2] {'x','y_hi'}, dimensions={0} | all-to-all | bytes 524288 | tf_op jit(solution)/shard_map/all_to_all | solution.py:150
  89.9 1.9 %collective-permute-start.9 = (bf16[8,64,256]{2,1,0:T(8,128)(2,1)S(1)}, bf16[8,64,256]{2,1,0:T(8,128)(2,1)S(1)}, u32[]{:S(2)}, u32[]{:S(2)}) collective-permute-start(bf16[8,64,256]{2,1,0:T(8,128)(2,1)S(1)} %all_to_all.21.refs_0_), channel_id=1, source_target_pairs={{16,0},{24,8},{32,16},{40,24},{48,32},{56,40},{64,48},{72,56},{80,... | collective-permute-start | bytes 786440 | tf_op jit(solution)/shard_map/ppermute | solution.py:145
  91.8 3.4 %collective-permute-start.8 = (bf16[8,64,256]{2,1,0:T(8,128)(2,1)S(1)}, bf16[8,64,256]{2,1,0:T(8,128)(2,1)S(1)}, u32[]{:S(2)}, u32[]{:S(2)}) collective-permute-start(bf16[8,64,256]{2,1,0:T(8,128)(2,1)S(1)} %all_to_all.21.refs_0_), channel_id=1, source_target_pairs={{496,0},{504,8},{0,16},{8,24},{16,32},{24,40},{32,48},{40,56},{48,... | collective-permute-start | bytes 786440 | tf_op jit(solution)/shard_map/ppermute | solution.py:145
  95.2 3.6 %collective-permute-start.6 = (bf16[8,64,256]{2,1,0:T(8,128)(2,1)S(1)}, bf16[8,64,256]{2,1,0:T(8,128)(2,1)S(1)}, u32[]{:S(2)}, u32[]{:S(2)}) collective-permute-start(bf16[8,64,256]{2,1,0:T(8,128)(2,1)S(1)} %all_to_all.21.refs_0_), channel_id=1, source_target_pairs={{0,8},{8,0},{1,9},{9,1},{2,10},{10,2},{3,11},{11,3},{4,12},{12,4},... | collective-permute-start | bytes 786440 | tf_op jit(solution)/shard_map/ppermute | solution.py:154
  98.8 1.9 %collective-permute-start.7 = (bf16[8,64,256]{2,1,0:T(8,128)(2,1)S(1)}, bf16[8,64,256]{2,1,0:T(8,128)(2,1)S(1)}, u32[]{:S(2)}, u32[]{:S(2)}) collective-permute-start(bf16[8,64,256]{2,1,0:T(8,128)(2,1)S(1)} %all_to_all.21.refs_0_), channel_id=1, source_target_pairs={{0,488},{8,32},{16,504},{24,48},{32,8},{40,64},{48,24},{56,80},{64... | collective-permute-start | bytes 786440 | tf_op jit(solution)/shard_map/ppermute | solution.py:157
  100.8 1.9 %collective-permute-start.11 = (bf16[8,64,256]{2,1,0:T(8,128)(2,1)S(1)}, bf16[8,64,256]{2,1,0:T(8,128)(2,1)S(1)}, u32[]{:S(2)}, u32[]{:S(2)}) collective-permute-start(bf16[8,64,256]{2,1,0:T(8,128)(2,1)S(1)} %collective-permute-done.9.refs_1_), channel_id=1, source_target_pairs={{0,8},{8,0},{1,9},{9,1},{2,10},{10,2},{3,11},{11,3},{4,12},{12,4},... | collective-permute-start | bytes 786440 | tf_op jit(solution)/shard_map/ppermute | solution.py:159
  102.7 1.6 %collective-permute-done.8.refs_0_ = bf16[8,64,256]{2,1,0:T(8,128)(2,1)S(1)} collective-permute-done((bf16[8,64,256]{2,1,0:T(8,128)(2,1)S(1)}, bf16[8,64,256]{2,1,0:T(8,128)(2,1)S(1)}, u32[]{:S(2)}, u32[]{:S(2)}) %collective-permute-start.8) | collective-permute-done | bytes 262176 | tf_op jit(solution)/shard_map/ppermute | solution.py:145
  104.3 4.0 %collective-permute-start.10 = (bf16[8,64,256]{2,1,0:T(8,128)(2,1)S(1)}, bf16[8,64,256]{2,1,0:T(8,128)(2,1)S(1)}, u32[]{:S(2)}, u32[]{:S(2)}) collective-permute-start(bf16[8,64,256]{2,1,0:T(8,128)(2,1)S(1)} %collective-permute-done.8.refs_0_), channel_id=1, source_target_pairs={{0,8},{8,0},{1,9},{9,1},{2,10},{10,2},{3,11},{11,3},{4,12},{12,4},... | collective-permute-start | bytes 786440 | tf_op jit(solution)/shard_map/ppermute | solution.py:158
  109.2 1.8 %collective-permute-done.7.refs_0_ = bf16[8,64,256]{2,1,0:T(8,128)(2,1)S(1)} collective-permute-done((bf16[8,64,256]{2,1,0:T(8,128)(2,1)S(1)}, bf16[8,64,256]{2,1,0:T(8,128)(2,1)S(1)}, u32[]{:S(2)}, u32[]{:S(2)}) %collective-permute-start.7) | collective-permute-done | bytes 262176 | tf_op jit(solution)/shard_map/ppermute | solution.py:157
  112.2 1.3 shard_map.68
  113.5 15.5 %all_to_all.22 = f32[32,8,128]{2,1,0:T(8,128)S(1)} all-to-all(f32[32,8,128]{2,1,0:T(8,128)S(1)} %broadcast_in_dim.13), channel_id=1, replica_groups=mesh['y_lo'=4,'z'=8,'core'=2,'x'=4,'y_hi'=2] {'x','y_hi','y_lo'}, dimensions={0} | all-to-all | bytes 262144 | tf_op jit(solution)/shard_map/all_to_all | solution.py:150
  129.1 12.9 %all_to_all.23 = f32[16,8,128]{2,1,0:T(8,128)S(1)} all-to-all(f32[16,8,128]{2,1,0:T(8,128)S(1)} %broadcast_in_dim.14), channel_id=1, replica_groups=mesh['y_lo'=4,'z'=8,'core'=2,'x'=4,'y_hi'=2] {'z','core'}, dimensions={0} | all-to-all | bytes 131072 | tf_op jit(solution)/shard_map/all_to_all | solution.py:150
  (34 shorter events, 6.8 us)
Async XLA Ops:
  27.2 18.4 %collective-permute-start.3 = (bf16[8,128,256]{2,1,0:T(8,128)(2,1)S(1)}, bf16[8,128,256]{2,1,0:T(8,128)(2,1)S(1)}, u32[]{:S(2)}, u32[]{:S(2)}) collective-permute-start(bf16[8,128,256]{2,1,0:T(8,128)(2,1)S(1)} %all_to_all.20.block_ref), channel_id=1, source_target_pairs={{16,0},{24,8},{32,16},{40,24},{48,32},{56,40},{64,48},{72,56},{80,... | collective-permute-start | bytes 1572872 | tf_op jit(solution)/shard_map/ppermute | solution.py:145
  36.5 17.8 %collective-permute-start.2 = (bf16[8,128,256]{2,1,0:T(8,128)(2,1)S(1)}, bf16[8,128,256]{2,1,0:T(8,128)(2,1)S(1)}, u32[]{:S(2)}, u32[]{:S(2)}) collective-permute-start(bf16[8,128,256]{2,1,0:T(8,128)(2,1)S(1)} %all_to_all.20.block_ref), channel_id=1, source_target_pairs={{496,0},{504,8},{0,16},{8,24},{16,32},{24,40},{32,48},{40,56},{48,... | collective-permute-start | bytes 1572872 | tf_op jit(solution)/shard_map/ppermute | solution.py:145
  38.4 30.0 %collective-permute-start = (bf16[8,128,256]{2,1,0:T(8,128)(2,1)S(1)}, bf16[8,128,256]{2,1,0:T(8,128)(2,1)S(1)}, u32[]{:S(2)}, u32[]{:S(2)}) collective-permute-start(bf16[8,128,256]{2,1,0:T(8,128)(2,1)S(1)} %all_to_all.20.block_ref), channel_id=1, source_target_pairs={{0,8},{8,0},{1,9},{9,1},{2,10},{10,2},{3,11},{11,3},{4,12},{12,4},... | collective-permute-start | bytes 1572872 | tf_op jit(solution)/shard_map/ppermute | solution.py:154
  42.7 26.8 %collective-permute-start.1 = (bf16[8,128,256]{2,1,0:T(8,128)(2,1)S(1)}, bf16[8,128,256]{2,1,0:T(8,128)(2,1)S(1)}, u32[]{:S(2)}, u32[]{:S(2)}) collective-permute-start(bf16[8,128,256]{2,1,0:T(8,128)(2,1)S(1)} %all_to_all.20.block_ref), channel_id=1, source_target_pairs={{0,488},{8,32},{16,504},{24,48},{32,8},{40,64},{48,24},{56,80},{64... | collective-permute-start | bytes 1572872 | tf_op jit(solution)/shard_map/ppermute | solution.py:157
  45.6 27.7 %collective-permute-start.5 = (bf16[8,128,256]{2,1,0:T(8,128)(2,1)S(1)}, bf16[8,128,256]{2,1,0:T(8,128)(2,1)S(1)}, u32[]{:S(2)}, u32[]{:S(2)}) collective-permute-start(bf16[8,128,256]{2,1,0:T(8,128)(2,1)S(1)} %collective-permute-done.3.refs_1_), channel_id=1, source_target_pairs={{0,8},{8,0},{1,9},{9,1},{2,10},{10,2},{3,11},{11,3},{4,12},{12,4},... | collective-permute-start | bytes 1572872 | tf_op jit(solution)/shard_map/ppermute | solution.py:159
  54.3 19.0 %collective-permute-start.4 = (bf16[8,128,256]{2,1,0:T(8,128)(2,1)S(1)}, bf16[8,128,256]{2,1,0:T(8,128)(2,1)}, u32[]{:S(2)}, u32[]{:S(2)}) collective-permute-start(bf16[8,128,256]{2,1,0:T(8,128)(2,1)S(1)} %collective-permute-done.2.refs_0_), channel_id=1, source_target_pairs={{0,8},{8,0},{1,9},{9,1},{2,10},{10,2},{3,11},{11,3},{4,12},{12,4},... | collective-permute-start | bytes 1572872 | tf_op jit(solution)/shard_map/ppermute | solution.py:158
  68.4 8.0 %copy-start = (f32[64,256]{1,0:T(8,128)S(1)}, f32[64,256]{1,0:T(8,128)}, u32[]{:S(2)}) copy-start(f32[64,256]{1,0:T(8,128)} %first_ref.1) | copy-start | bytes 196612
  68.4 8.0 %copy-start.1 = (f32[256]{0:T(256)S(1)}, f32[256]{0:T(256)}, u32[]{:S(2)}) copy-start(f32[256]{0:T(256)} %param.6) | copy-start | bytes 3076
  89.9 10.8 %collective-permute-start.9 = (bf16[8,64,256]{2,1,0:T(8,128)(2,1)S(1)}, bf16[8,64,256]{2,1,0:T(8,128)(2,1)S(1)}, u32[]{:S(2)}, u32[]{:S(2)}) collective-permute-start(bf16[8,64,256]{2,1,0:T(8,128)(2,1)S(1)} %all_to_all.21.refs_0_), channel_id=1, source_target_pairs={{16,0},{24,8},{32,16},{40,24},{48,32},{56,40},{64,48},{72,56},{80,... | collective-permute-start | bytes 786440 | tf_op jit(solution)/shard_map/ppermute | solution.py:145
  91.8 12.5 %collective-permute-start.8 = (bf16[8,64,256]{2,1,0:T(8,128)(2,1)S(1)}, bf16[8,64,256]{2,1,0:T(8,128)(2,1)S(1)}, u32[]{:S(2)}, u32[]{:S(2)}) collective-permute-start(bf16[8,64,256]{2,1,0:T(8,128)(2,1)S(1)} %all_to_all.21.refs_0_), channel_id=1, source_target_pairs={{496,0},{504,8},{0,16},{8,24},{16,32},{24,40},{32,48},{40,56},{48,... | collective-permute-start | bytes 786440 | tf_op jit(solution)/shard_map/ppermute | solution.py:145
  95.2 13.5 %collective-permute-start.6 = (bf16[8,64,256]{2,1,0:T(8,128)(2,1)S(1)}, bf16[8,64,256]{2,1,0:T(8,128)(2,1)S(1)}, u32[]{:S(2)}, u32[]{:S(2)}) collective-permute-start(bf16[8,64,256]{2,1,0:T(8,128)(2,1)S(1)} %all_to_all.21.refs_0_), channel_id=1, source_target_pairs={{0,8},{8,0},{1,9},{9,1},{2,10},{10,2},{3,11},{11,3},{4,12},{12,4},... | collective-permute-start | bytes 786440 | tf_op jit(solution)/shard_map/ppermute | solution.py:154
  98.8 12.1 %collective-permute-start.7 = (bf16[8,64,256]{2,1,0:T(8,128)(2,1)S(1)}, bf16[8,64,256]{2,1,0:T(8,128)(2,1)S(1)}, u32[]{:S(2)}, u32[]{:S(2)}) collective-permute-start(bf16[8,64,256]{2,1,0:T(8,128)(2,1)S(1)} %all_to_all.21.refs_0_), channel_id=1, source_target_pairs={{0,488},{8,32},{16,504},{24,48},{32,8},{40,64},{48,24},{56,80},{64... | collective-permute-start | bytes 786440 | tf_op jit(solution)/shard_map/ppermute | solution.py:157
  100.8 11.4 %collective-permute-start.11 = (bf16[8,64,256]{2,1,0:T(8,128)(2,1)S(1)}, bf16[8,64,256]{2,1,0:T(8,128)(2,1)S(1)}, u32[]{:S(2)}, u32[]{:S(2)}) collective-permute-start(bf16[8,64,256]{2,1,0:T(8,128)(2,1)S(1)} %collective-permute-done.9.refs_1_), channel_id=1, source_target_pairs={{0,8},{8,0},{1,9},{9,1},{2,10},{10,2},{3,11},{11,3},{4,12},{12,4},... | collective-permute-start | bytes 786440 | tf_op jit(solution)/shard_map/ppermute | solution.py:159
  104.3 7.9 %collective-permute-start.10 = (bf16[8,64,256]{2,1,0:T(8,128)(2,1)S(1)}, bf16[8,64,256]{2,1,0:T(8,128)(2,1)S(1)}, u32[]{:S(2)}, u32[]{:S(2)}) collective-permute-start(bf16[8,64,256]{2,1,0:T(8,128)(2,1)S(1)} %collective-permute-done.8.refs_0_), channel_id=1, source_target_pairs={{0,8},{8,0},{1,9},{9,1},{2,10},{10,2},{3,11},{11,3},{4,12},{12,4},... | collective-permute-start | bytes 786440 | tf_op jit(solution)/shard_map/ppermute | solution.py:158

commit v3 on v2

v3 whole, which is shorter than its diff:
```python
import math

import jax
import jax.numpy as jnp
from jax import lax
from jax.experimental import pallas as pl
from jax.experimental.pallas import tpu as pltpu
from jax.sharding import Mesh, PartitionSpec as P

F32, BF16 = jnp.float32, jnp.bfloat16
AXES = ("y_lo", "z", "core", "x", "y_hi")
SIZES = (4, 8, 2, 4, 2)
BLK = ("y_lo", "z", "core")
N_BLK = 64
SWAP = ((0, 1), (1, 0))

LN2 = math.log(2.0)
UNIT = math.sqrt(5.0) / LN2
SHIFT = 1.5 / LN2
OFFSET = 0.75 / LN2**2
LEVEL = math.log2(LN2**2 / 3.0) + SHIFT
LEVELS = tuple(LEVEL + math.log2(taper) for taper in (1.0, 0.75, 0.5, 0.25))
TINY = 1e-20

FEAT = 32
RHS = 64
WIDTH = 256
DEPTH = 144
SHARDS = 8
SIGMA = 0.5
NT = (((1,), (1,)), ((), ()))


def split(value):
    high = lax.reduce_precision(value, 8, 7)
    return high.astype(BF16), (value - high).astype(BF16)


def square_rows(coords, first, second):
    squares = jnp.sum(coords * coords, axis=0, keepdims=True)
    one = squares.astype(BF16).astype(F32)
    two = (squares - one).astype(BF16).astype(F32)
    three = squares - one - two
    row = lax.broadcasted_iota(jnp.int32, (16, coords.shape[1]), 0)
    out = jnp.where((row >= second) & (row < second + 3), 1.0, 0.0)
    for at, piece in enumerate((one, two, three)):
        out = jnp.where(row == first + at, piece, out)
    return out.astype(BF16)


def build_shard(weights, levels, shard, cols_ref, dist_ref, kernel_ref):
    coords = shard[: 2 * FEAT]
    wide = coords.astype(F32)
    cols_ref[: 2 * FEAT] = coords
    cols_ref[2 * FEAT : 4 * FEAT] = coords
    cols_ref[4 * FEAT :] = square_rows(wide[:FEAT] + wide[FEAT:], 0, 3)
    dist_ref[...] = jnp.dot(weights, cols_ref[...], preferred_element_type=F32)
    step = 64
    for half, level in enumerate(levels):
        for at in range(half * WIDTH, (half + 1) * WIDTH, step):
            part = jnp.maximum(dist_ref[at : at + step], TINY)
            moved = part * lax.rsqrt(part) + SHIFT
            entry = (moved * moved + OFFSET) * jnp.exp2(level - moved)
            kernel_ref[at : at + step] = entry.astype(BF16)
    return lax.dot_general(shard[2 * FEAT :], kernel_ref[...], NT, preferred_element_type=F32)


def build_block(weights, levels, block_ref, cols_ref, dist_ref, kernel_ref):
    total = None
    for i in range(SHARDS):
        part = build_shard(weights, levels, block_ref[i], cols_ref.at[i % 2], dist_ref.at[i % 2], kernel_ref.at[i])
        total = part if total is None else total + part
    return total


def build_first(own_ref, peer_ref, block_ref, weights_ref, total_ref, kernel_ref, cols_ref, dist_ref):
    for at, ref in enumerate((own_ref, peer_ref)):
        rows = slice(at * WIDTH, (at + 1) * WIDTH)
        coords = ref[: 2 * FEAT].astype(F32)
        high, low = coords[:FEAT], coords[FEAT:]
        extra = square_rows(high + low, 3, 0).astype(F32)
        stacked = jnp.concatenate([-2.0 * high, -2.0 * high, -2.0 * low, -2.0 * low], axis=0)
        weights_ref[rows, : 4 * FEAT] = jnp.transpose(stacked).astype(BF16)
        weights_ref[rows, 4 * FEAT :] = jnp.transpose(extra).astype(BF16)
    total_ref[...] = build_block(weights_ref[...], LEVELS[:2], block_ref, cols_ref, dist_ref, kernel_ref)


def build_more(level_ref, weights_ref, before_ref, block_ref, total_ref, kernel_ref, cols_ref, dist_ref):
    levels = (level_ref[0], level_ref[1])
    total_ref[...] = before_ref[...] + build_block(
        weights_ref[...], levels, block_ref, cols_ref, dist_ref, kernel_ref
    )


def build_far(weights_ref, before_ref, block_ref, total_ref, kernel_ref, cols_ref, dist_ref):
    total_ref[...] = before_ref[:, WIDTH:] + build_block(
        weights_ref[WIDTH:], LEVELS[3:], block_ref, cols_ref, dist_ref, kernel_ref
    )


def add_block(total, kernel_ref, block_ref):
    for i in range(SHARDS):
        total = total + lax.dot_general(block_ref[i], kernel_ref[i], NT, preferred_element_type=F32)
    return total


def apply_first(kernel_ref, block_ref, total_ref):
    total_ref[...] = add_block(jnp.zeros(total_ref.shape, F32), kernel_ref, block_ref)


def apply_more(kernel_ref, before_ref, block_ref, total_ref):
    total_ref[...] = add_block(before_ref[...], kernel_ref, block_ref)


def apply_far(kernel_ref, before_ref, block_ref, total_ref):
    total_ref[...] = add_block(before_ref[:, WIDTH:], kernel_ref, block_ref)


def row_sums(sums_ref, at, products):
    ones = jnp.ones((8, WIDTH), F32)
    row = lax.broadcasted_iota(jnp.int32, (8, RHS), 0)
    out = jnp.zeros((8, RHS), F32)
    for i, product in enumerate(products):
        total = lax.dot_general(ones, product, NT, precision=lax.Precision.HIGHEST, preferred_element_type=F32)
        out = jnp.where(row == at + i, total, out)
    sums_ref[:, :RHS] = out
    sums_ref[:, RHS:] = jnp.zeros_like(out)


def early_sums(first_ref, image_ref, sums_ref):
    first, image = first_ref[...], image_ref[...]
    row_sums(sums_ref, 0, (first * first, first * image, image * image))


def late_sums(early_ref, noise_ref, first_ref, first_total_ref, image_ref, own_ref, peer_ref, second_ref, sums_ref):
    first, image = first_ref[...], image_ref[...]
    total = own_ref[:, :WIDTH] + peer_ref[...]
    second = noise_ref[...] * image + (first_total_ref[...] - total) * (1.0 / SIGMA)
    second_ref[...] = second
    row_sums(sums_ref, 3, (first * second, image * second))
    sums_ref[...] += early_ref[...]


VMEM_LIMIT = pltpu.CompilerParams(vmem_limit_bytes=48 * 1024 * 1024)
SMEM = pl.BlockSpec(memory_space=pltpu.SMEM)
VMEM = pl.BlockSpec(memory_space=pltpu.VMEM)


def scratch(rows=2 * WIDTH):
    return [pltpu.VMEM((2, DEPTH, WIDTH), BF16), pltpu.VMEM((2, rows, WIDTH), F32)]


def shape(*dims, dtype=F32):
    return jax.ShapeDtypeStruct(dims, dtype)


def shifted(value, distance):
    route = [((i - distance) % N_BLK, i) for i in range(N_BLK)]
    return lax.ppermute(value, BLK, route)


def gathered(value, axes):
    count = math.prod(SIZES[AXES.index(axis)] for axis in axes)
    return lax.all_to_all(jnp.broadcast_to(value[None], (count,) + value.shape), axes, 0, 0)


def halo(block):
    fourth = [(i, (i - 4 if i % 2 == 0 else i + 4) % N_BLK) for i in range(N_BLK)]
    return lax.ppermute(block, BLK, fourth), shifted(block, 2), shifted(block, -2)


def kernel_shape(rows=2 * WIDTH):
    return shape(SHARDS, rows, WIDTH, dtype=BF16)


def call(body, out_shape, in_specs=None, scratch_shapes=()):
    extra = {} if in_specs is None else {"in_specs": in_specs}
    return pl.pallas_call(
        body, out_shape=out_shape, scratch_shapes=scratch_shapes, compiler_params=VMEM_LIMIT, **extra
    )


def body(points, lengthscale, noise_var, targets):
    coords = points / lengthscale[:, None] * UNIT
    message = jnp.concatenate(split(coords) + (targets.astype(BF16),), axis=0)
    block = gathered(message, ("x", "y_hi"))
    peer = lax.ppermute(message[: 2 * FEAT], "core", SWAP)
    far, up, down = halo(block)

    odd = lax.axis_index("core") == 1
    near_far = jnp.where(odd, LEVELS[1], LEVELS[3]), jnp.where(odd, LEVELS[3], LEVELS[1])
    weights, total, kernel_own = call(
        build_first,
        (shape(2 * WIDTH, DEPTH, dtype=BF16), shape(RHS, 2 * WIDTH), kernel_shape()),
        scratch_shapes=scratch(),
    )(message, peer, block)
    kernels = []
    for moved, level in zip((up, down), near_far):
        total, made = call(
            build_more,
            (shape(RHS, 2 * WIDTH), kernel_shape()),
            in_specs=[SMEM] + [VMEM] * 3,
            scratch_shapes=scratch(),
        )(jnp.stack([jnp.asarray(LEVELS[2], F32), level]), weights, total, moved)
        kernels.append(made)
    peer_total, kernel_far = call(
        build_far, (shape(RHS, WIDTH), kernel_shape(WIDTH)), scratch_shapes=scratch(WIDTH)
    )(weights, total, far)

    noise = noise_var[None, :]
    first_total = total[:, :WIDTH] + lax.ppermute(peer_total, "core", SWAP)
    image = noise * targets + first_total
    block = gathered((targets - SIGMA * image).astype(BF16), ("x", "y_hi"))
    far, up, down = halo(block)
    early = call(early_sums, shape(8, 2 * RHS))(targets, image)
    total = call(apply_first, shape(RHS, 2 * WIDTH))(kernel_own, block)
    for made, moved in zip(kernels, (up, down)):
        total = call(apply_more, shape(RHS, 2 * WIDTH))(made, total, moved)
    peer_total = call(apply_far, shape(RHS, WIDTH))(kernel_far, total, far)
    peer_total = lax.ppermute(peer_total, "core", SWAP)
    second, sums = call(late_sums, (shape(RHS, WIDTH), shape(8, 2 * RHS)))(
        early, noise, targets, first_total, image, total, peer_total
    )
    for axes in (("x", "y_hi", "y_lo"), ("z", "core")):
        sums = jnp.sum(gathered(sums, axes), axis=0)

    rr, rq, qq, rs, qs = (sums[i, :RHS] for i in range(5))
    step = rr / rq
    norm_next = jnp.maximum(rr - 2.0 * step * rq + step * step * qq, 0.0)
    grown = 1.0 + norm_next / rr
    curvature = grown * grown * rq - step * grown * (qq + rs) + step * step * qs
    step_next = norm_next / curvature
    along = (step + step_next * grown)[:, None]
    across = (step_next * step)[:, None]
    solution = along * targets - across * image
    residual = targets - along * image + across * second
    return solution, residual


def solution(mesh):
    fine = Mesh(mesh.devices.reshape(SIZES), AXES)
    placed = (P(None, AXES), P(), P(AXES), P(None, AXES))
    return jax.shard_map(
        body, mesh=fine, in_specs=placed, out_specs=(P(None, AXES), P(None, AXES)), check_vma=False
    )
```

time: 143 us -> 140 us (0.979)
  starting transfers between devices: 51.8 us -> 40.5 us
  waiting for transfers between devices: 8.08 us -> 12.1 us
  blocking collectives: 66.7 us -> 70.1 us
    ppermute x8 -> x5, starting transfers between devices: 35.4 us -> 20.1 us  [the longest x1 6.29 us: body(): peer = lax.ppermute(message[:2 * FEAT], 'core', SWAP)]
    ppermute x8 -> x5, waiting for transfers between devices: 1.81 us -> 12.1 us  [the longest x2 9.88 us: halo(): lax.ppermute(block, BLK, fourth)]
    ppermute x4, waiting for transfers between devices: 6.27 us -> 0.01 us  [shifted(): return lax.ppermute(value, BLK, route)]
    ppermute x4, starting transfers between devices: 16.5 us -> 20.4 us  [shifted(): return lax.ppermute(value, BLK, route)]
    all_to_all x4, blocking collectives: 66.7 us -> 70.1 us  [gathered(): lax.all_to_all(jnp.broadcast_to(value[None], (count,) + value.shape), axe...]
  transfers between devices with their start and end apart: 12 -> 9, of which waited for: 4 -> 5; matrix products, arithmetic and copies ran while one was open for 0% -> 0% of each run, Pallas kernels for 6% -> 8%
where the time goes in v3:
time: 140 us; the launch traced here: 139 us
  blocking collectives  70.1 us (50%)
  starting transfers between devices  40.5 us (29%)
  Pallas kernels  13.1 us (9%)
  waiting for transfers between devices  12.1 us (9%)
  other arithmetic  2.7 us (2%)
    all_to_all x4, blocking collectives, gathered(): lax.all_to_all(jnp.broadcast_to(value[None], (count,) + value.shape), axe...  70.1 us
    ppermute x4, starting transfers between devices, shifted(): return lax.ppermute(value, BLK, route)  20.4 us
    ppermute x2, waiting for transfers between devices, halo(): lax.ppermute(block, BLK, fourth)  9.88 us
    ppermute x1, starting transfers between devices, body(): peer = lax.ppermute(message[:2 * FEAT], 'core', SWAP)  6.29 us
    pallas_call x2, Pallas kernels, body(): call(build_more, (shape(RHS, 2 * WIDTH), kernel_shape()), in_specs=[SMEM]...  6.14 us
    ppermute x1, starting transfers between devices, body(): first_total = total[:, :WIDTH] + lax.ppermute(peer_total, 'core', SWAP)  5.99 us
    ppermute x1, starting transfers between devices, body(): peer_total = lax.ppermute(peer_total, 'core', SWAP)  3.98 us
    ppermute x2, starting transfers between devices, halo(): lax.ppermute(block, BLK, fourth)  3.84 us
  transfers between devices with their start and end apart: 9, of which 5 were waited for; matrix products, arithmetic and copies ran while one was open for 0% of the time, Pallas kernels for 8%

profile of v3, /device:TPU:1, one launch (start us, length us, event | category | flops | bytes accessed | tf_op | source)
XLA Modules:
  0.0 139.5 jit_solution(16265363400852850074)
XLA Ops:
  0.6 0.8 convert_element_type.14
  1.5 0.8 reduce-precision_convert_fusion
  2.4 25.0 %all_to_all.20.block_ref = bf16[8,128,256]{2,1,0:T(8,128)(2,1)S(1)} all-to-all(bf16[8,128,256]{2,1,0:T(8,128)(2,1)S(1)} %broadcast_in_dim.10), channel_id=1, replica_groups=mesh['y_lo'=4,'z'=8,'core'=2,'x'=4,'y_hi'=2] {'x','y_hi'}, dimensions={0} | all-to-all | bytes 1048576 | tf_op jit(solution)/shard_map/all_to_all | solution.py:164
  27.4 4.0 %collective-permute-start.1 = (bf16[8,128,256]{2,1,0:T(8,128)(2,1)S(1)}, bf16[8,128,256]{2,1,0:T(8,128)(2,1)S(1)}, u32[]{:S(2)}, u32[]{:S(2)}) collective-permute-start(bf16[8,128,256]{2,1,0:T(8,128)(2,1)S(1)} %all_to_all.20.block_ref), channel_id=1, source_target_pairs={{496,0},{504,8},{0,16},{8,24},{16,32},{24,40},{32,48},{40,56},{48,... | collective-permute-start | bytes 1572872 | tf_op jit(solution)/shard_map/ppermute | solution.py:159
  31.4 7.2 %collective-permute-start.2 = (bf16[8,128,256]{2,1,0:T(8,128)(2,1)S(1)}, bf16[8,128,256]{2,1,0:T(8,128)(2,1)S(1)}, u32[]{:S(2)}, u32[]{:S(2)}) collective-permute-start(bf16[8,128,256]{2,1,0:T(8,128)(2,1)S(1)} %all_to_all.20.block_ref), channel_id=1, source_target_pairs={{16,0},{24,8},{32,16},{40,24},{48,32},{56,40},{64,48},{72,56},{80,... | collective-permute-start | bytes 1572872 | tf_op jit(solution)/shard_map/ppermute | solution.py:159
  38.6 1.9 %collective-permute-start.3 = (bf16[8,128,256]{2,1,0:T(8,128)(2,1)S(1)}, bf16[8,128,256]{2,1,0:T(8,128)(2,1)S(1)}, u32[]{:S(2)}, u32[]{:S(2)}) collective-permute-start(bf16[8,128,256]{2,1,0:T(8,128)(2,1)S(1)} %all_to_all.20.block_ref), channel_id=1, source_target_pairs={{0,480},{8,40},{16,496},{24,56},{32,0},{40,72},{48,16},{56,88},{64... | collective-permute-start | bytes 1572872 | tf_op jit(solution)/shard_map/ppermute | solution.py:169
  40.5 6.3 %collective-permute-start = (bf16[64,256]{1,0:T(8,128)(2,1)S(1)}, bf16[64,256]{1,0:T(8,128)(2,1)S(1)}, u32[]{:S(2)}, u32[]{:S(2)}) collective-permute-start(bf16[64,256]{1,0:T(8,128)(2,1)S(1)} %pad_maximum_fusion.1), channel_id=1, source_target_pairs={{0,8},{8,0},{1,9},{9,1},{2,10},{10,2},{3,11},{11,3},{4,12},{12,4},... | collective-permute-start | bytes 98312 | tf_op jit(solution)/shard_map/ppermute | solution.py:187
  47.7 2.7 %shard_map.59 = (bf16[512,144]{1,0:T(8,128)(2,1)S(1)}, f32[64,512]{1,0:T(8,128)S(1)}, bf16[8,512,256]{2,1,0:T(8,128)(2,1)S(1)}) custom-call(bf16[128,256]{1,0:T(8,128)(2,1)S(1)} %pad_maximum_fusion.own_ref, bf16[64,256]{1,0:T(8,128)(2,1)S(1)} %collective-permute-done.peer_ref, bf16[8,128,256]{2,1,0:T(8,128)(2,1)S(1)} %all_to_all.20.block_ref), custom_call_target="tpu_custom_call" | custom-call | tf_op jit(solution)/shard_map/pallas_call | solution.py:192
  50.4 3.1 %shard_map.60 = (f32[64,512]{1,0:T(8,128)S(1)}, bf16[8,512,256]{2,1,0:T(8,128)(2,1)S(1)}) custom-call(f32[2]{0:T(128)S(1)} %pad_maximum_fusion.2.level_ref, bf16[512,144]{1,0:T(8,128)(2,1)S(1)} %get-tuple-element.13.weights_ref, f32[64,512]{1,0:T(8,128)S(1)} %get-tuple-element.14.before_ref, bf16[8,128,256]{2,1,0:T(8,128)(2,1)S(1)} %collective-permute-done.1.block_ref), custom_call_target="tpu_custom_call" | custom-call | tf_op jit(solution)/shard_map/pallas_call | solution.py:199
  53.5 3.1 %shard_map.61 = (f32[64,512]{1,0:T(8,128)S(1)}, bf16[8,512,256]{2,1,0:T(8,128)(2,1)S(1)}) custom-call(f32[2]{0:T(128)S(1)} %pad_maximum_fusion.3.level_ref, bf16[512,144]{1,0:T(8,128)(2,1)S(1)} %get-tuple-element.13.weights_ref, f32[64,512]{1,0:T(8,128)S(1)} %get-tuple-element.15.before_ref, bf16[8,128,256]{2,1,0:T(8,128)(2,1)S(1)} %collective-permute-done.2.block_ref), custom_call_target="tpu_custom_call" | custom-call | tf_op jit(solution)/shard_map/pallas_call | solution.py:199
  56.6 2.0 %collective-permute-done.3.block_ref = bf16[8,128,256]{2,1,0:T(8,128)(2,1)S(1)} collective-permute-done((bf16[8,128,256]{2,1,0:T(8,128)(2,1)S(1)}, bf16[8,128,256]{2,1,0:T(8,128)(2,1)S(1)}, u32[]{:S(2)}, u32[]{:S(2)}) %collective-permute-start.3) | collective-permute-done | bytes 524320 | tf_op jit(solution)/shard_map/ppermute | solution.py:169
  58.6 1.1 shard_map.62
  59.7 6.0 %collective-permute-start.4 = (f32[64,256]{1,0:T(8,128)S(1)}, f32[64,256]{1,0:T(8,128)S(1)}, u32[]{:S(2)}, u32[]{:S(2)}) collective-permute-start(f32[64,256]{1,0:T(8,128)S(1)} %get-tuple-element.17), channel_id=1, source_target_pairs={{0,8},{8,0},{1,9},{9,1},{2,10},{10,2},{3,11},{11,3},{4,12},{12,4},... | collective-permute-start | bytes 196616 | tf_op jit(solution)/shard_map/ppermute | solution.py:211
  65.7 0.9 collective-permute-done.4
  66.6 16.6 %all_to_all.21.block_ref = bf16[8,64,256]{2,1,0:T(8,128)(2,1)S(1)} all-to-all(bf16[8,64,256]{2,1,0:T(8,128)(2,1)S(1)} %broadcast_in_dim.12), channel_id=1, replica_groups=mesh['y_lo'=4,'z'=8,'core'=2,'x'=4,'y_hi'=2] {'x','y_hi'}, dimensions={0} | all-to-all | bytes 524288 | tf_op jit(solution)/shard_map/all_to_all | solution.py:164
  83.2 1.9 %collective-permute-start.5 = (bf16[8,64,256]{2,1,0:T(8,128)(2,1)S(1)}, bf16[8,64,256]{2,1,0:T(8,128)(2,1)S(1)}, u32[]{:S(2)}, u32[]{:S(2)}) collective-permute-start(bf16[8,64,256]{2,1,0:T(8,128)(2,1)S(1)} %all_to_all.21.block_ref), channel_id=1, source_target_pairs={{496,0},{504,8},{0,16},{8,24},{16,32},{24,40},{32,48},{40,56},{48,... | collective-permute-start | bytes 786440 | tf_op jit(solution)/shard_map/ppermute | solution.py:159
  85.1 7.3 %collective-permute-start.6 = (bf16[8,64,256]{2,1,0:T(8,128)(2,1)S(1)}, bf16[8,64,256]{2,1,0:T(8,128)(2,1)S(1)}, u32[]{:S(2)}, u32[]{:S(2)}) collective-permute-start(bf16[8,64,256]{2,1,0:T(8,128)(2,1)S(1)} %all_to_all.21.block_ref), channel_id=1, source_target_pairs={{16,0},{24,8},{32,16},{40,24},{48,32},{56,40},{64,48},{72,56},{80,... | collective-permute-start | bytes 786440 | tf_op jit(solution)/shard_map/ppermute | solution.py:159
  92.4 1.9 %collective-permute-start.7 = (bf16[8,64,256]{2,1,0:T(8,128)(2,1)S(1)}, bf16[8,64,256]{2,1,0:T(8,128)(2,1)S(1)}, u32[]{:S(2)}, u32[]{:S(2)}) collective-permute-start(bf16[8,64,256]{2,1,0:T(8,128)(2,1)S(1)} %all_to_all.21.block_ref), channel_id=1, source_target_pairs={{0,480},{8,40},{16,496},{24,56},{32,0},{40,72},{48,16},{56,88},{64... | collective-permute-start | bytes 786440 | tf_op jit(solution)/shard_map/ppermute | solution.py:169
  95.1 0.8 shard_map.65.before_ref
  95.8 0.8 shard_map.66.before_ref.own_ref
  96.6 7.9 %collective-permute-done.7.block_ref = bf16[8,64,256]{2,1,0:T(8,128)(2,1)S(1)} collective-permute-done((bf16[8,64,256]{2,1,0:T(8,128)(2,1)S(1)}, bf16[8,64,256]{2,1,0:T(8,128)(2,1)S(1)}, u32[]{:S(2)}, u32[]{:S(2)}) %collective-permute-start.7) | collective-permute-done | bytes 262176 | tf_op jit(solution)/shard_map/ppermute | solution.py:169
  104.9 4.0 %collective-permute-start.8 = (f32[64,256]{1,0:T(8,128)S(1)}, f32[64,256]{1,0:T(8,128)S(1)}, u32[]{:S(2)}, u32[]{:S(2)}) collective-permute-start(f32[64,256]{1,0:T(8,128)S(1)} %shard_map.67), channel_id=1, source_target_pairs={{0,8},{8,0},{1,9},{9,1},{2,10},{10,2},{3,11},{11,3},{4,12},{12,4},... | collective-permute-start | bytes 196616 | tf_op jit(solution)/shard_map/ppermute | solution.py:220
  110.1 14.2 %all_to_all.22 = f32[32,8,128]{2,1,0:T(8,128)S(1)} all-to-all(f32[32,8,128]{2,1,0:T(8,128)S(1)} %broadcast_in_dim.13), channel_id=1, replica_groups=mesh['y_lo'=4,'z'=8,'core'=2,'x'=4,'y_hi'=2] {'x','y_hi','y_lo'}, dimensions={0} | all-to-all | bytes 262144 | tf_op jit(solution)/shard_map/all_to_all | solution.py:164
  124.3 14.4 %all_to_all.23 = f32[16,8,128]{2,1,0:T(8,128)S(1)} all-to-all(f32[16,8,128]{2,1,0:T(8,128)S(1)} %broadcast_in_dim.14), channel_id=1, replica_groups=mesh['y_lo'=4,'z'=8,'core'=2,'x'=4,'y_hi'=2] {'z','core'}, dimensions={0} | all-to-all | bytes 131072 | tf_op jit(solution)/shard_map/all_to_all | solution.py:164
  (29 shorter events, 4.1 us)
Async XLA Ops:
  2.4 64.2 %copy-start = (f32[64,256]{1,0:T(8,128)S(1)}, f32[64,256]{1,0:T(8,128)}, u32[]{:S(2)}) copy-start(f32[64,256]{1,0:T(8,128)} %first_ref.3) | copy-start | bytes 196612
  2.4 64.1 %copy-start.1 = (f32[256]{0:T(256)S(1)}, f32[256]{0:T(256)}, u32[]{:S(2)}) copy-start(f32[256]{0:T(256)} %param.6) | copy-start | bytes 3076
  27.4 23.0 %collective-permute-start.1 = (bf16[8,128,256]{2,1,0:T(8,128)(2,1)S(1)}, bf16[8,128,256]{2,1,0:T(8,128)(2,1)S(1)}, u32[]{:S(2)}, u32[]{:S(2)}) collective-permute-start(bf16[8,128,256]{2,1,0:T(8,128)(2,1)S(1)} %all_to_all.20.block_ref), channel_id=1, source_target_pairs={{496,0},{504,8},{0,16},{8,24},{16,32},{24,40},{32,48},{40,56},{48,... | collective-permute-start | bytes 1572872 | tf_op jit(solution)/shard_map/ppermute | solution.py:159
  31.4 22.1 %collective-permute-start.2 = (bf16[8,128,256]{2,1,0:T(8,128)(2,1)S(1)}, bf16[8,128,256]{2,1,0:T(8,128)(2,1)S(1)}, u32[]{:S(2)}, u32[]{:S(2)}) collective-permute-start(bf16[8,128,256]{2,1,0:T(8,128)(2,1)S(1)} %all_to_all.20.block_ref), channel_id=1, source_target_pairs={{16,0},{24,8},{32,16},{40,24},{48,32},{56,40},{64,48},{72,56},{80,... | collective-permute-start | bytes 1572872 | tf_op jit(solution)/shard_map/ppermute | solution.py:159
  38.6 20.0 %collective-permute-start.3 = (bf16[8,128,256]{2,1,0:T(8,128)(2,1)S(1)}, bf16[8,128,256]{2,1,0:T(8,128)(2,1)S(1)}, u32[]{:S(2)}, u32[]{:S(2)}) collective-permute-start(bf16[8,128,256]{2,1,0:T(8,128)(2,1)S(1)} %all_to_all.20.block_ref), channel_id=1, source_target_pairs={{0,480},{8,40},{16,496},{24,56},{32,0},{40,72},{48,16},{56,88},{64... | collective-permute-start | bytes 1572872 | tf_op jit(solution)/shard_map/ppermute | solution.py:169
  40.5 7.1 %collective-permute-start = (bf16[64,256]{1,0:T(8,128)(2,1)S(1)}, bf16[64,256]{1,0:T(8,128)(2,1)S(1)}, u32[]{:S(2)}, u32[]{:S(2)}) collective-permute-start(bf16[64,256]{1,0:T(8,128)(2,1)S(1)} %pad_maximum_fusion.1), channel_id=1, source_target_pairs={{0,8},{8,0},{1,9},{9,1},{2,10},{10,2},{3,11},{11,3},{4,12},{12,4},... | collective-permute-start | bytes 98312 | tf_op jit(solution)/shard_map/ppermute | solution.py:187
  59.7 6.9 %collective-permute-start.4 = (f32[64,256]{1,0:T(8,128)S(1)}, f32[64,256]{1,0:T(8,128)S(1)}, u32[]{:S(2)}, u32[]{:S(2)}) collective-permute-start(f32[64,256]{1,0:T(8,128)S(1)} %get-tuple-element.17), channel_id=1, source_target_pairs={{0,8},{8,0},{1,9},{9,1},{2,10},{10,2},{3,11},{11,3},{4,12},{12,4},... | collective-permute-start | bytes 196616 | tf_op jit(solution)/shard_map/ppermute | solution.py:211
  83.2 11.9 %collective-permute-start.5 = (bf16[8,64,256]{2,1,0:T(8,128)(2,1)S(1)}, bf16[8,64,256]{2,1,0:T(8,128)(2,1)S(1)}, u32[]{:S(2)}, u32[]{:S(2)}) collective-permute-start(bf16[8,64,256]{2,1,0:T(8,128)(2,1)S(1)} %all_to_all.21.block_ref), channel_id=1, source_target_pairs={{496,0},{504,8},{0,16},{8,24},{16,32},{24,40},{32,48},{40,56},{48,... | collective-permute-start | bytes 786440 | tf_op jit(solution)/shard_map/ppermute | solution.py:159
  85.1 10.7 %collective-permute-start.6 = (bf16[8,64,256]{2,1,0:T(8,128)(2,1)S(1)}, bf16[8,64,256]{2,1,0:T(8,128)(2,1)S(1)}, u32[]{:S(2)}, u32[]{:S(2)}) collective-permute-start(bf16[8,64,256]{2,1,0:T(8,128)(2,1)S(1)} %all_to_all.21.block_ref), channel_id=1, source_target_pairs={{16,0},{24,8},{32,16},{40,24},{48,32},{56,40},{64,48},{72,56},{80,... | collective-permute-start | bytes 786440 | tf_op jit(solution)/shard_map/ppermute | solution.py:159
  92.4 12.1 %collective-permute-start.7 = (bf16[8,64,256]{2,1,0:T(8,128)(2,1)S(1)}, bf16[8,64,256]{2,1,0:T(8,128)(2,1)S(1)}, u32[]{:S(2)}, u32[]{:S(2)}) collective-permute-start(bf16[8,64,256]{2,1,0:T(8,128)(2,1)S(1)} %all_to_all.21.block_ref), channel_id=1, source_target_pairs={{0,480},{8,40},{16,496},{24,56},{32,0},{40,72},{48,16},{56,88},{64... | collective-permute-start | bytes 786440 | tf_op jit(solution)/shard_map/ppermute | solution.py:169
  104.9 4.9 %collective-permute-start.8 = (f32[64,256]{1,0:T(8,128)S(1)}, f32[64,256]{1,0:T(8,128)S(1)}, u32[]{:S(2)}, u32[]{:S(2)}) collective-permute-start(f32[64,256]{1,0:T(8,128)S(1)} %shard_map.67), channel_id=1, source_target_pairs={{0,8},{8,0},{1,9},{9,1},{2,10},{10,2},{3,11},{11,3},{4,12},{12,4},... | collective-permute-start | bytes 196616 | tf_op jit(solution)/shard_map/ppermute | solution.py:220

commit v4 on v3

--- a/solution.py
+++ b/solution.py
@@ -116,20 +116,18 @@
     total_ref[...] = add_block(before_ref[:, WIDTH:], kernel_ref, block_ref)
 
 
-def row_sums(sums_ref, at, products):
+def row_sum(product):
     ones = jnp.ones((8, WIDTH), F32)
-    row = lax.broadcasted_iota(jnp.int32, (8, RHS), 0)
-    out = jnp.zeros((8, RHS), F32)
-    for i, product in enumerate(products):
-        total = lax.dot_general(ones, product, NT, precision=lax.Precision.HIGHEST, preferred_element_type=F32)
-        out = jnp.where(row == at + i, total, out)
-    sums_ref[:, :RHS] = out
-    sums_ref[:, RHS:] = jnp.zeros_like(out)
+    total = lax.dot_general(ones, product, NT, precision=lax.Precision.HIGHEST, preferred_element_type=F32)
+    return total[:1]
 
 
 def early_sums(first_ref, image_ref, sums_ref):
     first, image = first_ref[...], image_ref[...]
-    row_sums(sums_ref, 0, (first * first, first * image, image * image))
+    sums_ref[0:1, :RHS] = row_sum(first * first)
+    sums_ref[0:1, RHS:] = row_sum(first * image)
+    sums_ref[1:2, :RHS] = row_sum(image * image)
+    sums_ref[1:2, RHS:] = jnp.zeros((1, RHS), F32)
 
 
 def late_sums(early_ref, noise_ref, first_ref, first_total_ref, image_ref, own_ref, peer_ref, second_ref, sums_ref):
@@ -137,8 +135,10 @@
     total = own_ref[:, :WIDTH] + peer_ref[...]
     second = noise_ref[...] * image + (first_total_ref[...] - total) * (1.0 / SIGMA)
     second_ref[...] = second
-    row_sums(sums_ref, 3, (first * second, image * second))
-    sums_ref[...] += early_ref[...]
+    sums_ref[0:2] = early_ref[...]
+    sums_ref[2:3, :RHS] = row_sum(first * second)
+    sums_ref[2:3, RHS:] = row_sum(image * second)
+    sums_ref[3:4] = jnp.zeros((1, 2 * RHS), F32)
 
 
 VMEM_LIMIT = pltpu.CompilerParams(vmem_limit_bytes=48 * 1024 * 1024)
@@ -154,19 +154,16 @@
     return jax.ShapeDtypeStruct(dims, dtype)
 
 
-def shifted(value, distance):
-    route = [((i - distance) % N_BLK, i) for i in range(N_BLK)]
-    return lax.ppermute(value, BLK, route)
-
-
 def gathered(value, axes):
     count = math.prod(SIZES[AXES.index(axis)] for axis in axes)
     return lax.all_to_all(jnp.broadcast_to(value[None], (count,) + value.shape), axes, 0, 0)
 
 
 def halo(block):
+    first = [(i, i + 2 if i // 2 % 2 == 0 else i - 2) for i in range(N_BLK)]
+    second = [(i, (i - 2 if i // 2 % 2 == 0 else i + 2) % N_BLK) for i in range(N_BLK)]
     fourth = [(i, (i - 4 if i % 2 == 0 else i + 4) % N_BLK) for i in range(N_BLK)]
-    return lax.ppermute(block, BLK, fourth), shifted(block, 2), shifted(block, -2)
+    return tuple(lax.ppermute(block, BLK, route) for route in (first, second, fourth))
 
 
 def kernel_shape(rows=2 * WIDTH):
@@ -185,17 +182,17 @@
     message = jnp.concatenate(split(coords) + (targets.astype(BF16),), axis=0)
     block = gathered(message, ("x", "y_hi"))
     peer = lax.ppermute(message[: 2 * FEAT], "core", SWAP)
-    far, up, down = halo(block)
-
-    odd = lax.axis_index("core") == 1
-    near_far = jnp.where(odd, LEVELS[1], LEVELS[3]), jnp.where(odd, LEVELS[3], LEVELS[1])
+    *pairs, far = halo(block)
+
+    near = lax.axis_index("z") % 2 == lax.axis_index("core")
+    near_far = jnp.where(near, LEVELS[1], LEVELS[3]), jnp.where(near, LEVELS[3], LEVELS[1])
     weights, total, kernel_own = call(
         build_first,
         (shape(2 * WIDTH, DEPTH, dtype=BF16), shape(RHS, 2 * WIDTH), kernel_shape()),
         scratch_shapes=scratch(),
     )(message, peer, block)
     kernels = []
-    for moved, level in zip((up, down), near_far):
+    for moved, level in zip(pairs, near_far):
         total, made = call(
             build_more,
             (shape(RHS, 2 * WIDTH), kernel_shape()),
@@ -211,20 +208,20 @@
     first_total = total[:, :WIDTH] + lax.ppermute(peer_total, "core", SWAP)
     image = noise * targets + first_total
     block = gathered((targets - SIGMA * image).astype(BF16), ("x", "y_hi"))
-    far, up, down = halo(block)
-    early = call(early_sums, shape(8, 2 * RHS))(targets, image)
+    *pairs, far = halo(block)
+    early = call(early_sums, shape(2, 2 * RHS))(targets, image)
     total = call(apply_first, shape(RHS, 2 * WIDTH))(kernel_own, block)
-    for made, moved in zip(kernels, (up, down)):
+    for made, moved in zip(kernels, pairs):
         total = call(apply_more, shape(RHS, 2 * WIDTH))(made, total, moved)
     peer_total = call(apply_far, shape(RHS, WIDTH))(kernel_far, total, far)
     peer_total = lax.ppermute(peer_total, "core", SWAP)
-    second, sums = call(late_sums, (shape(RHS, WIDTH), shape(8, 2 * RHS)))(
+    second, sums = call(late_sums, (shape(RHS, WIDTH), shape(4, 2 * RHS)))(
         early, noise, targets, first_total, image, total, peer_total
     )
     for axes in (("x", "y_hi", "y_lo"), ("z", "core")):
         sums = jnp.sum(gathered(sums, axes), axis=0)
 
-    rr, rq, qq, rs, qs = (sums[i, :RHS] for i in range(5))
+    (rr, rq), (qq, _), (rs, qs) = ((sums[i, :RHS], sums[i, RHS:]) for i in range(3))
     step = rr / rq
     norm_next = jnp.maximum(rr - 2.0 * step * rq + step * step * qq, 0.0)
     grown = 1.0 + norm_next / rr

time: 140 us -> 139 us (level)
  starting transfers between devices: 40.5 us -> 37.3 us
  waiting for transfers between devices: 12.1 us -> 14.7 us
    ppermute x6, waiting for transfers between devices: 9.89 us -> 12.3 us  [halo(): lax.ppermute(block, BLK, route)]
    ppermute x1, starting transfers between devices: 3.98 us -> 1.92 us  [body(): peer_total = lax.ppermute(peer_total, 'core', SWAP)]
  transfers between devices with their start and end apart: 9 -> 9, of which waited for: 5 -> 6; matrix products, arithmetic and copies ran while one was open for 0% -> 0% of each run, Pallas kernels for 8% -> 8%
where the time goes in v4:
time: 139 us
  blocking collectives  69.6 us (50%)
  starting transfers between devices  37.3 us (27%)
  waiting for transfers between devices  14.7 us (11%)
  Pallas kernels  13.2 us (9%)
  other arithmetic  2.86 us (2%)
    all_to_all x4, blocking collectives, gathered(): lax.all_to_all(jnp.broadcast_to(value[None], (count,) + value.shape), axe...  69.6 us
    ppermute x6, starting transfers between devices, halo(): lax.ppermute(block, BLK, route)  23.7 us
    ppermute x6, waiting for transfers between devices, halo(): lax.ppermute(block, BLK, route)  12.3 us
    pallas_call x2, Pallas kernels, body(): call(build_more, (shape(RHS, 2 * WIDTH), kernel_shape()), in_specs=[SMEM]...  6.14 us
    ppermute x1, starting transfers between devices, body(): first_total = total[:, :WIDTH] + lax.ppermute(peer_total, 'core', SWAP)  6.14 us
    ppermute x1, starting transfers between devices, body(): peer = lax.ppermute(message[:2 * FEAT], 'core', SWAP)  5.49 us
  transfers between devices with their start and end apart: 9, of which 6 were waited for; matrix products, arithmetic and copies ran while one was open for 0% of the time, Pallas kernels for 8%

profile of v4, /device:TPU:1, one launch (start us, length us, event | category | flops | bytes accessed | tf_op | source)
XLA Modules:
  0.0 138.7 jit_solution(252017757692914961)
XLA Ops:
  0.6 0.8 convert_element_type.14
  1.5 0.8 reduce-precision_convert_fusion
  2.4 25.0 %all_to_all.20.block_ref = bf16[8,128,256]{2,1,0:T(8,128)(2,1)S(1)} all-to-all(bf16[8,128,256]{2,1,0:T(8,128)(2,1)S(1)} %broadcast_in_dim.10), channel_id=1, replica_groups=mesh['y_lo'=4,'z'=8,'core'=2,'x'=4,'y_hi'=2] {'x','y_hi'}, dimensions={0} | all-to-all | bytes 1048576 | tf_op jit(solution)/shard_map/all_to_all | solution.py:159
  27.4 4.0 %collective-permute-start.1 = (bf16[8,128,256]{2,1,0:T(8,128)(2,1)S(1)}, bf16[8,128,256]{2,1,0:T(8,128)(2,1)S(1)}, u32[]{:S(2)}, u32[]{:S(2)}) collective-permute-start(bf16[8,128,256]{2,1,0:T(8,128)(2,1)S(1)} %all_to_all.20.block_ref), channel_id=1, source_target_pairs={{0,16},{8,24},{16,0},{24,8},{32,48},{40,56},{48,32},{56,40},{64,80... | collective-permute-start | bytes 1572872 | tf_op jit(solution)/shard_map/ppermute | solution.py:166
  31.4 7.5 %collective-permute-start.2 = (bf16[8,128,256]{2,1,0:T(8,128)(2,1)S(1)}, bf16[8,128,256]{2,1,0:T(8,128)(2,1)S(1)}, u32[]{:S(2)}, u32[]{:S(2)}) collective-permute-start(bf16[8,128,256]{2,1,0:T(8,128)(2,1)S(1)} %all_to_all.20.block_ref), channel_id=1, source_target_pairs={{0,496},{8,504},{16,32},{24,40},{32,16},{40,24},{48,64},{56,72},{6... | collective-permute-start | bytes 1572872 | tf_op jit(solution)/shard_map/ppermute | solution.py:166
  38.8 1.9 %collective-permute-start.3 = (bf16[8,128,256]{2,1,0:T(8,128)(2,1)S(1)}, bf16[8,128,256]{2,1,0:T(8,128)(2,1)S(1)}, u32[]{:S(2)}, u32[]{:S(2)}) collective-permute-start(bf16[8,128,256]{2,1,0:T(8,128)(2,1)S(1)} %all_to_all.20.block_ref), channel_id=1, source_target_pairs={{0,480},{8,40},{16,496},{24,56},{32,0},{40,72},{48,16},{56,88},{64... | collective-permute-start | bytes 1572872 | tf_op jit(solution)/shard_map/ppermute | solution.py:166
  40.8 5.5 %collective-permute-start = (bf16[64,256]{1,0:T(8,128)(2,1)S(1)}, bf16[64,256]{1,0:T(8,128)(2,1)S(1)}, u32[]{:S(2)}, u32[]{:S(2)}) collective-permute-start(bf16[64,256]{1,0:T(8,128)(2,1)S(1)} %pad_maximum_fusion.1), channel_id=1, source_target_pairs={{0,8},{8,0},{1,9},{9,1},{2,10},{10,2},{3,11},{11,3},{4,12},{12,4},... | collective-permute-start | bytes 98312 | tf_op jit(solution)/shard_map/ppermute | solution.py:184
  47.1 2.7 %shard_map.59 = (bf16[512,144]{1,0:T(8,128)(2,1)S(1)}, f32[64,512]{1,0:T(8,128)S(1)}, bf16[8,512,256]{2,1,0:T(8,128)(2,1)S(1)}) custom-call(bf16[128,256]{1,0:T(8,128)(2,1)S(1)} %pad_maximum_fusion.own_ref, bf16[64,256]{1,0:T(8,128)(2,1)S(1)} %collective-permute-done.peer_ref, bf16[8,128,256]{2,1,0:T(8,128)(2,1)S(1)} %all_to_all.20.block_ref), custom_call_target="tpu_custom_call" | custom-call | tf_op jit(solution)/shard_map/pallas_call | solution.py:189
  49.8 3.1 %shard_map.60 = (f32[64,512]{1,0:T(8,128)S(1)}, bf16[8,512,256]{2,1,0:T(8,128)(2,1)S(1)}) custom-call(f32[2]{0:T(128)S(1)} %pad_maximum_fusion.2.level_ref, bf16[512,144]{1,0:T(8,128)(2,1)S(1)} %get-tuple-element.13.weights_ref, f32[64,512]{1,0:T(8,128)S(1)} %get-tuple-element.14.before_ref, bf16[8,128,256]{2,1,0:T(8,128)(2,1)S(1)} %collective-permute-done.1.block_ref), custom_call_target="tpu_custom_call" | custom-call | tf_op jit(solution)/shard_map/pallas_call | solution.py:196
  52.9 3.1 %shard_map.61 = (f32[64,512]{1,0:T(8,128)S(1)}, bf16[8,512,256]{2,1,0:T(8,128)(2,1)S(1)}) custom-call(f32[2]{0:T(128)S(1)} %pad_maximum_fusion.3.level_ref, bf16[512,144]{1,0:T(8,128)(2,1)S(1)} %get-tuple-element.13.weights_ref, f32[64,512]{1,0:T(8,128)S(1)} %get-tuple-element.15.before_ref, bf16[8,128,256]{2,1,0:T(8,128)(2,1)S(1)} %collective-permute-done.2.block_ref), custom_call_target="tpu_custom_call" | custom-call | tf_op jit(solution)/shard_map/pallas_call | solution.py:196
  56.0 2.8 %collective-permute-done.3.block_ref = bf16[8,128,256]{2,1,0:T(8,128)(2,1)S(1)} collective-permute-done((bf16[8,128,256]{2,1,0:T(8,128)(2,1)S(1)}, bf16[8,128,256]{2,1,0:T(8,128)(2,1)S(1)}, u32[]{:S(2)}, u32[]{:S(2)}) %collective-permute-start.3) | collective-permute-done | bytes 524320 | tf_op jit(solution)/shard_map/ppermute | solution.py:166
  58.8 1.1 shard_map.62
  59.9 6.1 %collective-permute-start.4 = (f32[64,256]{1,0:T(8,128)S(1)}, f32[64,256]{1,0:T(8,128)S(1)}, u32[]{:S(2)}, u32[]{:S(2)}) collective-permute-start(f32[64,256]{1,0:T(8,128)S(1)} %get-tuple-element.17), channel_id=1, source_target_pairs={{0,8},{8,0},{1,9},{9,1},{2,10},{10,2},{3,11},{11,3},{4,12},{12,4},... | collective-permute-start | bytes 196616 | tf_op jit(solution)/shard_map/ppermute | solution.py:208
  66.1 0.9 collective-permute-done.4
  67.0 14.6 %all_to_all.21.block_ref = bf16[8,64,256]{2,1,0:T(8,128)(2,1)S(1)} all-to-all(bf16[8,64,256]{2,1,0:T(8,128)(2,1)S(1)} %broadcast_in_dim.12), channel_id=1, replica_groups=mesh['y_lo'=4,'z'=8,'core'=2,'x'=4,'y_hi'=2] {'x','y_hi'}, dimensions={0} | all-to-all | bytes 524288 | tf_op jit(solution)/shard_map/all_to_all | solution.py:159
  81.6 1.9 %collective-permute-start.5 = (bf16[8,64,256]{2,1,0:T(8,128)(2,1)S(1)}, bf16[8,64,256]{2,1,0:T(8,128)(2,1)S(1)}, u32[]{:S(2)}, u32[]{:S(2)}) collective-permute-start(bf16[8,64,256]{2,1,0:T(8,128)(2,1)S(1)} %all_to_all.21.block_ref), channel_id=1, source_target_pairs={{0,16},{8,24},{16,0},{24,8},{32,48},{40,56},{48,32},{56,40},{64,80... | collective-permute-start | bytes 786440 | tf_op jit(solution)/shard_map/ppermute | solution.py:166
  83.5 6.5 %collective-permute-start.6 = (bf16[8,64,256]{2,1,0:T(8,128)(2,1)S(1)}, bf16[8,64,256]{2,1,0:T(8,128)(2,1)S(1)}, u32[]{:S(2)}, u32[]{:S(2)}) collective-permute-start(bf16[8,64,256]{2,1,0:T(8,128)(2,1)S(1)} %all_to_all.21.block_ref), channel_id=1, source_target_pairs={{0,496},{8,504},{16,32},{24,40},{32,16},{40,24},{48,64},{56,72},{6... | collective-permute-start | bytes 786440 | tf_op jit(solution)/shard_map/ppermute | solution.py:166
  90.0 1.9 %collective-permute-start.7 = (bf16[8,64,256]{2,1,0:T(8,128)(2,1)S(1)}, bf16[8,64,256]{2,1,0:T(8,128)(2,1)S(1)}, u32[]{:S(2)}, u32[]{:S(2)}) collective-permute-start(bf16[8,64,256]{2,1,0:T(8,128)(2,1)S(1)} %all_to_all.21.block_ref), channel_id=1, source_target_pairs={{0,480},{8,40},{16,496},{24,56},{32,0},{40,72},{48,16},{56,88},{64... | collective-permute-start | bytes 786440 | tf_op jit(solution)/shard_map/ppermute | solution.py:166
  93.5 1.8 %collective-permute-done.6.block_ref = bf16[8,64,256]{2,1,0:T(8,128)(2,1)S(1)} collective-permute-done((bf16[8,64,256]{2,1,0:T(8,128)(2,1)S(1)}, bf16[8,64,256]{2,1,0:T(8,128)(2,1)S(1)}, u32[]{:S(2)}, u32[]{:S(2)}) %collective-permute-start.6) | collective-permute-done | bytes 262176 | tf_op jit(solution)/shard_map/ppermute | solution.py:166
  96.1 7.7 %collective-permute-done.7.block_ref = bf16[8,64,256]{2,1,0:T(8,128)(2,1)S(1)} collective-permute-done((bf16[8,64,256]{2,1,0:T(8,128)(2,1)S(1)}, bf16[8,64,256]{2,1,0:T(8,128)(2,1)S(1)}, u32[]{:S(2)}, u32[]{:S(2)}) %collective-permute-start.7) | collective-permute-done | bytes 262176 | tf_op jit(solution)/shard_map/ppermute | solution.py:166
  104.2 1.9 %collective-permute-start.8 = (f32[64,256]{1,0:T(8,128)S(1)}, f32[64,256]{1,0:T(8,128)S(1)}, u32[]{:S(2)}, u32[]{:S(2)}) collective-permute-start(f32[64,256]{1,0:T(8,128)S(1)} %shard_map.67), channel_id=1, source_target_pairs={{0,8},{8,0},{1,9},{9,1},{2,10},{10,2},{3,11},{11,3},{4,12},{12,4},... | collective-permute-start | bytes 196616 | tf_op jit(solution)/shard_map/ppermute | solution.py:217
  106.4 0.9 collective-permute-done.8.peer_ref
  107.6 15.6 %all_to_all.22 = f32[32,4,128]{2,1,0:T(4,128)S(1)} all-to-all(f32[32,4,128]{2,1,0:T(4,128)S(1)} %broadcast_in_dim.13), channel_id=1, replica_groups=mesh['y_lo'=4,'z'=8,'core'=2,'x'=4,'y_hi'=2] {'x','y_hi','y_lo'}, dimensions={0} | all-to-all | bytes 131072 | tf_op jit(solution)/shard_map/all_to_all | solution.py:159
  123.3 14.4 %all_to_all.23 = f32[16,4,128]{2,1,0:T(4,128)S(1)} all-to-all(f32[16,4,128]{2,1,0:T(4,128)S(1)} %broadcast_in_dim.14), channel_id=1, replica_groups=mesh['y_lo'=4,'z'=8,'core'=2,'x'=4,'y_hi'=2] {'z','core'}, dimensions={0} | all-to-all | bytes 65536 | tf_op jit(solution)/shard_map/all_to_all | solution.py:159
  (29 shorter events, 5.2 us)
Async XLA Ops:
  2.4 64.6 %copy-start = (f32[64,256]{1,0:T(8,128)S(1)}, f32[64,256]{1,0:T(8,128)}, u32[]{:S(2)}) copy-start(f32[64,256]{1,0:T(8,128)} %first_ref.3) | copy-start | bytes 196612
  2.4 64.6 %copy-start.1 = (f32[256]{0:T(256)S(1)}, f32[256]{0:T(256)}, u32[]{:S(2)}) copy-start(f32[256]{0:T(256)} %param.6) | copy-start | bytes 3076
  27.4 22.5 %collective-permute-start.1 = (bf16[8,128,256]{2,1,0:T(8,128)(2,1)S(1)}, bf16[8,128,256]{2,1,0:T(8,128)(2,1)S(1)}, u32[]{:S(2)}, u32[]{:S(2)}) collective-permute-start(bf16[8,128,256]{2,1,0:T(8,128)(2,1)S(1)} %all_to_all.20.block_ref), channel_id=1, source_target_pairs={{0,16},{8,24},{16,0},{24,8},{32,48},{40,56},{48,32},{56,40},{64,80... | collective-permute-start | bytes 1572872 | tf_op jit(solution)/shard_map/ppermute | solution.py:166
  31.4 21.6 %collective-permute-start.2 = (bf16[8,128,256]{2,1,0:T(8,128)(2,1)S(1)}, bf16[8,128,256]{2,1,0:T(8,128)(2,1)S(1)}, u32[]{:S(2)}, u32[]{:S(2)}) collective-permute-start(bf16[8,128,256]{2,1,0:T(8,128)(2,1)S(1)} %all_to_all.20.block_ref), channel_id=1, source_target_pairs={{0,496},{8,504},{16,32},{24,40},{32,16},{40,24},{48,64},{56,72},{6... | collective-permute-start | bytes 1572872 | tf_op jit(solution)/shard_map/ppermute | solution.py:166
  38.8 20.0 %collective-permute-start.3 = (bf16[8,128,256]{2,1,0:T(8,128)(2,1)S(1)}, bf16[8,128,256]{2,1,0:T(8,128)(2,1)S(1)}, u32[]{:S(2)}, u32[]{:S(2)}) collective-permute-start(bf16[8,128,256]{2,1,0:T(8,128)(2,1)S(1)} %all_to_all.20.block_ref), channel_id=1, source_target_pairs={{0,480},{8,40},{16,496},{24,56},{32,0},{40,72},{48,16},{56,88},{64... | collective-permute-start | bytes 1572872 | tf_op jit(solution)/shard_map/ppermute | solution.py:166
  40.8 6.3 %collective-permute-start = (bf16[64,256]{1,0:T(8,128)(2,1)S(1)}, bf16[64,256]{1,0:T(8,128)(2,1)S(1)}, u32[]{:S(2)}, u32[]{:S(2)}) collective-permute-start(bf16[64,256]{1,0:T(8,128)(2,1)S(1)} %pad_maximum_fusion.1), channel_id=1, source_target_pairs={{0,8},{8,0},{1,9},{9,1},{2,10},{10,2},{3,11},{11,3},{4,12},{12,4},... | collective-permute-start | bytes 98312 | tf_op jit(solution)/shard_map/ppermute | solution.py:184
  59.9 7.0 %collective-permute-start.4 = (f32[64,256]{1,0:T(8,128)S(1)}, f32[64,256]{1,0:T(8,128)S(1)}, u32[]{:S(2)}, u32[]{:S(2)}) collective-permute-start(f32[64,256]{1,0:T(8,128)S(1)} %get-tuple-element.17), channel_id=1, source_target_pairs={{0,8},{8,0},{1,9},{9,1},{2,10},{10,2},{3,11},{11,3},{4,12},{12,4},... | collective-permute-start | bytes 196616 | tf_op jit(solution)/shard_map/ppermute | solution.py:208
  81.6 11.1 %collective-permute-start.5 = (bf16[8,64,256]{2,1,0:T(8,128)(2,1)S(1)}, bf16[8,64,256]{2,1,0:T(8,128)(2,1)S(1)}, u32[]{:S(2)}, u32[]{:S(2)}) collective-permute-start(bf16[8,64,256]{2,1,0:T(8,128)(2,1)S(1)} %all_to_all.21.block_ref), channel_id=1, source_target_pairs={{0,16},{8,24},{16,0},{24,8},{32,48},{40,56},{48,32},{56,40},{64,80... | collective-permute-start | bytes 786440 | tf_op jit(solution)/shard_map/ppermute | solution.py:166
  83.5 11.8 %collective-permute-start.6 = (bf16[8,64,256]{2,1,0:T(8,128)(2,1)S(1)}, bf16[8,64,256]{2,1,0:T(8,128)(2,1)S(1)}, u32[]{:S(2)}, u32[]{:S(2)}) collective-permute-start(bf16[8,64,256]{2,1,0:T(8,128)(2,1)S(1)} %all_to_all.21.block_ref), channel_id=1, source_target_pairs={{0,496},{8,504},{16,32},{24,40},{32,16},{40,24},{48,64},{56,72},{6... | collective-permute-start | bytes 786440 | tf_op jit(solution)/shard_map/ppermute | solution.py:166
  90.0 13.7 %collective-permute-start.7 = (bf16[8,64,256]{2,1,0:T(8,128)(2,1)S(1)}, bf16[8,64,256]{2,1,0:T(8,128)(2,1)S(1)}, u32[]{:S(2)}, u32[]{:S(2)}) collective-permute-start(bf16[8,64,256]{2,1,0:T(8,128)(2,1)S(1)} %all_to_all.21.block_ref), channel_id=1, source_target_pairs={{0,480},{8,40},{16,496},{24,56},{32,0},{40,72},{48,16},{56,88},{64... | collective-permute-start | bytes 786440 | tf_op jit(solution)/shard_map/ppermute | solution.py:166
  104.2 3.1 %collective-permute-start.8 = (f32[64,256]{1,0:T(8,128)S(1)}, f32[64,256]{1,0:T(8,128)S(1)}, u32[]{:S(2)}, u32[]{:S(2)}) collective-permute-start(f32[64,256]{1,0:T(8,128)S(1)} %shard_map.67), channel_id=1, source_target_pairs={{0,8},{8,0},{1,9},{9,1},{2,10},{10,2},{3,11},{11,3},{4,12},{12,4},... | collective-permute-start | bytes 196616 | tf_op jit(solution)/shard_map/ppermute | solution.py:217

commit v5 on v4

--- a/solution.py
+++ b/solution.py
@@ -12,7 +12,6 @@
 SIZES = (4, 8, 2, 4, 2)
 BLK = ("y_lo", "z", "core")
 N_BLK = 64
-SWAP = ((0, 1), (1, 0))
 
 LN2 = math.log(2.0)
 UNIT = math.sqrt(5.0) / LN2
@@ -25,15 +24,26 @@
 FEAT = 32
 RHS = 64
 WIDTH = 256
+ROUGH = 80
 DEPTH = 144
+TOLD = 96
 SHARDS = 8
 SIGMA = 0.5
 NT = (((1,), (1,)), ((), ()))
 
 
-def split(value):
-    high = lax.reduce_precision(value, 8, 7)
-    return high.astype(BF16), (value - high).astype(BF16)
+def prepare(points_ref, scale_ref, targets_ref, message_ref):
+    row = lax.broadcasted_iota(jnp.int32, (FEAT, FEAT), 0)
+    column = lax.broadcasted_iota(jnp.int32, (FEAT, FEAT), 1)
+    scale = jnp.sum(jnp.where(row == column, scale_ref[...], 0.0), axis=1, keepdims=True)
+    coords = points_ref[...] / scale * UNIT
+    high = coords.astype(BF16)
+    low = (coords - high.astype(F32)).astype(BF16)
+    targets = targets_ref[...].astype(BF16)
+    for i in range(SHARDS):
+        message_ref[i, :FEAT] = high
+        message_ref[i, FEAT:TOLD] = targets
+        message_ref[i, TOLD:] = low
 
 
 def square_rows(coords, first, second):
@@ -49,12 +59,19 @@
 
 
 def build_shard(weights, levels, shard, cols_ref, dist_ref, kernel_ref):
-    coords = shard[: 2 * FEAT]
-    wide = coords.astype(F32)
-    cols_ref[: 2 * FEAT] = coords
-    cols_ref[2 * FEAT : 4 * FEAT] = coords
-    cols_ref[4 * FEAT :] = square_rows(wide[:FEAT] + wide[FEAT:], 0, 3)
-    dist_ref[...] = jnp.dot(weights, cols_ref[...], preferred_element_type=F32)
+    high = shard[:FEAT]
+    coords = high.astype(F32)
+    cols_ref[:FEAT] = high
+    cols_ref[FEAT : 2 * FEAT] = high
+    depth = ROUGH
+    if shard.shape[0] > TOLD:
+        low = shard[TOLD:]
+        coords = coords + low.astype(F32)
+        cols_ref[ROUGH : ROUGH + FEAT] = low
+        cols_ref[ROUGH + FEAT :] = low
+        depth = DEPTH
+    cols_ref[2 * FEAT : ROUGH] = square_rows(coords, 0, 3)
+    dist_ref[...] = jnp.dot(weights[:, :depth], cols_ref[:depth], preferred_element_type=F32)
     step = 64
     for half, level in enumerate(levels):
         for at in range(half * WIDTH, (half + 1) * WIDTH, step):
@@ -62,7 +79,7 @@
             moved = part * lax.rsqrt(part) + SHIFT
             entry = (moved * moved + OFFSET) * jnp.exp2(level - moved)
             kernel_ref[at : at + step] = entry.astype(BF16)
-    return lax.dot_general(shard[2 * FEAT :], kernel_ref[...], NT, preferred_element_type=F32)
+    return lax.dot_general(shard[FEAT:TOLD], kernel_ref[...], NT, preferred_element_type=F32)
 
 
 def build_block(weights, levels, block_ref, cols_ref, dist_ref, kernel_ref):
@@ -73,15 +90,15 @@
     return total
 
 
-def build_first(own_ref, peer_ref, block_ref, weights_ref, total_ref, kernel_ref, cols_ref, dist_ref):
-    for at, ref in enumerate((own_ref, peer_ref)):
+def build_first(core_ref, both_ref, block_ref, weights_ref, total_ref, kernel_ref, cols_ref, dist_ref):
+    for at, ref in enumerate((both_ref.at[core_ref[0]], both_ref.at[1 - core_ref[0]])):
         rows = slice(at * WIDTH, (at + 1) * WIDTH)
-        coords = ref[: 2 * FEAT].astype(F32)
-        high, low = coords[:FEAT], coords[FEAT:]
+        high, low = ref[:FEAT].astype(F32), ref[FEAT:].astype(F32)
         extra = square_rows(high + low, 3, 0).astype(F32)
-        stacked = jnp.concatenate([-2.0 * high, -2.0 * high, -2.0 * low, -2.0 * low], axis=0)
-        weights_ref[rows, : 4 * FEAT] = jnp.transpose(stacked).astype(BF16)
-        weights_ref[rows, 4 * FEAT :] = jnp.transpose(extra).astype(BF16)
+        halves = jnp.transpose(jnp.concatenate([-2.0 * high, -2.0 * low], axis=0)).astype(BF16)
+        weights_ref[rows, : 2 * FEAT] = halves
+        weights_ref[rows, 2 * FEAT : ROUGH] = jnp.transpose(extra).astype(BF16)
+        weights_ref[rows, ROUGH:] = halves
     total_ref[...] = build_block(weights_ref[...], LEVELS[:2], block_ref, cols_ref, dist_ref, kernel_ref)
 
 
@@ -130,9 +147,11 @@
     sums_ref[1:2, RHS:] = jnp.zeros((1, RHS), F32)
 
 
-def late_sums(early_ref, noise_ref, first_ref, first_total_ref, image_ref, own_ref, peer_ref, second_ref, sums_ref):
+def late_sums(
+    core_ref, early_ref, noise_ref, first_ref, first_total_ref, image_ref, own_ref, both_ref, second_ref, sums_ref
+):
     first, image = first_ref[...], image_ref[...]
-    total = own_ref[:, :WIDTH] + peer_ref[...]
+    total = own_ref[:, :WIDTH] + both_ref[1 - core_ref[0]]
     second = noise_ref[...] * image + (first_total_ref[...] - total) * (1.0 / SIGMA)
     second_ref[...] = second
     sums_ref[0:2] = early_ref[...]
@@ -178,19 +197,22 @@
 
 
 def body(points, lengthscale, noise_var, targets):
-    coords = points / lengthscale[:, None] * UNIT
-    message = jnp.concatenate(split(coords) + (targets.astype(BF16),), axis=0)
-    block = gathered(message, ("x", "y_hi"))
-    peer = lax.ppermute(message[: 2 * FEAT], "core", SWAP)
-    *pairs, far = halo(block)
-
-    near = lax.axis_index("z") % 2 == lax.axis_index("core")
+    core = lax.axis_index("core")
+    which = core.astype(jnp.int32).reshape(1)
+    message = call(prepare, shape(SHARDS, 2 * FEAT + RHS, WIDTH, dtype=BF16))(points, lengthscale[None, :], targets)
+    coords = jnp.concatenate([message[0, :FEAT], message[0, TOLD:]], axis=0)
+    both = lax.all_gather(coords, "core")
+    block = lax.all_to_all(message, ("x", "y_hi"), 0, 0)
+    *pairs, far = halo(block[:, :TOLD])
+
+    near = lax.axis_index("z") % 2 == core
     near_far = jnp.where(near, LEVELS[1], LEVELS[3]), jnp.where(near, LEVELS[3], LEVELS[1])
     weights, total, kernel_own = call(
         build_first,
         (shape(2 * WIDTH, DEPTH, dtype=BF16), shape(RHS, 2 * WIDTH), kernel_shape()),
+        in_specs=[SMEM] + [VMEM] * 2,
         scratch_shapes=scratch(),
-    )(message, peer, block)
+    )(which, both, block)
     kernels = []
     for moved, level in zip(pairs, near_far):
         total, made = call(
@@ -205,7 +227,8 @@
     )(weights, total, far)
 
     noise = noise_var[None, :]
-    first_total = total[:, :WIDTH] + lax.ppermute(peer_total, "core", SWAP)
+    both = lax.all_gather(peer_total, "core")
+    first_total = total[:, :WIDTH] + jnp.where(core == 0, both[1], both[0])
     image = noise * targets + first_total
     block = gathered((targets - SIGMA * image).astype(BF16), ("x", "y_hi"))
     *pairs, far = halo(block)
@@ -214,10 +237,10 @@
     for made, moved in zip(kernels, pairs):
         total = call(apply_more, shape(RHS, 2 * WIDTH))(made, total, moved)
     peer_total = call(apply_far, shape(RHS, WIDTH))(kernel_far, total, far)
-    peer_total = lax.ppermute(peer_total, "core", SWAP)
-    second, sums = call(late_sums, (shape(RHS, WIDTH), shape(4, 2 * RHS)))(
-        early, noise, targets, first_total, image, total, peer_total
-    )
+    both = lax.all_gather(peer_total, "core")
+    second, sums = call(
+        late_sums, (shape(RHS, WIDTH), shape(4, 2 * RHS)), in_specs=[SMEM] + [VMEM] * 7
+    )(which, early, noise, targets, first_total, image, total, both)
     for axes in (("x", "y_hi", "y_lo"), ("z", "core")):
         sums = jnp.sum(gathered(sums, axes), axis=0)
 

time: 139 us -> 132 us (0.950)
  starting transfers between devices: 37.3 us -> 24.7 us
  blocking collectives: 69.6 us -> 78.2 us
  waiting for transfers between devices: 14.7 us -> 10.6 us
  local copies, waits for them, and re-layouts: 0.1 us -> 2.34 us
  other arithmetic: 2.86 us -> 1.17 us
    all_to_all x4 -> x3, blocking collectives: 69.6 us -> 43 us  [gathered(): lax.all_to_all(jnp.broadcast_to(value[None], (count,) + value.shape), axe...]
    all_to_all x0 -> x1, blocking collectives: none -> 24.8 us  [body(): block = lax.all_to_all(message, ('x', 'y_hi'), 0, 0)]
    ppermute x3 -> x0, starting transfers between devices: 13.5 us -> none  [the longest x1 6.14 us: body(): first_total = total[:, :WIDTH] + lax.ppermute(peer_total, 'core', SWAP)]
    all_gather x0 -> x3, blocking collectives: none -> 10.4 us  [the longest x2 5.29 us: body(): both = lax.all_gather(peer_total, 'core')]
    ppermute x3 -> x0, waiting for transfers between devices: 2.46 us -> none  [the longest x1 0.91 us: body(): peer_total = lax.ppermute(peer_total, 'core', SWAP)]
    unnamed x4 -> x10, local copies, waits for them, and re-layouts: 0.01 us -> 2.25 us
    convert_element_type x2 -> x0, other arithmetic: 1.69 us -> none  [the longest x1 0.85 us: body(): message = jnp.concatenate(split(coords) + (targets.astype(BF16),), axis=0)]
    ppermute x6, waiting for transfers between devices: 12.3 us -> 10.6 us  [halo(): lax.ppermute(block, BLK, route)]
  transfers between devices with their start and end apart: 9 -> 6, of which waited for: 6 -> 3; matrix products, arithmetic and copies ran while one was open for 0% -> 0% of each run, Pallas kernels for 8% -> 9%
where the time goes in v5:
time: 132 us; the launch traced here: 131 us
  blocking collectives  78.2 us (59%)
  starting transfers between devices  24.7 us (19%)
  Pallas kernels  13.4 us (10%)
  waiting for transfers between devices  10.6 us (8%)
  local copies, waits for them, and re-layouts  2.34 us (2%)
    all_to_all x3, blocking collectives, gathered(): lax.all_to_all(jnp.broadcast_to(value[None], (count,) + value.shape), axe...  43 us
    all_to_all x1, blocking collectives, body(): block = lax.all_to_all(message, ('x', 'y_hi'), 0, 0)  24.8 us
    ppermute x6, starting transfers between devices, halo(): lax.ppermute(block, BLK, route)  24.7 us
    ppermute x6, waiting for transfers between devices, halo(): lax.ppermute(block, BLK, route)  10.6 us
    pallas_call x2, Pallas kernels, body(): call(build_more, (shape(RHS, 2 * WIDTH), kernel_shape()), in_specs=[SMEM]...  6.08 us
    all_gather x2, blocking collectives, body(): both = lax.all_gather(peer_total, 'core')  5.29 us
    all_gather x1, blocking collectives, body(): both = lax.all_gather(coords, 'core')  5.09 us
    pallas_call x1, Pallas kernels, body(): call(build_first, (shape(2 * WIDTH, DEPTH, dtype=BF16), shape(RHS, 2 * WI...  2.71 us
  transfers between devices with their start and end apart: 6, of which 3 were waited for; matrix products, arithmetic and copies ran while one was open for 0% of the time, Pallas kernels for 9%

profile of v5, /device:TPU:1, one launch (start us, length us, event | category | flops | bytes accessed | tf_op | source)
XLA Modules:
  0.0 131.2 jit_solution(13280074457106065124)
XLA Ops:
  0.6 0.8 copy-done
  1.5 0.8 copy-done.2
  3.0 24.8 %all_to_all.20.block_ref = bf16[8,128,256]{2,1,0:T(8,128)(2,1)S(1)} all-to-all(bf16[8,128,256]{2,1,0:T(8,128)(2,1)S(1)} %shard_map.59), channel_id=1, replica_groups=mesh['y_lo'=4,'z'=8,'core'=2,'x'=4,'y_hi'=2] {'x','y_hi'}, dimensions={0} | all-to-all | bytes 1048576 | tf_op jit(solution)/shard_map/all_to_all | solution.py:205
  27.9 4.0 %collective-permute-start = (bf16[8,96,256]{2,1,0:T(8,128)(2,1)S(1)}, bf16[8,96,256]{2,1,0:T(8,128)(2,1)S(1)}, u32[]{:S(2)}, u32[]{:S(2)}) collective-permute-start(bf16[8,96,256]{2,1,0:T(8,128)(2,1)S(1)} %slice.48), channel_id=1, source_target_pairs={{0,16},{8,24},{16,0},{24,8},{32,48},{40,56},{48,32},{56,40},{64,80... | collective-permute-start | bytes 1179656 | tf_op jit(solution)/shard_map/ppermute | solution.py:185
  31.9 7.5 %collective-permute-start.1 = (bf16[8,96,256]{2,1,0:T(8,128)(2,1)S(1)}, bf16[8,96,256]{2,1,0:T(8,128)(2,1)S(1)}, u32[]{:S(2)}, u32[]{:S(2)}) collective-permute-start(bf16[8,96,256]{2,1,0:T(8,128)(2,1)S(1)} %slice.48), channel_id=1, source_target_pairs={{0,496},{8,504},{16,32},{24,40},{32,16},{40,24},{48,64},{56,72},{6... | collective-permute-start | bytes 1179656 | tf_op jit(solution)/shard_map/ppermute | solution.py:185
  39.4 1.9 %collective-permute-start.2 = (bf16[8,96,256]{2,1,0:T(8,128)(2,1)S(1)}, bf16[8,96,256]{2,1,0:T(8,128)(2,1)S(1)}, u32[]{:S(2)}, u32[]{:S(2)}) collective-permute-start(bf16[8,96,256]{2,1,0:T(8,128)(2,1)S(1)} %slice.48), channel_id=1, source_target_pairs={{0,480},{8,40},{16,496},{24,56},{32,0},{40,72},{48,16},{56,88},{64... | collective-permute-start | bytes 1179656 | tf_op jit(solution)/shard_map/ppermute | solution.py:185
  41.3 5.1 %all-gather = bf16[128,256]{1,0:T(8,128)(2,1)S(1)} all-gather(bf16[64,256]{1,0:T(8,128)(2,1)S(1)} %pad_maximum_fusion), channel_id=2, replica_groups=mesh['y_lo'=4,'z'=8,'core'=2,'x'=4,'y_hi'=2] {'core'}, dimensions={0}, use_global_device_ids=true | all-gather | bytes 98304 | tf_op jit(solution)/shard_map/all_gather | solution.py:204
  46.6 2.7 %shard_map.60 = (bf16[512,144]{1,0:T(8,128)(2,1)S(1)}, f32[64,512]{1,0:T(8,128)S(1)}, bf16[8,512,256]{2,1,0:T(8,128)(2,1)S(1)}) custom-call(s32[1]{0:T(128)} %bitcast.core_ref, bf16[2,64,256]{2,1,0:T(8,128)(2,1)S(1)} %bitcast.60, bf16[8,128,256]{2,1,0:T(8,128)(2,1)S(1)} %all_to_all.20.block_ref), custom_call_target="tpu_custom_call" | custom-call | tf_op jit(solution)/shard_map/pallas_call | solution.py:210
  49.3 3.0 %shard_map.61 = (f32[64,512]{1,0:T(8,128)S(1)}, bf16[8,512,256]{2,1,0:T(8,128)(2,1)S(1)}) custom-call(f32[2]{0:T(128)S(1)} %pad_maximum_fusion.1.level_ref, bf16[512,144]{1,0:T(8,128)(2,1)S(1)} %get-tuple-element.13.weights_ref, f32[64,512]{1,0:T(8,128)S(1)} %get-tuple-element.14.before_ref, bf16[8,96,256]{2,1,0:T(8,128)(2,1)S(1)} %collective-permute-done.block_ref), custom_call_target="tpu_custom_call" | custom-call | tf_op jit(solution)/shard_map/pallas_call | solution.py:218
  52.4 3.0 %shard_map.62 = (f32[64,512]{1,0:T(8,128)S(1)}, bf16[8,512,256]{2,1,0:T(8,128)(2,1)S(1)}) custom-call(f32[2]{0:T(128)S(1)} %pad_maximum_fusion.2.level_ref, bf16[512,144]{1,0:T(8,128)(2,1)S(1)} %get-tuple-element.13.weights_ref, f32[64,512]{1,0:T(8,128)S(1)} %get-tuple-element.15.before_ref, bf16[8,96,256]{2,1,0:T(8,128)(2,1)S(1)} %collective-permute-done.1.block_ref), custom_call_target="tpu_custom_call" | custom-call | tf_op jit(solution)/shard_map/pallas_call | solution.py:218
  55.4 1.3 collective-permute-done.2.block_ref
  56.7 1.2 shard_map.63
  57.8 3.4 %all-gather.1 = f32[128,256]{1,0:T(8,128)S(1)} all-gather(f32[64,256]{1,0:T(8,128)S(1)} %get-tuple-element.17), channel_id=3, replica_groups=mesh['y_lo'=4,'z'=8,'core'=2,'x'=4,'y_hi'=2] {'core'}, dimensions={0}, use_global_device_ids=true | all-gather | bytes 196608 | tf_op jit(solution)/shard_map/all_gather | solution.py:230
  61.3 14.5 %all_to_all.21.block_ref = bf16[8,64,256]{2,1,0:T(8,128)(2,1)S(1)} all-to-all(bf16[8,64,256]{2,1,0:T(8,128)(2,1)S(1)} %broadcast_in_dim.12), channel_id=1, replica_groups=mesh['y_lo'=4,'z'=8,'core'=2,'x'=4,'y_hi'=2] {'x','y_hi'}, dimensions={0} | all-to-all | bytes 524288 | tf_op jit(solution)/shard_map/all_to_all | solution.py:178
  75.8 1.9 %collective-permute-start.3 = (bf16[8,64,256]{2,1,0:T(8,128)(2,1)S(1)}, bf16[8,64,256]{2,1,0:T(8,128)(2,1)S(1)}, u32[]{:S(2)}, u32[]{:S(2)}) collective-permute-start(bf16[8,64,256]{2,1,0:T(8,128)(2,1)S(1)} %all_to_all.21.block_ref), channel_id=1, source_target_pairs={{0,16},{8,24},{16,0},{24,8},{32,48},{40,56},{48,32},{56,40},{64,80... | collective-permute-start | bytes 786440 | tf_op jit(solution)/shard_map/ppermute | solution.py:185
  77.7 7.4 %collective-permute-start.4 = (bf16[8,64,256]{2,1,0:T(8,128)(2,1)S(1)}, bf16[8,64,256]{2,1,0:T(8,128)(2,1)S(1)}, u32[]{:S(2)}, u32[]{:S(2)}) collective-permute-start(bf16[8,64,256]{2,1,0:T(8,128)(2,1)S(1)} %all_to_all.21.block_ref), channel_id=1, source_target_pairs={{0,496},{8,504},{16,32},{24,40},{32,16},{40,24},{48,64},{56,72},{6... | collective-permute-start | bytes 786440 | tf_op jit(solution)/shard_map/ppermute | solution.py:185
  85.1 1.9 %collective-permute-start.5 = (bf16[8,64,256]{2,1,0:T(8,128)(2,1)S(1)}, bf16[8,64,256]{2,1,0:T(8,128)(2,1)S(1)}, u32[]{:S(2)}, u32[]{:S(2)}) collective-permute-start(bf16[8,64,256]{2,1,0:T(8,128)(2,1)S(1)} %all_to_all.21.block_ref), channel_id=1, source_target_pairs={{0,480},{8,40},{16,496},{24,56},{32,0},{40,72},{48,16},{56,88},{64... | collective-permute-start | bytes 786440 | tf_op jit(solution)/shard_map/ppermute | solution.py:185
  87.4 0.8 shard_map.65.before_ref
  88.1 0.8 shard_map.66.before_ref
  90.4 8.6 %collective-permute-done.5.block_ref = bf16[8,64,256]{2,1,0:T(8,128)(2,1)S(1)} collective-permute-done((bf16[8,64,256]{2,1,0:T(8,128)(2,1)S(1)}, bf16[8,64,256]{2,1,0:T(8,128)(2,1)S(1)}, u32[]{:S(2)}, u32[]{:S(2)}) %collective-permute-start.5) | collective-permute-done | bytes 262176 | tf_op jit(solution)/shard_map/ppermute | solution.py:185
  99.4 1.9 %all-gather.2 = f32[128,256]{1,0:T(8,128)S(1)} all-gather(f32[64,256]{1,0:T(8,128)S(1)} %shard_map.68), channel_id=4, replica_groups=mesh['y_lo'=4,'z'=8,'core'=2,'x'=4,'y_hi'=2] {'core'}, dimensions={0}, use_global_device_ids=true | all-gather | bytes 196608 | tf_op jit(solution)/shard_map/all_gather | solution.py:240
  101.6 14.1 %all_to_all.22 = f32[32,4,128]{2,1,0:T(4,128)S(1)} all-to-all(f32[32,4,128]{2,1,0:T(4,128)S(1)} %broadcast_in_dim.13), channel_id=1, replica_groups=mesh['y_lo'=4,'z'=8,'core'=2,'x'=4,'y_hi'=2] {'x','y_hi','y_lo'}, dimensions={0} | all-to-all | bytes 131072 | tf_op jit(solution)/shard_map/all_to_all | solution.py:178
  115.8 14.4 %all_to_all.23 = f32[16,4,128]{2,1,0:T(4,128)S(1)} all-to-all(f32[16,4,128]{2,1,0:T(4,128)S(1)} %broadcast_in_dim.14), channel_id=1, replica_groups=mesh['y_lo'=4,'z'=8,'core'=2,'x'=4,'y_hi'=2] {'z','core'}, dimensions={0} | all-to-all | bytes 65536 | tf_op jit(solution)/shard_map/all_to_all | solution.py:178
  130.4 0.8 multiply_add_fusion
  (31 shorter events, 3.8 us)
Async XLA Ops:
  0.6 0.8 copy-start
  1.5 0.8 copy-start.2
  2.2 0.7 copy-start.4
  27.8 33.4 %copy-start.1 = (f32[64,256]{1,0:T(8,128)S(1)}, f32[64,256]{1,0:T(8,128)}, u32[]{:S(2)}) copy-start(f32[64,256]{1,0:T(8,128)} %first_ref.3) | copy-start | bytes 196612
  27.8 33.4 %copy-start.3 = (f32[256]{0:T(256)S(1)}, f32[256]{0:T(256)}, u32[]{:S(2)}) copy-start(f32[256]{0:T(256)} %param.6) | copy-start | bytes 3076
  27.9 21.4 %collective-permute-start = (bf16[8,96,256]{2,1,0:T(8,128)(2,1)S(1)}, bf16[8,96,256]{2,1,0:T(8,128)(2,1)S(1)}, u32[]{:S(2)}, u32[]{:S(2)}) collective-permute-start(bf16[8,96,256]{2,1,0:T(8,128)(2,1)S(1)} %slice.48), channel_id=1, source_target_pairs={{0,16},{8,24},{16,0},{24,8},{32,48},{40,56},{48,32},{56,40},{64,80... | collective-permute-start | bytes 1179656 | tf_op jit(solution)/shard_map/ppermute | solution.py:185
  31.9 20.5 %collective-permute-start.1 = (bf16[8,96,256]{2,1,0:T(8,128)(2,1)S(1)}, bf16[8,96,256]{2,1,0:T(8,128)(2,1)S(1)}, u32[]{:S(2)}, u32[]{:S(2)}) collective-permute-start(bf16[8,96,256]{2,1,0:T(8,128)(2,1)S(1)} %slice.48), channel_id=1, source_target_pairs={{0,496},{8,504},{16,32},{24,40},{32,16},{40,24},{48,64},{56,72},{6... | collective-permute-start | bytes 1179656 | tf_op jit(solution)/shard_map/ppermute | solution.py:185
  39.4 17.3 %collective-permute-start.2 = (bf16[8,96,256]{2,1,0:T(8,128)(2,1)S(1)}, bf16[8,96,256]{2,1,0:T(8,128)(2,1)S(1)}, u32[]{:S(2)}, u32[]{:S(2)}) collective-permute-start(bf16[8,96,256]{2,1,0:T(8,128)(2,1)S(1)} %slice.48), channel_id=1, source_target_pairs={{0,480},{8,40},{16,496},{24,56},{32,0},{40,72},{48,16},{56,88},{64... | collective-permute-start | bytes 1179656 | tf_op jit(solution)/shard_map/ppermute | solution.py:185
  75.8 12.4 %collective-permute-start.3 = (bf16[8,64,256]{2,1,0:T(8,128)(2,1)S(1)}, bf16[8,64,256]{2,1,0:T(8,128)(2,1)S(1)}, u32[]{:S(2)}, u32[]{:S(2)}) collective-permute-start(bf16[8,64,256]{2,1,0:T(8,128)(2,1)S(1)} %all_to_all.21.block_ref), channel_id=1, source_target_pairs={{0,16},{8,24},{16,0},{24,8},{32,48},{40,56},{48,32},{56,40},{64,80... | collective-permute-start | bytes 786440 | tf_op jit(solution)/shard_map/ppermute | solution.py:185
  77.7 12.0 %collective-permute-start.4 = (bf16[8,64,256]{2,1,0:T(8,128)(2,1)S(1)}, bf16[8,64,256]{2,1,0:T(8,128)(2,1)S(1)}, u32[]{:S(2)}, u32[]{:S(2)}) collective-permute-start(bf16[8,64,256]{2,1,0:T(8,128)(2,1)S(1)} %all_to_all.21.block_ref), channel_id=1, source_target_pairs={{0,496},{8,504},{16,32},{24,40},{32,16},{40,24},{48,64},{56,72},{6... | collective-permute-start | bytes 786440 | tf_op jit(solution)/shard_map/ppermute | solution.py:185
  85.1 13.9 %collective-permute-start.5 = (bf16[8,64,256]{2,1,0:T(8,128)(2,1)S(1)}, bf16[8,64,256]{2,1,0:T(8,128)(2,1)S(1)}, u32[]{:S(2)}, u32[]{:S(2)}) collective-permute-start(bf16[8,64,256]{2,1,0:T(8,128)(2,1)S(1)} %all_to_all.21.block_ref), channel_id=1, source_target_pairs={{0,480},{8,40},{16,496},{24,56},{32,0},{40,72},{48,16},{56,88},{64... | collective-permute-start | bytes 786440 | tf_op jit(solution)/shard_map/ppermute | solution.py:185

commit v6 on v5

v6 whole, which is shorter than its diff:
```python
import functools
import math

import jax
import jax.numpy as jnp
from jax import lax
from jax.experimental import pallas as pl
from jax.experimental.pallas import tpu as pltpu
from jax.sharding import Mesh, PartitionSpec as P

F32, BF16 = jnp.float32, jnp.bfloat16
AXES = ("y_lo", "z", "core", "x", "y_hi")
SIZES = (4, 8, 2, 4, 2)
BLK = ("y_lo", "z", "core")
N_BLK = 64

LN2 = math.log(2.0)
UNIT = math.sqrt(5.0) / LN2
SHIFT = 1.5 / LN2
OFFSET = 0.75 / LN2**2
LEVEL = math.log2(LN2**2 / 3.0) + SHIFT
LEVELS = tuple(LEVEL + math.log2(taper) for taper in (1.0, 0.75, 0.5, 0.25))
TINY = 1e-20

FEAT = 32
RHS = 64
WIDTH = 256
ROUGH = 80
DEPTH = 144
TOLD = 96
SHARDS = 8
SIGMA = 0.5
NT = (((1,), (1,)), ((), ()))


def square_rows(coords, first, second):
    squares = jnp.sum(coords * coords, axis=0, keepdims=True)
    one = squares.astype(BF16).astype(F32)
    two = (squares - one).astype(BF16).astype(F32)
    three = squares - one - two
    row = lax.broadcasted_iota(jnp.int32, (16, coords.shape[1]), 0)
    out = jnp.where((row >= second) & (row < second + 3), 1.0, 0.0)
    for at, piece in enumerate((one, two, three)):
        out = jnp.where(row == first + at, piece, out)
    return out.astype(BF16)


def build_shard(weights, levels, shard, cols_ref, dist_ref, kernel_ref):
    high = shard[:FEAT]
    coords = high.astype(F32)
    cols_ref[:FEAT] = high
    cols_ref[FEAT : 2 * FEAT] = high
    depth = ROUGH
    if shard.shape[0] > TOLD:
        low = shard[TOLD:]
        coords = coords + low.astype(F32)
        cols_ref[ROUGH : ROUGH + FEAT] = low
        cols_ref[ROUGH + FEAT :] = low
        depth = DEPTH
    cols_ref[2 * FEAT : ROUGH] = square_rows(coords, 0, 3)
    dist_ref[...] = jnp.dot(weights[:, :depth], cols_ref[:depth], preferred_element_type=F32)
    step = 64
    for half, level in enumerate(levels):
        for at in range(half * WIDTH, (half + 1) * WIDTH, step):
            part = jnp.maximum(dist_ref[at : at + step], TINY)
            moved = part * lax.rsqrt(part) + SHIFT
            entry = (moved * moved + OFFSET) * jnp.exp2(level - moved)
            kernel_ref[at : at + step] = entry.astype(BF16)
    return lax.dot_general(shard[FEAT:TOLD], kernel_ref[...], NT, preferred_element_type=F32)


def build_block(weights, levels, block_ref, cols_ref, dist_ref, kernel_ref):
    total = None
    for i in range(SHARDS):
        part = build_shard(weights, levels, block_ref[i], cols_ref.at[i % 2], dist_ref.at[i % 2], kernel_ref.at[i])
        total = part if total is None else total + part
    return total


def build_first(both_ref, block_ref, weights_ref, own_ref, peer_ref, kernel_ref, cols_ref, dist_ref):
    core = lax.axis_index("core")
    for at, ref in enumerate((both_ref.at[core], both_ref.at[1 - core])):
        rows = slice(at * WIDTH, (at + 1) * WIDTH)
        high, low = ref[:FEAT].astype(F32), ref[FEAT:].astype(F32)
        extra = square_rows(high + low, 3, 0).astype(F32)
        halves = jnp.transpose(jnp.concatenate([-2.0 * high, -2.0 * low], axis=0)).astype(BF16)
        weights_ref[rows, : 2 * FEAT] = halves
        weights_ref[rows, 2 * FEAT : ROUGH] = jnp.transpose(extra).astype(BF16)
        weights_ref[rows, ROUGH:] = halves
    total = build_block(weights_ref[...], LEVELS[:2], block_ref, cols_ref, dist_ref, kernel_ref)
    own_ref[...] = total[:, :WIDTH]
    peer_ref[...] = total[:, WIDTH:]


def build_far(weights_ref, before_ref, block_ref, peer_ref, kernel_ref, cols_ref, dist_ref):
    peer_ref[...] = before_ref[...] + build_block(
        weights_ref[WIDTH:], LEVELS[3:], block_ref, cols_ref, dist_ref, kernel_ref
    )


def build_pair(
    second, weights_ref, own_before, peer_before, block_ref, own_ref, peer_ref, kernel_ref, cols_ref, dist_ref
):
    near = (lax.axis_index("z") + lax.axis_index("core") + second) % 2 == 0
    levels = LEVELS[2], jnp.where(near, LEVELS[1], LEVELS[3])
    total = build_block(weights_ref[...], levels, block_ref, cols_ref, dist_ref, kernel_ref)
    own_ref[...] = own_before[...] + total[:, :WIDTH]
    peer_ref[...] = peer_before[...] + total[:, WIDTH:]


def apply_block(kernel_ref, block_ref):
    total = None
    for i in range(SHARDS):
        part = lax.dot_general(block_ref[i], kernel_ref[i], NT, preferred_element_type=F32)
        total = part if total is None else total + part
    return total


def apply_first(kernel_ref, block_ref, own_ref, peer_ref):
    total = apply_block(kernel_ref, block_ref)
    own_ref[...] = total[:, :WIDTH]
    peer_ref[...] = total[:, WIDTH:]


def apply_far(kernel_ref, before_ref, block_ref, peer_ref):
    peer_ref[...] = before_ref[...] + apply_block(kernel_ref, block_ref)


def apply_pair(kernel_ref, own_before, peer_before, block_ref, own_ref, peer_ref):
    total = apply_block(kernel_ref, block_ref)
    own_ref[...] = own_before[...] + total[:, :WIDTH]
    peer_ref[...] = peer_before[...] + total[:, WIDTH:]


def row_sum(product):
    ones = jnp.ones((8, WIDTH), F32)
    total = lax.dot_general(ones, product, NT, precision=lax.Precision.HIGHEST, preferred_element_type=F32)
    return total[:1]


def early_sums(first_ref, image_ref, sums_ref):
    first, image = first_ref[...], image_ref[...]
    sums_ref[0:1, :RHS] = row_sum(first * first)
    sums_ref[0:1, RHS:] = row_sum(first * image)
    sums_ref[1:2, :RHS] = row_sum(image * image)
    sums_ref[1:2, RHS:] = jnp.zeros((1, RHS), F32)


def late_sums(
    early_ref, noise_ref, first_ref, first_total_ref, image_ref, own_ref, both_ref, second_ref, sums_ref
):
    first, image = first_ref[...], image_ref[...]
    total = own_ref[...] + both_ref[1 - lax.axis_index("core")]
    second = noise_ref[...] * image + (first_total_ref[...] - total) * (1.0 / SIGMA)
    second_ref[...] = second
    sums_ref[0:2] = early_ref[...]
    sums_ref[2:3, :RHS] = row_sum(first * second)
    sums_ref[2:3, RHS:] = row_sum(image * second)
    sums_ref[3:4] = jnp.zeros((1, 2 * RHS), F32)


VMEM_LIMIT = pltpu.CompilerParams(vmem_limit_bytes=48 * 1024 * 1024)


def scratch(rows=2 * WIDTH):
    return [pltpu.VMEM((2, DEPTH, WIDTH), BF16), pltpu.VMEM((2, rows, WIDTH), F32)]


def shape(*dims, dtype=F32):
    return jax.ShapeDtypeStruct(dims, dtype)


def gathered(value, axes):
    count = math.prod(SIZES[AXES.index(axis)] for axis in axes)
    return lax.all_to_all(jnp.broadcast_to(value[None], (count,) + value.shape), axes, 0, 0)


def halo(block):
    first = [(i, i + 2 if i // 2 % 2 == 0 else i - 2) for i in range(N_BLK)]
    second = [(i, (i - 2 if i // 2 % 2 == 0 else i + 2) % N_BLK) for i in range(N_BLK)]
    fourth = [(i, (i - 4 if i % 2 == 0 else i + 4) % N_BLK) for i in range(N_BLK)]
    return tuple(lax.ppermute(block, BLK, route) for route in (fourth, first, second))


def kernel_shape(rows=2 * WIDTH):
    return shape(SHARDS, rows, WIDTH, dtype=BF16)


def call(body, out_shape, scratch_shapes=()):
    return pl.pallas_call(body, out_shape=out_shape, scratch_shapes=scratch_shapes, compiler_params=VMEM_LIMIT)


def body(points, lengthscale, noise_var, targets):
    coords = points / lengthscale[:, None] * UNIT
    high = lax.reduce_precision(coords, 8, 7)
    message = jnp.concatenate([high, targets, coords - high], axis=0).astype(BF16)
    coords = jnp.concatenate([message[:FEAT], message[TOLD:]], axis=0)
    both = lax.all_gather(coords, "core")
    block = gathered(message, ("x", "y_hi"))
    far, *pairs = halo(block[:, :TOLD])

    half = shape(RHS, WIDTH)
    weights, own, peer, kernel_own = call(
        build_first,
        (shape(2 * WIDTH, DEPTH, dtype=BF16), half, half, kernel_shape()),
        scratch_shapes=scratch(),
    )(both, block)
    peer, kernel_far = call(build_far, (half, kernel_shape(WIDTH)), scratch_shapes=scratch(WIDTH))(weights, peer, far)
    kernels = []
    for second, moved in enumerate(pairs):
        own, peer, made = call(
            functools.partial(build_pair, second), (half, half, kernel_shape()), scratch_shapes=scratch()
        )(weights, own, peer, moved)
        kernels.append(made)

    noise = noise_var[None, :]
    both = lax.all_gather(peer, "core")
    first_total = own + jnp.where(lax.axis_index("core") == 0, both[1], both[0])
    image = noise * targets + first_total
    block = gathered((targets - SIGMA * image).astype(BF16), ("x", "y_hi"))
    far, *pairs = halo(block)
    early = call(early_sums, shape(2, 2 * RHS))(targets, image)
    own, peer = call(apply_first, (half, half))(kernel_own, block)
    peer = call(apply_far, half)(kernel_far, peer, far)
    for made, moved in zip(kernels, pairs):
        own, peer = call(apply_pair, (half, half))(made, own, peer, moved)
    both = lax.all_gather(peer, "core")
    second, sums = call(late_sums, (half, shape(4, 2 * RHS)))(
        early, noise, targets, first_total, image, own, both
    )
    for axes in (("x", "y_hi", "y_lo"), ("z", "core")):
        sums = jnp.sum(gathered(sums, axes), axis=0)

    (rr, rq), (qq, _), (rs, qs) = ((sums[i, :RHS], sums[i, RHS:]) for i in range(3))
    step = rr / rq
    norm_next = jnp.maximum(rr - 2.0 * step * rq + step * step * qq, 0.0)
    grown = 1.0 + norm_next / rr
    curvature = grown * grown * rq - step * grown * (qq + rs) + step * step * qs
    step_next = norm_next / curvature
    along = (step + step_next * grown)[:, None]
    across = (step_next * step)[:, None]
    solution = along * targets - across * image
    residual = targets - along * image + across * second
    return solution, residual


def solution(mesh):
    fine = Mesh(mesh.devices.reshape(SIZES), AXES)
    placed = (P(None, AXES), P(), P(AXES), P(None, AXES))
    return jax.shard_map(
        body, mesh=fine, in_specs=placed, out_specs=(P(None, AXES), P(None, AXES)), check_vma=False
    )
```

time: 132 us -> 130 us (0.985)
  waiting for transfers between devices: 10.6 us -> 5.64 us
  blocking collectives: 78.2 us -> 82.8 us
  local copies, waits for them, and re-layouts: 2.34 us -> 0.13 us
  other arithmetic: 1.17 us -> 2.71 us
    all_to_all x1 -> x0, blocking collectives: 24.8 us -> none  [body(): block = lax.all_to_all(message, ('x', 'y_hi'), 0, 0)]
    all_to_all x3 -> x4, blocking collectives: 43 us -> 66.5 us  [gathered(): lax.all_to_all(jnp.broadcast_to(value[None], (count,) + value.shape), axe...]
    all_gather x2, blocking collectives: 5.29 us -> 11.2 us  [body(): both = lax.all_gather(peer, 'core')]
    ppermute x6, waiting for transfers between devices: 10.6 us -> 5.64 us  [halo(): lax.ppermute(block, BLK, route)]
    unnamed x10 -> x4, local copies, waits for them, and re-layouts: 2.25 us -> 0.01 us
    pallas_call x10 -> x9, Pallas kernels: 13.1 us -> 11.9 us  [the longest x2 5.01 us: body(): call(functools.partial(build_pair, second), (half, half, kernel_shape()),...]
  transfers between devices with their start and end apart: 6 -> 6, of which waited for: 3 -> 4; matrix products, arithmetic and copies ran while one was open for 0% -> 0% of each run, Pallas kernels for 9% -> 7%
where the time goes in v6:
time: 130 us
  blocking collectives  82.8 us (64%)
  starting transfers between devices  25.7 us (20%)
  Pallas kernels  12.2 us (9%)
  waiting for transfers between devices  5.64 us (4%)
  other arithmetic  2.71 us (2%)
    all_to_all x4, blocking collectives, gathered(): lax.all_to_all(jnp.broadcast_to(value[None], (count,) + value.shape), axe...  66.5 us
    ppermute x6, starting transfers between devices, halo(): lax.ppermute(block, BLK, route)  25.7 us
    all_gather x2, blocking collectives, body(): both = lax.all_gather(peer, 'core')  11.2 us
    ppermute x6, waiting for transfers between devices, halo(): lax.ppermute(block, BLK, route)  5.64 us
    all_gather x1, blocking collectives, body(): both = lax.all_gather(coords, 'core')  5.09 us
    pallas_call x2, Pallas kernels, body(): call(functools.partial(build_pair, second), (half, half, kernel_shape()),...  5.01 us
    pallas_call x1, Pallas kernels, body(): call(build_first, (shape(2 * WIDTH, DEPTH, dtype=BF16), half, half, kerne...  2.7 us
  transfers between devices with their start and end apart: 6, of which 4 were waited for; matrix products, arithmetic and copies ran while one was open for 0% of the time, Pallas kernels for 7%

profile of v6, /device:TPU:1, one launch (start us, length us, event | category | flops | bytes accessed | tf_op | source)
XLA Modules:
  0.0 129.9 jit_solution(11617242715304387943)
XLA Ops:
  0.6 0.8 convert.5
  1.5 0.8 reduce-precision_convert_fusion
  2.4 24.8 %all_to_all.20.block_ref = bf16[8,128,256]{2,1,0:T(8,128)(2,1)S(1)} all-to-all(bf16[8,128,256]{2,1,0:T(8,128)(2,1)S(1)} %broadcast_in_dim.10), channel_id=1, replica_groups=mesh['y_lo'=4,'z'=8,'core'=2,'x'=4,'y_hi'=2] {'x','y_hi'}, dimensions={0} | all-to-all | bytes 1048576 | tf_op jit(solution)/shard_map/all_to_all | solution.py:175
  27.2 5.8 %collective-permute-start = (bf16[8,96,256]{2,1,0:T(8,128)(2,1)S(1)}, bf16[8,96,256]{2,1,0:T(8,128)(2,1)S(1)}, u32[]{:S(2)}, u32[]{:S(2)}) collective-permute-start(bf16[8,96,256]{2,1,0:T(8,128)(2,1)S(1)} %slice.42), channel_id=1, source_target_pairs={{0,480},{8,40},{16,496},{24,56},{32,0},{40,72},{48,16},{56,88},{64... | collective-permute-start | bytes 1179656 | tf_op jit(solution)/shard_map/ppermute | solution.py:182
  33.1 4.0 %collective-permute-start.1 = (bf16[8,96,256]{2,1,0:T(8,128)(2,1)S(1)}, bf16[8,96,256]{2,1,0:T(8,128)(2,1)S(1)}, u32[]{:S(2)}, u32[]{:S(2)}) collective-permute-start(bf16[8,96,256]{2,1,0:T(8,128)(2,1)S(1)} %slice.42), channel_id=1, source_target_pairs={{0,16},{8,24},{16,0},{24,8},{32,48},{40,56},{48,32},{56,40},{64,80... | collective-permute-start | bytes 1179656 | tf_op jit(solution)/shard_map/ppermute | solution.py:182
  37.1 3.6 %collective-permute-start.2 = (bf16[8,96,256]{2,1,0:T(8,128)(2,1)S(1)}, bf16[8,96,256]{2,1,0:T(8,128)(2,1)S(1)}, u32[]{:S(2)}, u32[]{:S(2)}) collective-permute-start(bf16[8,96,256]{2,1,0:T(8,128)(2,1)S(1)} %slice.42), channel_id=1, source_target_pairs={{0,496},{8,504},{16,32},{24,40},{32,16},{40,24},{48,64},{56,72},{6... | collective-permute-start | bytes 1179656 | tf_op jit(solution)/shard_map/ppermute | solution.py:182
  40.7 5.1 %all-gather = bf16[128,256]{1,0:T(8,128)(2,1)S(1)} all-gather(bf16[64,256]{1,0:T(8,128)(2,1)S(1)} %pad_maximum_fusion.1), channel_id=2, replica_groups=mesh['y_lo'=4,'z'=8,'core'=2,'x'=4,'y_hi'=2] {'core'}, dimensions={0}, use_global_device_ids=true | all-gather | bytes 98304 | tf_op jit(solution)/shard_map/all_gather | solution.py:198
  45.8 2.7 %shard_map.59 = (bf16[512,144]{1,0:T(8,128)(2,1)S(1)}, f32[64,256]{1,0:T(8,128)S(1)}, f32[64,256]{1,0:T(8,128)S(1)}, bf16[8,512,256]{2,1,0:T(8,128)(2,1)S(1)}) custom-call(bf16[2,64,256]{2,1,0:T(8,128)(2,1)S(1)} %bitcast.52, bf16[8,128,256]{2,1,0:T(8,128)(2,1)S(1)} %all_to_all.20.block_ref), custom_call_target="tpu_custom_call" | custom-call | tf_op jit(solution)/shard_map/pallas_call | solution.py:203
  48.5 1.2 shard_map.60
  49.7 2.5 %shard_map.61 = (f32[64,256]{1,0:T(8,128)S(1)}, f32[64,256]{1,0:T(8,128)S(1)}, bf16[8,512,256]{2,1,0:T(8,128)(2,1)S(1)}) custom-call(bf16[512,144]{1,0:T(8,128)(2,1)S(1)} %get-tuple-element.22.weights_ref, f32[64,256]{1,0:T(8,128)S(1)} %get-tuple-element.23.own_before, f32[64,256]{1,0:T(8,128)S(1)} %get-tuple-element.25.peer_before, ...), custom_call_target="tpu_custom_call" | custom-call | tf_op jit(solution)/shard_map/pallas_call | solution.py:211
  52.2 1.5 %collective-permute-done.2.block_ref = bf16[8,96,256]{2,1,0:T(8,128)(2,1)S(1)} collective-permute-done((bf16[8,96,256]{2,1,0:T(8,128)(2,1)S(1)}, bf16[8,96,256]{2,1,0:T(8,128)(2,1)S(1)}, u32[]{:S(2)}, u32[]{:S(2)}) %collective-permute-start.2) | collective-permute-done | bytes 393248 | tf_op jit(solution)/shard_map/ppermute | solution.py:182
  53.7 2.5 %shard_map.62 = (f32[64,256]{1,0:T(8,128)S(1)}, f32[64,256]{1,0:T(8,128)S(1)}, bf16[8,512,256]{2,1,0:T(8,128)(2,1)S(1)}) custom-call(bf16[512,144]{1,0:T(8,128)(2,1)S(1)} %get-tuple-element.22.weights_ref, f32[64,256]{1,0:T(8,128)S(1)} %get-tuple-element.26.own_before, f32[64,256]{1,0:T(8,128)S(1)} %get-tuple-element.27.peer_before, ...), custom_call_target="tpu_custom_call" | custom-call | tf_op jit(solution)/shard_map/pallas_call | solution.py:211
  56.2 4.5 %all-gather.1 = f32[128,256]{1,0:T(8,128)S(1)} all-gather(f32[64,256]{1,0:T(8,128)S(1)} %get-tuple-element.29), channel_id=3, replica_groups=mesh['y_lo'=4,'z'=8,'core'=2,'x'=4,'y_hi'=2] {'core'}, dimensions={0}, use_global_device_ids=true | all-gather | bytes 196608 | tf_op jit(solution)/shard_map/all_gather | solution.py:217
  60.8 14.7 %all_to_all.21.block_ref = bf16[8,64,256]{2,1,0:T(8,128)(2,1)S(1)} all-to-all(bf16[8,64,256]{2,1,0:T(8,128)(2,1)S(1)} %broadcast_in_dim.12), channel_id=1, replica_groups=mesh['y_lo'=4,'z'=8,'core'=2,'x'=4,'y_hi'=2] {'x','y_hi'}, dimensions={0} | all-to-all | bytes 524288 | tf_op jit(solution)/shard_map/all_to_all | solution.py:175
  75.5 2.1 %collective-permute-start.3 = (bf16[8,64,256]{2,1,0:T(8,128)(2,1)S(1)}, bf16[8,64,256]{2,1,0:T(8,128)(2,1)S(1)}, u32[]{:S(2)}, u32[]{:S(2)}) collective-permute-start(bf16[8,64,256]{2,1,0:T(8,128)(2,1)S(1)} %all_to_all.21.block_ref), channel_id=1, source_target_pairs={{0,480},{8,40},{16,496},{24,56},{32,0},{40,72},{48,16},{56,88},{64... | collective-permute-start | bytes 786440 | tf_op jit(solution)/shard_map/ppermute | solution.py:182
  77.7 4.4 %collective-permute-start.4 = (bf16[8,64,256]{2,1,0:T(8,128)(2,1)S(1)}, bf16[8,64,256]{2,1,0:T(8,128)(2,1)S(1)}, u32[]{:S(2)}, u32[]{:S(2)}) collective-permute-start(bf16[8,64,256]{2,1,0:T(8,128)(2,1)S(1)} %all_to_all.21.block_ref), channel_id=1, source_target_pairs={{0,16},{8,24},{16,0},{24,8},{32,48},{40,56},{48,32},{56,40},{64,80... | collective-permute-start | bytes 786440 | tf_op jit(solution)/shard_map/ppermute | solution.py:182
  82.0 5.8 %collective-permute-start.5 = (bf16[8,64,256]{2,1,0:T(8,128)(2,1)S(1)}, bf16[8,64,256]{2,1,0:T(8,128)(2,1)S(1)}, u32[]{:S(2)}, u32[]{:S(2)}) collective-permute-start(bf16[8,64,256]{2,1,0:T(8,128)(2,1)S(1)} %all_to_all.21.block_ref), channel_id=1, source_target_pairs={{0,496},{8,504},{16,32},{24,40},{32,16},{40,24},{48,64},{56,72},{6... | collective-permute-start | bytes 786440 | tf_op jit(solution)/shard_map/ppermute | solution.py:182
  88.1 0.8 shard_map.64
  88.9 0.8 collective-permute-done.3.block_ref
  90.1 2.6 %collective-permute-done.4.block_ref = bf16[8,64,256]{2,1,0:T(8,128)(2,1)S(1)} collective-permute-done((bf16[8,64,256]{2,1,0:T(8,128)(2,1)S(1)}, bf16[8,64,256]{2,1,0:T(8,128)(2,1)S(1)}, u32[]{:S(2)}, u32[]{:S(2)}) %collective-permute-start.4) | collective-permute-done | bytes 262176 | tf_op jit(solution)/shard_map/ppermute | solution.py:182
  93.5 0.8 collective-permute-done.5.block_ref
  95.0 6.7 %all-gather.2 = f32[128,256]{1,0:T(8,128)S(1)} all-gather(f32[64,256]{1,0:T(8,128)S(1)} %get-tuple-element.39), channel_id=4, replica_groups=mesh['y_lo'=4,'z'=8,'core'=2,'x'=4,'y_hi'=2] {'core'}, dimensions={0}, use_global_device_ids=true | all-gather | bytes 196608 | tf_op jit(solution)/shard_map/all_gather | solution.py:227
  102.0 14.1 %all_to_all.22 = f32[32,4,128]{2,1,0:T(4,128)S(1)} all-to-all(f32[32,4,128]{2,1,0:T(4,128)S(1)} %broadcast_in_dim.13), channel_id=1, replica_groups=mesh['y_lo'=4,'z'=8,'core'=2,'x'=4,'y_hi'=2] {'x','y_hi','y_lo'}, dimensions={0} | all-to-all | bytes 131072 | tf_op jit(solution)/shard_map/all_to_all | solution.py:175
  116.2 12.8 %all_to_all.23 = f32[16,4,128]{2,1,0:T(4,128)S(1)} all-to-all(f32[16,4,128]{2,1,0:T(4,128)S(1)} %broadcast_in_dim.14), channel_id=1, replica_groups=mesh['y_lo'=4,'z'=8,'core'=2,'x'=4,'y_hi'=2] {'z','core'}, dimensions={0} | all-to-all | bytes 65536 | tf_op jit(solution)/shard_map/all_to_all | solution.py:175
  (25 shorter events, 3.7 us)
Async XLA Ops:
  27.2 33.5 %copy-start = (f32[64,256]{1,0:T(8,128)S(1)}, f32[64,256]{1,0:T(8,128)}, u32[]{:S(2)}) copy-start(f32[64,256]{1,0:T(8,128)} %first_ref.3) | copy-start | bytes 196612
  27.2 33.5 %copy-start.1 = (f32[256]{0:T(256)S(1)}, f32[256]{0:T(256)}, u32[]{:S(2)}) copy-start(f32[256]{0:T(256)} %param.6) | copy-start | bytes 3076
  27.2 21.2 %collective-permute-start = (bf16[8,96,256]{2,1,0:T(8,128)(2,1)S(1)}, bf16[8,96,256]{2,1,0:T(8,128)(2,1)S(1)}, u32[]{:S(2)}, u32[]{:S(2)}) collective-permute-start(bf16[8,96,256]{2,1,0:T(8,128)(2,1)S(1)} %slice.42), channel_id=1, source_target_pairs={{0,480},{8,40},{16,496},{24,56},{32,0},{40,72},{48,16},{56,88},{64... | collective-permute-start | bytes 1179656 | tf_op jit(solution)/shard_map/ppermute | solution.py:182
  33.1 16.6 %collective-permute-start.1 = (bf16[8,96,256]{2,1,0:T(8,128)(2,1)S(1)}, bf16[8,96,256]{2,1,0:T(8,128)(2,1)S(1)}, u32[]{:S(2)}, u32[]{:S(2)}) collective-permute-start(bf16[8,96,256]{2,1,0:T(8,128)(2,1)S(1)} %slice.42), channel_id=1, source_target_pairs={{0,16},{8,24},{16,0},{24,8},{32,48},{40,56},{48,32},{56,40},{64,80... | collective-permute-start | bytes 1179656 | tf_op jit(solution)/shard_map/ppermute | solution.py:182
  37.1 16.6 %collective-permute-start.2 = (bf16[8,96,256]{2,1,0:T(8,128)(2,1)S(1)}, bf16[8,96,256]{2,1,0:T(8,128)(2,1)S(1)}, u32[]{:S(2)}, u32[]{:S(2)}) collective-permute-start(bf16[8,96,256]{2,1,0:T(8,128)(2,1)S(1)} %slice.42), channel_id=1, source_target_pairs={{0,496},{8,504},{16,32},{24,40},{32,16},{40,24},{48,64},{56,72},{6... | collective-permute-start | bytes 1179656 | tf_op jit(solution)/shard_map/ppermute | solution.py:182
  75.5 14.2 %collective-permute-start.3 = (bf16[8,64,256]{2,1,0:T(8,128)(2,1)S(1)}, bf16[8,64,256]{2,1,0:T(8,128)(2,1)S(1)}, u32[]{:S(2)}, u32[]{:S(2)}) collective-permute-start(bf16[8,64,256]{2,1,0:T(8,128)(2,1)S(1)} %all_to_all.21.block_ref), channel_id=1, source_target_pairs={{0,480},{8,40},{16,496},{24,56},{32,0},{40,72},{48,16},{56,88},{64... | collective-permute-start | bytes 786440 | tf_op jit(solution)/shard_map/ppermute | solution.py:182
  77.7 15.1 %collective-permute-start.4 = (bf16[8,64,256]{2,1,0:T(8,128)(2,1)S(1)}, bf16[8,64,256]{2,1,0:T(8,128)(2,1)S(1)}, u32[]{:S(2)}, u32[]{:S(2)}) collective-permute-start(bf16[8,64,256]{2,1,0:T(8,128)(2,1)S(1)} %all_to_all.21.block_ref), channel_id=1, source_target_pairs={{0,16},{8,24},{16,0},{24,8},{32,48},{40,56},{48,32},{56,40},{64,80... | collective-permute-start | bytes 786440 | tf_op jit(solution)/shard_map/ppermute | solution.py:182
  82.0 12.2 %collective-permute-start.5 = (bf16[8,64,256]{2,1,0:T(8,128)(2,1)S(1)}, bf16[8,64,256]{2,1,0:T(8,128)(2,1)S(1)}, u32[]{:S(2)}, u32[]{:S(2)}) collective-permute-start(bf16[8,64,256]{2,1,0:T(8,128)(2,1)S(1)} %all_to_all.21.block_ref), channel_id=1, source_target_pairs={{0,496},{8,504},{16,32},{24,40},{32,16},{40,24},{48,64},{56,72},{6... | collective-permute-start | bytes 786440 | tf_op jit(solution)/shard_map/ppermute | solution.py:182

commit v7 on v6

--- a/solution.py
+++ b/solution.py
@@ -16,6 +16,8 @@
 
 LN2 = math.log(2.0)
 UNIT = math.sqrt(5.0) / LN2
+GRID = 2.0 / 1.5
+SPAN = UNIT / GRID
 SHIFT = 1.5 / LN2
 OFFSET = 0.75 / LN2**2
 LEVEL = math.log2(LN2**2 / 3.0) + SHIFT
@@ -25,16 +27,14 @@
 FEAT = 32
 RHS = 64
 WIDTH = 256
-ROUGH = 80
-DEPTH = 144
-TOLD = 96
+DEPTH = 80
 SHARDS = 8
 SIGMA = 0.5
 NT = (((1,), (1,)), ((), ()))
 
 
 def square_rows(coords, first, second):
-    squares = jnp.sum(coords * coords, axis=0, keepdims=True)
+    squares = jnp.sum(coords * coords, axis=0, keepdims=True) * SPAN**2
     one = squares.astype(BF16).astype(F32)
     two = (squares - one).astype(BF16).astype(F32)
     three = squares - one - two
@@ -42,23 +42,15 @@
     out = jnp.where((row >= second) & (row < second + 3), 1.0, 0.0)
     for at, piece in enumerate((one, two, three)):
         out = jnp.where(row == first + at, piece, out)
-    return out.astype(BF16)
+    return out
 
 
 def build_shard(weights, levels, shard, cols_ref, dist_ref, kernel_ref):
-    high = shard[:FEAT]
-    coords = high.astype(F32)
-    cols_ref[:FEAT] = high
-    cols_ref[FEAT : 2 * FEAT] = high
-    depth = ROUGH
-    if shard.shape[0] > TOLD:
-        low = shard[TOLD:]
-        coords = coords + low.astype(F32)
-        cols_ref[ROUGH : ROUGH + FEAT] = low
-        cols_ref[ROUGH + FEAT :] = low
-        depth = DEPTH
-    cols_ref[2 * FEAT : ROUGH] = square_rows(coords, 0, 3)
-    dist_ref[...] = jnp.dot(weights[:, :depth], cols_ref[:depth], preferred_element_type=F32)
+    coords = shard[:FEAT]
+    cols_ref[:FEAT] = coords
+    cols_ref[FEAT : 2 * FEAT] = coords
+    cols_ref[2 * FEAT :] = square_rows(coords.astype(F32), 0, 3).astype(BF16)
+    dist_ref[...] = jnp.dot(weights, cols_ref[...], preferred_element_type=F32)
     step = 64
     for half, level in enumerate(levels):
         for at in range(half * WIDTH, (half + 1) * WIDTH, step):
@@ -66,7 +58,7 @@
             moved = part * lax.rsqrt(part) + SHIFT
             entry = (moved * moved + OFFSET) * jnp.exp2(level - moved)
             kernel_ref[at : at + step] = entry.astype(BF16)
-    return lax.dot_general(shard[FEAT:TOLD], kernel_ref[...], NT, preferred_element_type=F32)
+    return lax.dot_general(shard[FEAT:], kernel_ref[...], NT, preferred_element_type=F32)
 
 
 def build_block(weights, levels, block_ref, cols_ref, dist_ref, kernel_ref):
@@ -81,12 +73,11 @@
     core = lax.axis_index("core")
     for at, ref in enumerate((both_ref.at[core], both_ref.at[1 - core])):
         rows = slice(at * WIDTH, (at + 1) * WIDTH)
-        high, low = ref[:FEAT].astype(F32), ref[FEAT:].astype(F32)
-        extra = square_rows(high + low, 3, 0).astype(F32)
-        halves = jnp.transpose(jnp.concatenate([-2.0 * high, -2.0 * low], axis=0)).astype(BF16)
-        weights_ref[rows, : 2 * FEAT] = halves
-        weights_ref[rows, 2 * FEAT : ROUGH] = jnp.transpose(extra).astype(BF16)
-        weights_ref[rows, ROUGH:] = halves
+        coords = ref[...]
+        scaled = coords * (-2.0 * SPAN**2)
+        high = scaled.astype(BF16).astype(F32)
+        stacked = jnp.concatenate([high, scaled - high, square_rows(coords, 3, 0)], axis=0)
+        weights_ref[rows] = jnp.transpose(stacked).astype(BF16)
     total = build_block(weights_ref[...], LEVELS[:2], block_ref, cols_ref, dist_ref, kernel_ref)
     own_ref[...] = total[:, :WIDTH]
     peer_ref[...] = total[:, WIDTH:]
@@ -191,13 +182,10 @@
 
 
 def body(points, lengthscale, noise_var, targets):
-    coords = points / lengthscale[:, None] * UNIT
-    high = lax.reduce_precision(coords, 8, 7)
-    message = jnp.concatenate([high, targets, coords - high], axis=0).astype(BF16)
-    coords = jnp.concatenate([message[:FEAT], message[TOLD:]], axis=0)
+    coords = points / lengthscale[:, None] * GRID
     both = lax.all_gather(coords, "core")
-    block = gathered(message, ("x", "y_hi"))
-    far, *pairs = halo(block[:, :TOLD])
+    block = gathered(jnp.concatenate([coords, targets], axis=0).astype(BF16), ("x", "y_hi"))
+    far, *pairs = halo(block)
 
     half = shape(RHS, WIDTH)
     weights, own, peer, kernel_own = call(

time: 130 us -> 128 us (0.985)
  blocking collectives: 82.8 us -> 76.5 us
  waiting for transfers between devices: 5.64 us -> 7.87 us
  starting transfers between devices: 25.7 us -> 27.4 us
    all_to_all x4, blocking collectives: 66.5 us -> 60.9 us  [gathered(): lax.all_to_all(jnp.broadcast_to(value[None], (count,) + value.shape), axe...]
    ppermute x6, waiting for transfers between devices: 5.64 us -> 7.87 us  [halo(): lax.ppermute(block, BLK, route)]
    ppermute x6, starting transfers between devices: 25.7 us -> 27.4 us  [halo(): lax.ppermute(block, BLK, route)]
where the time goes in v7:
time: 128 us
  blocking collectives  76.5 us (60%)
  starting transfers between devices  27.4 us (21%)
  Pallas kernels  12.1 us (9%)
  waiting for transfers between devices  7.87 us (6%)
  other arithmetic  2.76 us (2%)
    all_to_all x4, blocking collectives, gathered(): lax.all_to_all(jnp.broadcast_to(value[None], (count,) + value.shape), axe...  60.9 us
    ppermute x6, starting transfers between devices, halo(): lax.ppermute(block, BLK, route)  27.4 us
    all_gather x2, blocking collectives, body(): both = lax.all_gather(peer, 'core')  10.8 us
    ppermute x6, waiting for transfers between devices, halo(): lax.ppermute(block, BLK, route)  7.87 us
    pallas_call x2, Pallas kernels, body(): call(functools.partial(build_pair, second), (half, half, kernel_shape()),...  5.01 us
    all_gather x1, blocking collectives, body(): both = lax.all_gather(coords, 'core')  4.86 us
    pallas_call x1, Pallas kernels, body(): call(build_first, (shape(2 * WIDTH, DEPTH, dtype=BF16), half, half, kerne...  2.6 us
  transfers between devices with their start and end apart: 6, of which 4 were waited for; matrix products, arithmetic and copies ran while one was open for 0% of the time, Pallas kernels for 7%

profile of v7, /device:TPU:1, one launch (start us, length us, event | category | flops | bytes accessed | tf_op | source)
XLA Modules:
  0.0 127.5 jit_solution(8318954817893242217)
XLA Ops:
  0.6 0.9 convert.7
  1.5 0.8 fusion.11
  2.4 21.8 %all_to_all.20.block_ref = bf16[8,96,256]{2,1,0:T(8,128)(2,1)S(1)} all-to-all(bf16[8,96,256]{2,1,0:T(8,128)(2,1)S(1)} %broadcast_in_dim.10), channel_id=1, replica_groups=mesh['y_lo'=4,'z'=8,'core'=2,'x'=4,'y_hi'=2] {'x','y_hi'}, dimensions={0} | all-to-all | bytes 786432 | tf_op jit(solution)/shard_map/all_to_all | solution.py:166
  24.2 5.8 %collective-permute-start = (bf16[8,96,256]{2,1,0:T(8,128)(2,1)S(1)}, bf16[8,96,256]{2,1,0:T(8,128)(2,1)S(1)}, u32[]{:S(2)}, u32[]{:S(2)}) collective-permute-start(bf16[8,96,256]{2,1,0:T(8,128)(2,1)S(1)} %all_to_all.20.block_ref), channel_id=1, source_target_pairs={{0,480},{8,40},{16,496},{24,56},{32,0},{40,72},{48,16},{56,88},{64... | collective-permute-start | bytes 1179656 | tf_op jit(solution)/shard_map/ppermute | solution.py:173
  30.0 4.0 %collective-permute-start.1 = (bf16[8,96,256]{2,1,0:T(8,128)(2,1)S(1)}, bf16[8,96,256]{2,1,0:T(8,128)(2,1)S(1)}, u32[]{:S(2)}, u32[]{:S(2)}) collective-permute-start(bf16[8,96,256]{2,1,0:T(8,128)(2,1)S(1)} %all_to_all.20.block_ref), channel_id=1, source_target_pairs={{0,16},{8,24},{16,0},{24,8},{32,48},{40,56},{48,32},{56,40},{64,80... | collective-permute-start | bytes 1179656 | tf_op jit(solution)/shard_map/ppermute | solution.py:173
  34.0 5.3 %collective-permute-start.2 = (bf16[8,96,256]{2,1,0:T(8,128)(2,1)S(1)}, bf16[8,96,256]{2,1,0:T(8,128)(2,1)S(1)}, u32[]{:S(2)}, u32[]{:S(2)}) collective-permute-start(bf16[8,96,256]{2,1,0:T(8,128)(2,1)S(1)} %all_to_all.20.block_ref), channel_id=1, source_target_pairs={{0,496},{8,504},{16,32},{24,40},{32,16},{40,24},{48,64},{56,72},{6... | collective-permute-start | bytes 1179656 | tf_op jit(solution)/shard_map/ppermute | solution.py:173
  39.4 4.9 %all-gather = f32[64,256]{1,0:T(8,128)S(1)} all-gather(f32[32,256]{1,0:T(8,128)S(1)} %get-tuple-element.50), channel_id=2, replica_groups=mesh['y_lo'=4,'z'=8,'core'=2,'x'=4,'y_hi'=2] {'core'}, dimensions={0}, use_global_device_ids=true | all-gather | bytes 98304 | tf_op jit(solution)/shard_map/all_gather | solution.py:186
  44.2 2.6 %shard_map.59 = (bf16[512,80]{1,0:T(8,128)(2,1)S(1)}, f32[64,256]{1,0:T(8,128)S(1)}, f32[64,256]{1,0:T(8,128)S(1)}, bf16[8,512,256]{2,1,0:T(8,128)(2,1)S(1)}) custom-call(f32[2,32,256]{2,1,0:T(8,128)S(1)} %bitcast.52, bf16[8,96,256]{2,1,0:T(8,128)(2,1)S(1)} %all_to_all.20.block_ref), custom_call_target="tpu_custom_call" | custom-call | tf_op jit(solution)/shard_map/pallas_call | solution.py:191
  46.8 1.2 shard_map.60
  48.0 2.5 %shard_map.61 = (f32[64,256]{1,0:T(8,128)S(1)}, f32[64,256]{1,0:T(8,128)S(1)}, bf16[8,512,256]{2,1,0:T(8,128)(2,1)S(1)}) custom-call(bf16[512,80]{1,0:T(8,128)(2,1)S(1)} %get-tuple-element.22.weights_ref, f32[64,256]{1,0:T(8,128)S(1)} %get-tuple-element.23.own_before, f32[64,256]{1,0:T(8,128)S(1)} %get-tuple-element.25.peer_before, ...), custom_call_target="tpu_custom_call" | custom-call | tf_op jit(solution)/shard_map/pallas_call | solution.py:199
  50.5 1.8 %collective-permute-done.2.block_ref = bf16[8,96,256]{2,1,0:T(8,128)(2,1)S(1)} collective-permute-done((bf16[8,96,256]{2,1,0:T(8,128)(2,1)S(1)}, bf16[8,96,256]{2,1,0:T(8,128)(2,1)S(1)}, u32[]{:S(2)}, u32[]{:S(2)}) %collective-permute-start.2) | collective-permute-done | bytes 393248 | tf_op jit(solution)/shard_map/ppermute | solution.py:173
  52.4 2.5 %shard_map.62 = (f32[64,256]{1,0:T(8,128)S(1)}, f32[64,256]{1,0:T(8,128)S(1)}, bf16[8,512,256]{2,1,0:T(8,128)(2,1)S(1)}) custom-call(bf16[512,80]{1,0:T(8,128)(2,1)S(1)} %get-tuple-element.22.weights_ref, f32[64,256]{1,0:T(8,128)S(1)} %get-tuple-element.26.own_before, f32[64,256]{1,0:T(8,128)S(1)} %get-tuple-element.27.peer_before, ...), custom_call_target="tpu_custom_call" | custom-call | tf_op jit(solution)/shard_map/pallas_call | solution.py:199
  54.9 4.3 %all-gather.1 = f32[128,256]{1,0:T(8,128)S(1)} all-gather(f32[64,256]{1,0:T(8,128)S(1)} %get-tuple-element.29), channel_id=3, replica_groups=mesh['y_lo'=4,'z'=8,'core'=2,'x'=4,'y_hi'=2] {'core'}, dimensions={0}, use_global_device_ids=true | all-gather | bytes 196608 | tf_op jit(solution)/shard_map/all_gather | solution.py:205
  59.2 13.5 %all_to_all.21.block_ref = bf16[8,64,256]{2,1,0:T(8,128)(2,1)S(1)} all-to-all(bf16[8,64,256]{2,1,0:T(8,128)(2,1)S(1)} %broadcast_in_dim.12), channel_id=1, replica_groups=mesh['y_lo'=4,'z'=8,'core'=2,'x'=4,'y_hi'=2] {'x','y_hi'}, dimensions={0} | all-to-all | bytes 524288 | tf_op jit(solution)/shard_map/all_to_all | solution.py:166
  72.7 3.8 %collective-permute-start.3 = (bf16[8,64,256]{2,1,0:T(8,128)(2,1)S(1)}, bf16[8,64,256]{2,1,0:T(8,128)(2,1)S(1)}, u32[]{:S(2)}, u32[]{:S(2)}) collective-permute-start(bf16[8,64,256]{2,1,0:T(8,128)(2,1)S(1)} %all_to_all.21.block_ref), channel_id=1, source_target_pairs={{0,480},{8,40},{16,496},{24,56},{32,0},{40,72},{48,16},{56,88},{64... | collective-permute-start | bytes 786440 | tf_op jit(solution)/shard_map/ppermute | solution.py:173
  76.5 2.6 %collective-permute-start.4 = (bf16[8,64,256]{2,1,0:T(8,128)(2,1)S(1)}, bf16[8,64,256]{2,1,0:T(8,128)(2,1)S(1)}, u32[]{:S(2)}, u32[]{:S(2)}) collective-permute-start(bf16[8,64,256]{2,1,0:T(8,128)(2,1)S(1)} %all_to_all.21.block_ref), channel_id=1, source_target_pairs={{0,16},{8,24},{16,0},{24,8},{32,48},{40,56},{48,32},{56,40},{64,80... | collective-permute-start | bytes 786440 | tf_op jit(solution)/shard_map/ppermute | solution.py:173
  79.1 5.9 %collective-permute-start.5 = (bf16[8,64,256]{2,1,0:T(8,128)(2,1)S(1)}, bf16[8,64,256]{2,1,0:T(8,128)(2,1)S(1)}, u32[]{:S(2)}, u32[]{:S(2)}) collective-permute-start(bf16[8,64,256]{2,1,0:T(8,128)(2,1)S(1)} %all_to_all.21.block_ref), channel_id=1, source_target_pairs={{0,496},{8,504},{16,32},{24,40},{32,16},{40,24},{48,64},{56,72},{6... | collective-permute-start | bytes 786440 | tf_op jit(solution)/shard_map/ppermute | solution.py:173
  85.3 0.8 shard_map.64
  86.1 0.9 collective-permute-done.3.block_ref
  87.5 2.3 %collective-permute-done.4.block_ref = bf16[8,64,256]{2,1,0:T(8,128)(2,1)S(1)} collective-permute-done((bf16[8,64,256]{2,1,0:T(8,128)(2,1)S(1)}, bf16[8,64,256]{2,1,0:T(8,128)(2,1)S(1)}, u32[]{:S(2)}, u32[]{:S(2)}) %collective-permute-start.4) | collective-permute-done | bytes 262176 | tf_op jit(solution)/shard_map/ppermute | solution.py:173
  90.6 2.8 %collective-permute-done.5.block_ref = bf16[8,64,256]{2,1,0:T(8,128)(2,1)S(1)} collective-permute-done((bf16[8,64,256]{2,1,0:T(8,128)(2,1)S(1)}, bf16[8,64,256]{2,1,0:T(8,128)(2,1)S(1)}, u32[]{:S(2)}, u32[]{:S(2)}) %collective-permute-start.5) | collective-permute-done | bytes 262176 | tf_op jit(solution)/shard_map/ppermute | solution.py:173
  94.1 6.4 %all-gather.2 = f32[128,256]{1,0:T(8,128)S(1)} all-gather(f32[64,256]{1,0:T(8,128)S(1)} %get-tuple-element.39), channel_id=4, replica_groups=mesh['y_lo'=4,'z'=8,'core'=2,'x'=4,'y_hi'=2] {'core'}, dimensions={0}, use_global_device_ids=true | all-gather | bytes 196608 | tf_op jit(solution)/shard_map/all_gather | solution.py:215
  100.8 14.0 %all_to_all.22 = f32[32,4,128]{2,1,0:T(4,128)S(1)} all-to-all(f32[32,4,128]{2,1,0:T(4,128)S(1)} %broadcast_in_dim.13), channel_id=1, replica_groups=mesh['y_lo'=4,'z'=8,'core'=2,'x'=4,'y_hi'=2] {'x','y_hi','y_lo'}, dimensions={0} | all-to-all | bytes 131072 | tf_op jit(solution)/shard_map/all_to_all | solution.py:166
  114.9 11.7 %all_to_all.23 = f32[16,4,128]{2,1,0:T(4,128)S(1)} all-to-all(f32[16,4,128]{2,1,0:T(4,128)S(1)} %broadcast_in_dim.14), channel_id=1, replica_groups=mesh['y_lo'=4,'z'=8,'core'=2,'x'=4,'y_hi'=2] {'z','core'}, dimensions={0} | all-to-all | bytes 65536 | tf_op jit(solution)/shard_map/all_to_all | solution.py:166
  (23 shorter events, 3.6 us)
Async XLA Ops:
  0.6 58.6 %copy-start = (f32[64,256]{1,0:T(8,128)S(1)}, f32[64,256]{1,0:T(8,128)}, u32[]{:S(2)}) copy-start(f32[64,256]{1,0:T(8,128)} %first_ref.3) | copy-start | bytes 196612
  0.6 58.6 %copy-start.1 = (f32[256]{0:T(256)S(1)}, f32[256]{0:T(256)}, u32[]{:S(2)}) copy-start(f32[256]{0:T(256)} %param.6) | copy-start | bytes 3076
  24.2 22.6 %collective-permute-start = (bf16[8,96,256]{2,1,0:T(8,128)(2,1)S(1)}, bf16[8,96,256]{2,1,0:T(8,128)(2,1)S(1)}, u32[]{:S(2)}, u32[]{:S(2)}) collective-permute-start(bf16[8,96,256]{2,1,0:T(8,128)(2,1)S(1)} %all_to_all.20.block_ref), channel_id=1, source_target_pairs={{0,480},{8,40},{16,496},{24,56},{32,0},{40,72},{48,16},{56,88},{64... | collective-permute-start | bytes 1179656 | tf_op jit(solution)/shard_map/ppermute | solution.py:173
  30.0 18.0 %collective-permute-start.1 = (bf16[8,96,256]{2,1,0:T(8,128)(2,1)S(1)}, bf16[8,96,256]{2,1,0:T(8,128)(2,1)S(1)}, u32[]{:S(2)}, u32[]{:S(2)}) collective-permute-start(bf16[8,96,256]{2,1,0:T(8,128)(2,1)S(1)} %all_to_all.20.block_ref), channel_id=1, source_target_pairs={{0,16},{8,24},{16,0},{24,8},{32,48},{40,56},{48,32},{56,40},{64,80... | collective-permute-start | bytes 1179656 | tf_op jit(solution)/shard_map/ppermute | solution.py:173
  34.0 18.3 %collective-permute-start.2 = (bf16[8,96,256]{2,1,0:T(8,128)(2,1)S(1)}, bf16[8,96,256]{2,1,0:T(8,128)(2,1)S(1)}, u32[]{:S(2)}, u32[]{:S(2)}) collective-permute-start(bf16[8,96,256]{2,1,0:T(8,128)(2,1)S(1)} %all_to_all.20.block_ref), channel_id=1, source_target_pairs={{0,496},{8,504},{16,32},{24,40},{32,16},{40,24},{48,64},{56,72},{6... | collective-permute-start | bytes 1179656 | tf_op jit(solution)/shard_map/ppermute | solution.py:173
  72.7 14.3 %collective-permute-start.3 = (bf16[8,64,256]{2,1,0:T(8,128)(2,1)S(1)}, bf16[8,64,256]{2,1,0:T(8,128)(2,1)S(1)}, u32[]{:S(2)}, u32[]{:S(2)}) collective-permute-start(bf16[8,64,256]{2,1,0:T(8,128)(2,1)S(1)} %all_to_all.21.block_ref), channel_id=1, source_target_pairs={{0,480},{8,40},{16,496},{24,56},{32,0},{40,72},{48,16},{56,88},{64... | collective-permute-start | bytes 786440 | tf_op jit(solution)/shard_map/ppermute | solution.py:173
  76.5 13.3 %collective-permute-start.4 = (bf16[8,64,256]{2,1,0:T(8,128)(2,1)S(1)}, bf16[8,64,256]{2,1,0:T(8,128)(2,1)S(1)}, u32[]{:S(2)}, u32[]{:S(2)}) collective-permute-start(bf16[8,64,256]{2,1,0:T(8,128)(2,1)S(1)} %all_to_all.21.block_ref), channel_id=1, source_target_pairs={{0,16},{8,24},{16,0},{24,8},{32,48},{40,56},{48,32},{56,40},{64,80... | collective-permute-start | bytes 786440 | tf_op jit(solution)/shard_map/ppermute | solution.py:173
  79.1 14.2 %collective-permute-start.5 = (bf16[8,64,256]{2,1,0:T(8,128)(2,1)S(1)}, bf16[8,64,256]{2,1,0:T(8,128)(2,1)S(1)}, u32[]{:S(2)}, u32[]{:S(2)}) collective-permute-start(bf16[8,64,256]{2,1,0:T(8,128)(2,1)S(1)} %all_to_all.21.block_ref), channel_id=1, source_target_pairs={{0,496},{8,504},{16,32},{24,40},{32,16},{40,24},{48,64},{56,72},{6... | collective-permute-start | bytes 786440 | tf_op jit(solution)/shard_map/ppermute | solution.py:173

commit v8 on v7

--- a/solution.py
+++ b/solution.py
@@ -69,11 +69,14 @@
     return total
 
 
-def build_first(both_ref, block_ref, weights_ref, own_ref, peer_ref, kernel_ref, cols_ref, dist_ref):
+def build_first(scale_ref, both_ref, block_ref, weights_ref, own_ref, peer_ref, kernel_ref, cols_ref, dist_ref):
     core = lax.axis_index("core")
+    row = lax.broadcasted_iota(jnp.int32, (FEAT, FEAT), 0)
+    column = lax.broadcasted_iota(jnp.int32, (FEAT, FEAT), 1)
+    scale = jnp.sum(jnp.where(row == column, scale_ref[:, :FEAT], 0.0), axis=1, keepdims=True)
     for at, ref in enumerate((both_ref.at[core], both_ref.at[1 - core])):
         rows = slice(at * WIDTH, (at + 1) * WIDTH)
-        coords = ref[...]
+        coords = ref[...] * scale
         scaled = coords * (-2.0 * SPAN**2)
         high = scaled.astype(BF16).astype(F32)
         stacked = jnp.concatenate([high, scaled - high, square_rows(coords, 3, 0)], axis=0)
@@ -138,15 +141,15 @@
 
 
 def late_sums(
-    early_ref, noise_ref, first_ref, first_total_ref, image_ref, own_ref, both_ref, second_ref, sums_ref
+    early_ref, noise_ref, images_ref, first_ref, image_ref, first_total_ref, own_ref, peer_ref, sums_ref
 ):
-    first, image = first_ref[...], image_ref[...]
-    total = own_ref[...] + both_ref[1 - lax.axis_index("core")]
-    second = noise_ref[...] * image + (first_total_ref[...] - total) * (1.0 / SIGMA)
-    second_ref[...] = second
+    core = lax.axis_index("core")
+    image = image_ref[...]
+    known = noise_ref[...] * image + (first_total_ref[...] - own_ref[...]) * (1.0 / SIGMA)
+    lent = peer_ref[...] * (1.0 / SIGMA)
     sums_ref[0:2] = early_ref[...]
-    sums_ref[2:3, :RHS] = row_sum(first * second)
-    sums_ref[2:3, RHS:] = row_sum(image * second)
+    sums_ref[2:3, :RHS] = row_sum(first_ref[...] * known - images_ref[1 - core, :RHS] * lent)
+    sums_ref[2:3, RHS:] = row_sum(image * known - images_ref[1 - core, RHS:] * lent)
     sums_ref[3:4] = jnp.zeros((1, 2 * RHS), F32)
 
 
@@ -182,9 +185,10 @@
 
 
 def body(points, lengthscale, noise_var, targets):
-    coords = points / lengthscale[:, None] * GRID
-    both = lax.all_gather(coords, "core")
-    block = gathered(jnp.concatenate([coords, targets], axis=0).astype(BF16), ("x", "y_hi"))
+    scale = GRID / jnp.pad(lengthscale, (0, RHS), constant_values=GRID)
+    exact = jnp.concatenate([points, targets], axis=0) * scale[:, None]
+    block = gathered(exact.astype(BF16), ("x", "y_hi"))
+    both = lax.all_gather(points, "core")
     far, *pairs = halo(block)
 
     half = shape(RHS, WIDTH)
@@ -192,30 +196,39 @@
         build_first,
         (shape(2 * WIDTH, DEPTH, dtype=BF16), half, half, kernel_shape()),
         scratch_shapes=scratch(),
-    )(both, block)
-    peer, kernel_far = call(build_far, (half, kernel_shape(WIDTH)), scratch_shapes=scratch(WIDTH))(weights, peer, far)
-    kernels = []
-    for second, moved in enumerate(pairs):
-        own, peer, made = call(
-            functools.partial(build_pair, second), (half, half, kernel_shape()), scratch_shapes=scratch()
-        )(weights, own, peer, moved)
-        kernels.append(made)
+    )(scale[None], both, block)
+    kernels = {}
+    for kind in "ABF":
+        if kind == "F":
+            peer, kernels[kind] = call(build_far, (half, kernel_shape(WIDTH)), scratch_shapes=scratch(WIDTH))(
+                weights, peer, far
+            )
+        else:
+            second = "AB".index(kind)
+            own, peer, kernels[kind] = call(
+                functools.partial(build_pair, second), (half, half, kernel_shape()), scratch_shapes=scratch()
+            )(weights, own, peer, pairs[second])
 
     noise = noise_var[None, :]
-    both = lax.all_gather(peer, "core")
-    first_total = own + jnp.where(lax.axis_index("core") == 0, both[1], both[0])
+    even = lax.axis_index("core") == 0
+    lent = lax.all_gather(peer, "core")
+    first_total = own + jnp.where(even, lent[1], lent[0])
     image = noise * targets + first_total
     block = gathered((targets - SIGMA * image).astype(BF16), ("x", "y_hi"))
+    images = lax.all_gather(jnp.concatenate([targets, image], axis=0), "core")
     far, *pairs = halo(block)
     early = call(early_sums, shape(2, 2 * RHS))(targets, image)
     own, peer = call(apply_first, (half, half))(kernel_own, block)
-    peer = call(apply_far, half)(kernel_far, peer, far)
-    for made, moved in zip(kernels, pairs):
-        own, peer = call(apply_pair, (half, half))(made, own, peer, moved)
-    both = lax.all_gather(peer, "core")
-    second, sums = call(late_sums, (half, shape(4, 2 * RHS)))(
-        early, noise, targets, first_total, image, own, both
+    for kind in "FAB":
+        if kind == "F":
+            peer = call(apply_far, half)(kernels[kind], peer, far)
+        else:
+            own, peer = call(apply_pair, (half, half))(kernels[kind], own, peer, pairs["AB".index(kind)])
+    sums = call(late_sums, shape(4, 2 * RHS))(
+        early, noise, images, targets, image, first_total, own, peer
     )
+    lent = lax.all_gather(peer, "core")
+    second = noise * image + (first_total - own - jnp.where(even, lent[1], lent[0])) * (1.0 / SIGMA)
     for axes in (("x", "y_hi", "y_lo"), ("z", "core")):
         sums = jnp.sum(gathered(sums, axes), axis=0)
 

time: 128 us -> 125 us (0.977)
  blocking collectives: 76.5 us -> 65.6 us
  starting transfers between devices: 27.4 us -> 33.6 us
    all_to_all x4 -> x3, blocking collectives: 60.9 us -> 52.9 us  [gathered(): lax.all_to_all(jnp.broadcast_to(value[None], (count,) + value.shape), axe...]
    all_to_all x0 -> x1, starting transfers between devices: none -> 6.22 us  [gathered(): lax.all_to_all(jnp.broadcast_to(value[None], (count,) + value.shape), axe...]
    all_to_all x0 -> x1, waiting for transfers between devices: none -> 5.5 us  [gathered(): lax.all_to_all(jnp.broadcast_to(value[None], (count,) + value.shape), axe...]
    ppermute x6, waiting for transfers between devices: 7.87 us -> 3.16 us  [halo(): lax.ppermute(block, BLK, route)]
    all_gather x3 -> x4, blocking collectives: 15.6 us -> 12.6 us  [the longest x1 5.07 us: body(): both = lax.all_gather(points, 'core')]
    another operation x2 -> x0, other arithmetic: 1.74 us -> none
  transfers between devices with their start and end apart: 6 -> 7, of which waited for: 4 -> 3; matrix products, arithmetic and copies ran while one was open for 0% -> 1% of each run, Pallas kernels for 7% -> 8%
where the time goes in v8:
time: 125 us
  blocking collectives  65.6 us (52%)
  starting transfers between devices  33.6 us (27%)
  Pallas kernels  12.1 us (10%)
  waiting for transfers between devices  8.66 us (7%)
  other arithmetic  3.34 us (3%)
    all_to_all x3, blocking collectives, gathered(): lax.all_to_all(jnp.broadcast_to(value[None], (count,) + value.shape), axe...  52.9 us
    ppermute x6, starting transfers between devices, halo(): lax.ppermute(block, BLK, route)  27.4 us
    all_to_all x1, starting transfers between devices, gathered(): lax.all_to_all(jnp.broadcast_to(value[None], (count,) + value.shape), axe...  6.22 us
    all_to_all x1, waiting for transfers between devices, gathered(): lax.all_to_all(jnp.broadcast_to(value[None], (count,) + value.shape), axe...  5.5 us
    all_gather x1, blocking collectives, body(): both = lax.all_gather(points, 'core')  5.07 us
    pallas_call x2, Pallas kernels, body(): call(functools.partial(build_pair, second), (half, half, kernel_shape()),...  5.01 us
    all_gather x2, blocking collectives, body(): lent = lax.all_gather(peer, 'core')  4.61 us
    ppermute x6, waiting for transfers between devices, halo(): lax.ppermute(block, BLK, route)  3.16 us
  transfers between devices with their start and end apart: 7, of which 3 were waited for; matrix products, arithmetic and copies ran while one was open for 1% of the time, Pallas kernels for 8%

profile of v8, /device:TPU:1, one launch (start us, length us, event | category | flops | bytes accessed | tf_op | source)
XLA Modules:
  0.0 124.8 jit_solution(6630181265568892165)
XLA Ops:
  1.3 0.9 fusion
  2.3 21.8 %all_to_all.20.block_ref = bf16[8,96,256]{2,1,0:T(8,128)(2,1)S(1)} all-to-all(bf16[8,96,256]{2,1,0:T(8,128)(2,1)S(1)} %broadcast_in_dim.13), channel_id=1, replica_groups=mesh['y_lo'=4,'z'=8,'core'=2,'x'=4,'y_hi'=2] {'x','y_hi'}, dimensions={0} | all-to-all | bytes 786432 | tf_op jit(solution)/shard_map/all_to_all | solution.py:169
  24.1 4.0 %collective-permute-start = (bf16[8,96,256]{2,1,0:T(8,128)(2,1)S(1)}, bf16[8,96,256]{2,1,0:T(8,128)(2,1)S(1)}, u32[]{:S(2)}, u32[]{:S(2)}) collective-permute-start(bf16[8,96,256]{2,1,0:T(8,128)(2,1)S(1)} %all_to_all.20.block_ref), channel_id=1, source_target_pairs={{0,16},{8,24},{16,0},{24,8},{32,48},{40,56},{48,32},{56,40},{64,80... | collective-permute-start | bytes 1179656 | tf_op jit(solution)/shard_map/ppermute | solution.py:176
  28.1 9.2 %collective-permute-start.1 = (bf16[8,96,256]{2,1,0:T(8,128)(2,1)S(1)}, bf16[8,96,256]{2,1,0:T(8,128)(2,1)S(1)}, u32[]{:S(2)}, u32[]{:S(2)}) collective-permute-start(bf16[8,96,256]{2,1,0:T(8,128)(2,1)S(1)} %all_to_all.20.block_ref), channel_id=1, source_target_pairs={{0,496},{8,504},{16,32},{24,40},{32,16},{40,24},{48,64},{56,72},{6... | collective-permute-start | bytes 1179656 | tf_op jit(solution)/shard_map/ppermute | solution.py:176
  37.3 1.9 %collective-permute-start.2 = (bf16[8,96,256]{2,1,0:T(8,128)(2,1)S(1)}, bf16[8,96,256]{2,1,0:T(8,128)(2,1)S(1)}, u32[]{:S(2)}, u32[]{:S(2)}) collective-permute-start(bf16[8,96,256]{2,1,0:T(8,128)(2,1)S(1)} %all_to_all.20.block_ref), channel_id=1, source_target_pairs={{0,480},{8,40},{16,496},{24,56},{32,0},{40,72},{48,16},{56,88},{64... | collective-permute-start | bytes 1179656 | tf_op jit(solution)/shard_map/ppermute | solution.py:176
  39.2 5.1 %all-gather = f32[64,256]{1,0:T(8,128)S(1)} all-gather(f32[32,256]{1,0:T(8,128)} %param.4), channel_id=2, replica_groups=mesh['y_lo'=4,'z'=8,'core'=2,'x'=4,'y_hi'=2] {'core'}, dimensions={0}, use_global_device_ids=true | all-gather | bytes 98304 | tf_op jit(solution)/shard_map/all_gather | solution.py:191
  45.0 2.7 %shard_map.59 = (bf16[512,80]{1,0:T(8,128)(2,1)S(1)}, f32[64,256]{1,0:T(8,128)S(1)}, f32[64,256]{1,0:T(8,128)S(1)}, bf16[8,512,256]{2,1,0:T(8,128)(2,1)S(1)}) custom-call(f32[1,96]{1,0:T(1,128)S(1)} %fusion.17.scale_ref, f32[2,32,256]{2,1,0:T(8,128)S(1)} %bitcast.54, bf16[8,96,256]{2,1,0:T(8,128)(2,1)S(1)} %all_to_all.20.block_ref), custom_call_target="tpu_custom_call" | custom-call | tf_op jit(solution)/shard_map/pallas_call | solution.py:195
  47.7 2.5 %shard_map.60 = (f32[64,256]{1,0:T(8,128)S(1)}, f32[64,256]{1,0:T(8,128)S(1)}, bf16[8,512,256]{2,1,0:T(8,128)(2,1)S(1)}) custom-call(bf16[512,80]{1,0:T(8,128)(2,1)S(1)} %get-tuple-element.20.weights_ref, f32[64,256]{1,0:T(8,128)S(1)} %get-tuple-element.21.own_before, f32[64,256]{1,0:T(8,128)S(1)} %get-tuple-element.22.peer_before, ...), custom_call_target="tpu_custom_call" | custom-call | tf_op jit(solution)/shard_map/pallas_call | solution.py:208
  50.2 2.5 %shard_map.61 = (f32[64,256]{1,0:T(8,128)S(1)}, f32[64,256]{1,0:T(8,128)S(1)}, bf16[8,512,256]{2,1,0:T(8,128)(2,1)S(1)}) custom-call(bf16[512,80]{1,0:T(8,128)(2,1)S(1)} %get-tuple-element.20.weights_ref, f32[64,256]{1,0:T(8,128)S(1)} %get-tuple-element.23.own_before, f32[64,256]{1,0:T(8,128)S(1)} %get-tuple-element.24.peer_before, ...), custom_call_target="tpu_custom_call" | custom-call | tf_op jit(solution)/shard_map/pallas_call | solution.py:208
  52.7 1.9 %collective-permute-done.2.block_ref = bf16[8,96,256]{2,1,0:T(8,128)(2,1)S(1)} collective-permute-done((bf16[8,96,256]{2,1,0:T(8,128)(2,1)S(1)}, bf16[8,96,256]{2,1,0:T(8,128)(2,1)S(1)}, u32[]{:S(2)}, u32[]{:S(2)}) %collective-permute-start.2) | collective-permute-done | bytes 393248 | tf_op jit(solution)/shard_map/ppermute | solution.py:176
  54.6 1.2 shard_map.62
  55.8 2.7 %all-gather.1 = f32[128,256]{1,0:T(8,128)S(1)} all-gather(f32[64,256]{1,0:T(8,128)S(1)} %get-tuple-element.27), channel_id=3, replica_groups=mesh['y_lo'=4,'z'=8,'core'=2,'x'=4,'y_hi'=2] {'core'}, dimensions={0}, use_global_device_ids=true | all-gather | bytes 196608 | tf_op jit(solution)/shard_map/all_gather | solution.py:214
  58.6 13.8 %all_to_all.21.block_ref = bf16[8,64,256]{2,1,0:T(8,128)(2,1)S(1)} all-to-all(bf16[8,64,256]{2,1,0:T(8,128)(2,1)S(1)} %broadcast_in_dim.15), channel_id=1, replica_groups=mesh['y_lo'=4,'z'=8,'core'=2,'x'=4,'y_hi'=2] {'x','y_hi'}, dimensions={0} | all-to-all | bytes 524288 | tf_op jit(solution)/shard_map/all_to_all | solution.py:169
  72.4 2.3 %collective-permute-start.3 = (bf16[8,64,256]{2,1,0:T(8,128)(2,1)S(1)}, bf16[8,64,256]{2,1,0:T(8,128)(2,1)S(1)}, u32[]{:S(2)}, u32[]{:S(2)}) collective-permute-start(bf16[8,64,256]{2,1,0:T(8,128)(2,1)S(1)} %all_to_all.21.block_ref), channel_id=1, source_target_pairs={{0,480},{8,40},{16,496},{24,56},{32,0},{40,72},{48,16},{56,88},{64... | collective-permute-start | bytes 786440 | tf_op jit(solution)/shard_map/ppermute | solution.py:176
  74.7 3.1 %collective-permute-start.4 = (bf16[8,64,256]{2,1,0:T(8,128)(2,1)S(1)}, bf16[8,64,256]{2,1,0:T(8,128)(2,1)S(1)}, u32[]{:S(2)}, u32[]{:S(2)}) collective-permute-start(bf16[8,64,256]{2,1,0:T(8,128)(2,1)S(1)} %all_to_all.21.block_ref), channel_id=1, source_target_pairs={{0,16},{8,24},{16,0},{24,8},{32,48},{40,56},{48,32},{56,40},{64,80... | collective-permute-start | bytes 786440 | tf_op jit(solution)/shard_map/ppermute | solution.py:176
  77.8 6.8 %collective-permute-start.5 = (bf16[8,64,256]{2,1,0:T(8,128)(2,1)S(1)}, bf16[8,64,256]{2,1,0:T(8,128)(2,1)S(1)}, u32[]{:S(2)}, u32[]{:S(2)}) collective-permute-start(bf16[8,64,256]{2,1,0:T(8,128)(2,1)S(1)} %all_to_all.21.block_ref), channel_id=1, source_target_pairs={{0,496},{8,504},{16,32},{24,40},{32,16},{40,24},{48,64},{56,72},{6... | collective-permute-start | bytes 786440 | tf_op jit(solution)/shard_map/ppermute | solution.py:176
  85.0 2.9 %all-gather.2 = f32[256,256]{1,0:T(8,128)S(1)} all-gather(f32[128,256]{1,0:T(8,128)S(1)} %pad_maximum_fusion), channel_id=4, replica_groups=mesh['y_lo'=4,'z'=8,'core'=2,'x'=4,'y_hi'=2] {'core'}, dimensions={0}, use_global_device_ids=true | all-gather | bytes 393216 | tf_op jit(solution)/shard_map/all_gather | solution.py:218
  89.9 1.2 collective-permute-done.5.block_ref
  91.2 0.8 shard_map.67
  92.2 17.4 %all_to_all.22 = f32[32,4,128]{2,1,0:T(4,128)S(1)} all-to-all(f32[32,4,128]{2,1,0:T(4,128)S(1)} %broadcast_in_dim.16), channel_id=1, replica_groups=mesh['y_lo'=4,'z'=8,'core'=2,'x'=4,'y_hi'=2] {'x','y_hi','y_lo'}, dimensions={0} | all-to-all | bytes 131072 | tf_op jit(solution)/shard_map/all_to_all | solution.py:169
  110.3 6.2 %all-to-all-start.3 = ((f32[16,4,128]{2,1,0:T(4,128)}), f32[16,4,128]{2,1,0:T(4,128)S(1)}, u32[]{:S(2)}, u32[]{:S(2)}) async-start(f32[16,4,128]{2,1,0:T(4,128)} %broadcast_in_dim.17), calls=%async_computation.3 | async-start | bytes 65536 | tf_op jit(solution)/shard_map/all_to_all | solution.py:169
  116.5 1.9 %all-gather.3 = f32[128,256]{1,0:T(8,128)S(1)} all-gather(f32[64,256]{1,0:T(8,128)S(1)} %get-tuple-element.37.peer_ref), channel_id=5, replica_groups=mesh['y_lo'=4,'z'=8,'core'=2,'x'=4,'y_hi'=2] {'core'}, dimensions={0}, use_global_device_ids=true | all-gather | bytes 196608 | tf_op jit(solution)/shard_map/all_gather | solution.py:230
  118.4 5.5 %all-to-all-done.3 = f32[16,4,128]{2,1,0:T(4,128)S(1)} async-done(((f32[16,4,128]{2,1,0:T(4,128)}), f32[16,4,128]{2,1,0:T(4,128)S(1)}, u32[]{:S(2)}, u32[]{:S(2)}) %all-to-all-start.3) | async-done | bytes 32800 | tf_op jit(solution)/shard_map/all_to_all | solution.py:169
  124.1 0.8 fusion.5
  (27 shorter events, 4.9 us)
Async XLA Ops:
  0.6 57.9 %copy-start = (f32[64,256]{1,0:T(8,128)S(1)}, f32[64,256]{1,0:T(8,128)}, u32[]{:S(2)}) copy-start(f32[64,256]{1,0:T(8,128)} %first_ref.3) | copy-start | bytes 196612
  0.6 57.9 %copy-start.1 = (f32[256]{0:T(256)S(1)}, f32[256]{0:T(256)}, u32[]{:S(2)}) copy-start(f32[256]{0:T(256)} %param.6) | copy-start | bytes 3076
  24.1 23.6 %collective-permute-start = (bf16[8,96,256]{2,1,0:T(8,128)(2,1)S(1)}, bf16[8,96,256]{2,1,0:T(8,128)(2,1)S(1)}, u32[]{:S(2)}, u32[]{:S(2)}) collective-permute-start(bf16[8,96,256]{2,1,0:T(8,128)(2,1)S(1)} %all_to_all.20.block_ref), channel_id=1, source_target_pairs={{0,16},{8,24},{16,0},{24,8},{32,48},{40,56},{48,32},{56,40},{64,80... | collective-permute-start | bytes 1179656 | tf_op jit(solution)/shard_map/ppermute | solution.py:176
  28.1 22.1 %collective-permute-start.1 = (bf16[8,96,256]{2,1,0:T(8,128)(2,1)S(1)}, bf16[8,96,256]{2,1,0:T(8,128)(2,1)S(1)}, u32[]{:S(2)}, u32[]{:S(2)}) collective-permute-start(bf16[8,96,256]{2,1,0:T(8,128)(2,1)S(1)} %all_to_all.20.block_ref), channel_id=1, source_target_pairs={{0,496},{8,504},{16,32},{24,40},{32,16},{40,24},{48,64},{56,72},{6... | collective-permute-start | bytes 1179656 | tf_op jit(solution)/shard_map/ppermute | solution.py:176
  37.3 17.3 %collective-permute-start.2 = (bf16[8,96,256]{2,1,0:T(8,128)(2,1)S(1)}, bf16[8,96,256]{2,1,0:T(8,128)(2,1)S(1)}, u32[]{:S(2)}, u32[]{:S(2)}) collective-permute-start(bf16[8,96,256]{2,1,0:T(8,128)(2,1)S(1)} %all_to_all.20.block_ref), channel_id=1, source_target_pairs={{0,480},{8,40},{16,496},{24,56},{32,0},{40,72},{48,16},{56,88},{64... | collective-permute-start | bytes 1179656 | tf_op jit(solution)/shard_map/ppermute | solution.py:176
  72.4 16.3 %collective-permute-start.3 = (bf16[8,64,256]{2,1,0:T(8,128)(2,1)S(1)}, bf16[8,64,256]{2,1,0:T(8,128)(2,1)S(1)}, u32[]{:S(2)}, u32[]{:S(2)}) collective-permute-start(bf16[8,64,256]{2,1,0:T(8,128)(2,1)S(1)} %all_to_all.21.block_ref), channel_id=1, source_target_pairs={{0,480},{8,40},{16,496},{24,56},{32,0},{40,72},{48,16},{56,88},{64... | collective-permute-start | bytes 786440 | tf_op jit(solution)/shard_map/ppermute | solution.py:176
  74.7 14.5 %collective-permute-start.4 = (bf16[8,64,256]{2,1,0:T(8,128)(2,1)S(1)}, bf16[8,64,256]{2,1,0:T(8,128)(2,1)S(1)}, u32[]{:S(2)}, u32[]{:S(2)}) collective-permute-start(bf16[8,64,256]{2,1,0:T(8,128)(2,1)S(1)} %all_to_all.21.block_ref), channel_id=1, source_target_pairs={{0,16},{8,24},{16,0},{24,8},{32,48},{40,56},{48,32},{56,40},{64,80... | collective-permute-start | bytes 786440 | tf_op jit(solution)/shard_map/ppermute | solution.py:176
  77.8 13.3 %collective-permute-start.5 = (bf16[8,64,256]{2,1,0:T(8,128)(2,1)S(1)}, bf16[8,64,256]{2,1,0:T(8,128)(2,1)S(1)}, u32[]{:S(2)}, u32[]{:S(2)}) collective-permute-start(bf16[8,64,256]{2,1,0:T(8,128)(2,1)S(1)} %all_to_all.21.block_ref), channel_id=1, source_target_pairs={{0,496},{8,504},{16,32},{24,40},{32,16},{40,24},{48,64},{56,72},{6... | collective-permute-start | bytes 786440 | tf_op jit(solution)/shard_map/ppermute | solution.py:176
  110.3 13.6 %all-to-all-start.3 = ((f32[16,4,128]{2,1,0:T(4,128)}), f32[16,4,128]{2,1,0:T(4,128)S(1)}, u32[]{:S(2)}, u32[]{:S(2)}) async-start(f32[16,4,128]{2,1,0:T(4,128)} %broadcast_in_dim.17), calls=%async_computation.3 | async-start | bytes 65536 | tf_op jit(solution)/shard_map/all_to_all | solution.py:169

commit v9 on v8

--- a/solution.py
+++ b/solution.py
@@ -13,6 +13,7 @@
 SIZES = (4, 8, 2, 4, 2)
 BLK = ("y_lo", "z", "core")
 N_BLK = 64
+SWAP = ((0, 1), (1, 0))
 
 LN2 = math.log(2.0)
 UNIT = math.sqrt(5.0) / LN2
@@ -28,7 +29,8 @@
 RHS = 64
 WIDTH = 256
 DEPTH = 80
-SHARDS = 8
+SHARDS = 4
+ROWS = 2 * WIDTH
 SIGMA = 0.5
 NT = (((1,), (1,)), ((), ()))
 
@@ -53,7 +55,7 @@
     dist_ref[...] = jnp.dot(weights, cols_ref[...], preferred_element_type=F32)
     step = 64
     for half, level in enumerate(levels):
-        for at in range(half * WIDTH, (half + 1) * WIDTH, step):
+        for at in range(half * ROWS, (half + 1) * ROWS, step):
             part = jnp.maximum(dist_ref[at : at + step], TINY)
             moved = part * lax.rsqrt(part) + SHIFT
             entry = (moved * moved + OFFSET) * jnp.exp2(level - moved)
@@ -73,22 +75,22 @@
     core = lax.axis_index("core")
     row = lax.broadcasted_iota(jnp.int32, (FEAT, FEAT), 0)
     column = lax.broadcasted_iota(jnp.int32, (FEAT, FEAT), 1)
-    scale = jnp.sum(jnp.where(row == column, scale_ref[:, :FEAT], 0.0), axis=1, keepdims=True)
-    for at, ref in enumerate((both_ref.at[core], both_ref.at[1 - core])):
+    scale = GRID / jnp.sum(jnp.where(row == column, scale_ref[...], 0.0), axis=1, keepdims=True)
+    for at, ref in enumerate(both_ref.at[which, peer] for which in (core, 1 - core) for peer in range(2)):
         rows = slice(at * WIDTH, (at + 1) * WIDTH)
-        coords = ref[...] * scale
+        coords = ref[:FEAT] * scale
         scaled = coords * (-2.0 * SPAN**2)
         high = scaled.astype(BF16).astype(F32)
         stacked = jnp.concatenate([high, scaled - high, square_rows(coords, 3, 0)], axis=0)
         weights_ref[rows] = jnp.transpose(stacked).astype(BF16)
     total = build_block(weights_ref[...], LEVELS[:2], block_ref, cols_ref, dist_ref, kernel_ref)
-    own_ref[...] = total[:, :WIDTH]
-    peer_ref[...] = total[:, WIDTH:]
+    own_ref[...] = total[:, :ROWS]
+    peer_ref[...] = total[:, ROWS:]
 
 
 def build_far(weights_ref, before_ref, block_ref, peer_ref, kernel_ref, cols_ref, dist_ref):
     peer_ref[...] = before_ref[...] + build_block(
-        weights_ref[WIDTH:], LEVELS[3:], block_ref, cols_ref, dist_ref, kernel_ref
+        weights_ref[ROWS:], LEVELS[3:], block_ref, cols_ref, dist_ref, kernel_ref
     )
 
 
@@ -98,8 +100,8 @@
     near = (lax.axis_index("z") + lax.axis_index("core") + second) % 2 == 0
     levels = LEVELS[2], jnp.where(near, LEVELS[1], LEVELS[3])
     total = build_block(weights_ref[...], levels, block_ref, cols_ref, dist_ref, kernel_ref)
-    own_ref[...] = own_before[...] + total[:, :WIDTH]
-    peer_ref[...] = peer_before[...] + total[:, WIDTH:]
+    own_ref[...] = own_before[...] + total[:, :ROWS]
+    peer_ref[...] = peer_before[...] + total[:, ROWS:]
 
 
 def apply_block(kernel_ref, block_ref):
@@ -112,8 +114,8 @@
 
 def apply_first(kernel_ref, block_ref, own_ref, peer_ref):
     total = apply_block(kernel_ref, block_ref)
-    own_ref[...] = total[:, :WIDTH]
-    peer_ref[...] = total[:, WIDTH:]
+    own_ref[...] = total[:, :ROWS]
+    peer_ref[...] = total[:, ROWS:]
 
 
 def apply_far(kernel_ref, before_ref, block_ref, peer_ref):
@@ -122,8 +124,8 @@
 
 def apply_pair(kernel_ref, own_before, peer_before, block_ref, own_ref, peer_ref):
     total = apply_block(kernel_ref, block_ref)
-    own_ref[...] = own_before[...] + total[:, :WIDTH]
-    peer_ref[...] = peer_before[...] + total[:, WIDTH:]
+    own_ref[...] = own_before[...] + total[:, :ROWS]
+    peer_ref[...] = peer_before[...] + total[:, ROWS:]
 
 
 def row_sum(product):
@@ -141,22 +143,27 @@
 
 
 def late_sums(
-    early_ref, noise_ref, images_ref, first_ref, image_ref, first_total_ref, own_ref, peer_ref, sums_ref
+    early_ref, noise_ref, first_ref, image_ref, first_total_ref, firsts_ref, images_ref, own_ref, peer_ref, sums_ref
 ):
     core = lax.axis_index("core")
     image = image_ref[...]
-    known = noise_ref[...] * image + (first_total_ref[...] - own_ref[...]) * (1.0 / SIGMA)
-    lent = peer_ref[...] * (1.0 / SIGMA)
+    known = noise_ref[...] * image + first_total_ref[...] * (1.0 / SIGMA)
+    rows = [first_ref[...] * known, image * known]
+    for which, part_ref in ((core, own_ref), (1 - core, peer_ref)):
+        for peer in range(2):
+            sent = part_ref[:, peer * WIDTH : (peer + 1) * WIDTH] * (1.0 / SIGMA)
+            rows[0] -= firsts_ref[which, peer, FEAT:] * sent
+            rows[1] -= images_ref[which, peer] * sent
     sums_ref[0:2] = early_ref[...]
-    sums_ref[2:3, :RHS] = row_sum(first_ref[...] * known - images_ref[1 - core, :RHS] * lent)
-    sums_ref[2:3, RHS:] = row_sum(image * known - images_ref[1 - core, RHS:] * lent)
+    sums_ref[2:3, :RHS] = row_sum(rows[0])
+    sums_ref[2:3, RHS:] = row_sum(rows[1])
     sums_ref[3:4] = jnp.zeros((1, 2 * RHS), F32)
 
 
-VMEM_LIMIT = pltpu.CompilerParams(vmem_limit_bytes=48 * 1024 * 1024)
-
-
-def scratch(rows=2 * WIDTH):
+VMEM_LIMIT = pltpu.CompilerParams(vmem_limit_bytes=20 * 1024 * 1024)
+
+
+def scratch(rows=2 * ROWS):
     return [pltpu.VMEM((2, DEPTH, WIDTH), BF16), pltpu.VMEM((2, rows, WIDTH), F32)]
 
 
@@ -176,7 +183,7 @@
     return tuple(lax.ppermute(block, BLK, route) for route in (fourth, first, second))
 
 
-def kernel_shape(rows=2 * WIDTH):
+def kernel_shape(rows=2 * ROWS):
     return shape(SHARDS, rows, WIDTH, dtype=BF16)
 
 
@@ -184,23 +191,31 @@
     return pl.pallas_call(body, out_shape=out_shape, scratch_shapes=scratch_shapes, compiler_params=VMEM_LIMIT)
 
 
+def summed(own, peer):
+    lent = lax.all_gather(peer, "core")
+    total = own + jnp.where(lax.axis_index("core") == 0, lent[1], lent[0])
+    return total[:, :WIDTH] + lax.ppermute(total[:, WIDTH:], "y_hi", SWAP)
+
+
 def body(points, lengthscale, noise_var, targets):
     scale = GRID / jnp.pad(lengthscale, (0, RHS), constant_values=GRID)
-    exact = jnp.concatenate([points, targets], axis=0) * scale[:, None]
-    block = gathered(exact.astype(BF16), ("x", "y_hi"))
-    both = lax.all_gather(points, "core")
+    known = lax.optimization_barrier(jnp.concatenate([points, targets], axis=0))
+    exact = known * scale[:, None]
+    across = lax.ppermute(known, "y_hi", SWAP)
+    block = gathered(exact.astype(BF16), ("x",))
+    both = lax.all_gather(jnp.stack([known, across]), "core")
     far, *pairs = halo(block)
 
-    half = shape(RHS, WIDTH)
+    half = shape(RHS, ROWS)
     weights, own, peer, kernel_own = call(
         build_first,
-        (shape(2 * WIDTH, DEPTH, dtype=BF16), half, half, kernel_shape()),
+        (shape(2 * ROWS, DEPTH, dtype=BF16), half, half, kernel_shape()),
         scratch_shapes=scratch(),
-    )(scale[None], both, block)
+    )(lengthscale[None], both, block)
     kernels = {}
     for kind in "ABF":
         if kind == "F":
-            peer, kernels[kind] = call(build_far, (half, kernel_shape(WIDTH)), scratch_shapes=scratch(WIDTH))(
+            peer, kernels[kind] = call(build_far, (half, kernel_shape(ROWS)), scratch_shapes=scratch(ROWS))(
                 weights, peer, far
             )
         else:
@@ -210,25 +225,24 @@
             )(weights, own, peer, pairs[second])
 
     noise = noise_var[None, :]
-    even = lax.axis_index("core") == 0
-    lent = lax.all_gather(peer, "core")
-    first_total = own + jnp.where(even, lent[1], lent[0])
+    first_total = summed(own, peer)
     image = noise * targets + first_total
-    block = gathered((targets - SIGMA * image).astype(BF16), ("x", "y_hi"))
-    images = lax.all_gather(jnp.concatenate([targets, image], axis=0), "core")
+    block = gathered((targets - SIGMA * image).astype(BF16), ("x",))
+    block, later = lax.optimization_barrier((block, image))
+    across = lax.ppermute(later, "y_hi", SWAP)
+    images = lax.all_gather(jnp.stack([image, across]), "core")
     far, *pairs = halo(block)
     early = call(early_sums, shape(2, 2 * RHS))(targets, image)
     own, peer = call(apply_first, (half, half))(kernel_own, block)
-    for kind in "FAB":
+    for kind in "FBA":
         if kind == "F":
             peer = call(apply_far, half)(kernels[kind], peer, far)
         else:
             own, peer = call(apply_pair, (half, half))(kernels[kind], own, peer, pairs["AB".index(kind)])
     sums = call(late_sums, shape(4, 2 * RHS))(
-        early, noise, images, targets, image, first_total, own, peer
+        early, noise, targets, image, first_total, both, images, own, peer
     )
-    lent = lax.all_gather(peer, "core")
-    second = noise * image + (first_total - own - jnp.where(even, lent[1], lent[0])) * (1.0 / SIGMA)
+    second = noise * image + (first_total - summed(own, peer)) * (1.0 / SIGMA)
     for axes in (("x", "y_hi", "y_lo"), ("z", "core")):
         sums = jnp.sum(gathered(sums, axes), axis=0)
 

time: 125 us -> 122 us (0.976)
  blocking collectives: 65.6 us -> 25.3 us
  starting transfers between devices: 33.6 us -> 63.4 us
  waiting for transfers between devices: 8.66 us -> 14.9 us
  local copies, waits for them, and re-layouts: 0.71 us -> 2.67 us
    all_to_all x3 -> x1, blocking collectives: 52.9 us -> 9.98 us  [gathered(): lax.all_to_all(jnp.broadcast_to(value[None], (count,) + value.shape), axe...]
    ppermute x0 -> x4, starting transfers between devices: none -> 18.9 us  [the longest x1 7.44 us: body(): across = lax.ppermute(known, 'y_hi', SWAP)]
    all_to_all x1 -> x3, starting transfers between devices: 6.22 us -> 17.9 us  [gathered(): lax.all_to_all(jnp.broadcast_to(value[None], (count,) + value.shape), axe...]
    ppermute x0 -> x4, waiting for transfers between devices: none -> 6.27 us  [the longest x2 6.26 us: summed(): return total[:, :WIDTH] + lax.ppermute(total[:, WIDTH:], 'y_hi', SWAP)]
    ppermute x6, waiting for transfers between devices: 3.16 us -> 0.02 us  [halo(): lax.ppermute(block, BLK, route)]
    all_to_all x1 -> x3, waiting for transfers between devices: 5.5 us -> 8.62 us  [gathered(): lax.all_to_all(jnp.broadcast_to(value[None], (count,) + value.shape), axe...]
    all_gather x4, blocking collectives: 12.6 us -> 15.3 us  [the longest x2 6.97 us: summed(): lent = lax.all_gather(peer, 'core')]
    broadcast_in_dim x4, local copies, waits for them, and re-layouts: 0.7 us -> 1.99 us  [gathered(): jnp.broadcast_to(value[None], (count,) + value.shape)]
  transfers between devices with their start and end apart: 7 -> 13, of which waited for: 3 -> 4; matrix products, arithmetic and copies ran while one was open for 1% -> 0% of each run, Pallas kernels for 8% -> 7%
where the time goes in v9:
time: 122 us; the launch traced here: 121 us
  starting transfers between devices  63.4 us (52%)
  blocking collectives  25.3 us (21%)
  waiting for transfers between devices  14.9 us (12%)
  Pallas kernels  11.4 us (9%)
  other arithmetic  2.69 us (2%)
  local copies, waits for them, and re-layouts  2.67 us (2%)
    ppermute x6, starting transfers between devices, halo(): lax.ppermute(block, BLK, route)  26.6 us
    all_to_all x3, starting transfers between devices, gathered(): lax.all_to_all(jnp.broadcast_to(value[None], (count,) + value.shape), axe...  17.9 us
    all_to_all x1, blocking collectives, gathered(): lax.all_to_all(jnp.broadcast_to(value[None], (count,) + value.shape), axe...  9.98 us
    all_to_all x3, waiting for transfers between devices, gathered(): lax.all_to_all(jnp.broadcast_to(value[None], (count,) + value.shape), axe...  8.62 us
    ppermute x1, starting transfers between devices, body(): across = lax.ppermute(known, 'y_hi', SWAP)  7.44 us
    ppermute x2, starting transfers between devices, summed(): return total[:, :WIDTH] + lax.ppermute(total[:, WIDTH:], 'y_hi', SWAP)  7.36 us
    all_gather x2, blocking collectives, summed(): lent = lax.all_gather(peer, 'core')  6.97 us
    ppermute x2, waiting for transfers between devices, summed(): return total[:, :WIDTH] + lax.ppermute(total[:, WIDTH:], 'y_hi', SWAP)  6.26 us
  transfers between devices with their start and end apart: 13, of which 4 were waited for; matrix products, arithmetic and copies ran while one was open for 0% of the time, Pallas kernels for 7%

profile of v9, /device:TPU:1, one launch (start us, length us, event | category | flops | bytes accessed | tf_op | source)
XLA Modules:
  0.0 121.3 jit_solution(1680563346697412760)
XLA Ops:
  2.9 4.8 %all-to-all-start = ((bf16[4,96,256]{2,1,0:T(8,128)(2,1)}), bf16[4,96,256]{2,1,0:T(8,128)(2,1)S(1)}, u32[]{:S(2)}, u32[]{:S(2)}) async-start(bf16[4,96,256]{2,1,0:T(8,128)(2,1)} %broadcast_in_dim.13), calls=%async_computation | async-start | bytes 393216 | tf_op jit(solution)/shard_map/all_to_all | solution.py:176
  7.8 7.4 %collective-permute-start = (f32[96,256]{1,0:T(8,128)S(1)}, f32[96,256]{1,0:T(8,128)S(1)}, u32[]{:S(2)}, u32[]{:S(2)}) collective-permute-start(f32[96,256]{1,0:T(8,128)S(1)} %pad_maximum_fusion.2), channel_id=1, source_target_pairs={{0,1},{1,0},{2,3},{3,2},{4,5},{5,4},{6,7},{7,6},{8,9},{9,8},{10,11... | collective-permute-start | bytes 294920 | tf_op jit(solution)/shard_map/ppermute | solution.py:204
  15.2 4.0 %collective-permute-start.1 = (bf16[4,96,256]{2,1,0:T(8,128)(2,1)S(1)}, bf16[4,96,256]{2,1,0:T(8,128)(2,1)S(1)}, u32[]{:S(2)}, u32[]{:S(2)}) collective-permute-start(bf16[4,96,256]{2,1,0:T(8,128)(2,1)S(1)} %all-to-all-done.block_ref), channel_id=1, source_target_pairs={{0,16},{8,24},{16,0},{24,8},{32,48},{40,56},{48,32},{56,40},{64,80... | collective-permute-start | bytes 589832 | tf_op jit(solution)/shard_map/ppermute | solution.py:183
  19.2 9.6 %collective-permute-start.2 = (bf16[4,96,256]{2,1,0:T(8,128)(2,1)S(1)}, bf16[4,96,256]{2,1,0:T(8,128)(2,1)S(1)}, u32[]{:S(2)}, u32[]{:S(2)}) collective-permute-start(bf16[4,96,256]{2,1,0:T(8,128)(2,1)S(1)} %all-to-all-done.block_ref), channel_id=1, source_target_pairs={{0,496},{8,504},{16,32},{24,40},{32,16},{40,24},{48,64},{56,72},{6... | collective-permute-start | bytes 589832 | tf_op jit(solution)/shard_map/ppermute | solution.py:183
  28.8 1.9 %collective-permute-start.3 = (bf16[4,96,256]{2,1,0:T(8,128)(2,1)S(1)}, bf16[4,96,256]{2,1,0:T(8,128)(2,1)S(1)}, u32[]{:S(2)}, u32[]{:S(2)}) collective-permute-start(bf16[4,96,256]{2,1,0:T(8,128)(2,1)S(1)} %all-to-all-done.block_ref), channel_id=1, source_target_pairs={{0,480},{8,40},{16,496},{24,56},{32,0},{40,72},{48,16},{56,88},{64... | collective-permute-start | bytes 589832 | tf_op jit(solution)/shard_map/ppermute | solution.py:183
  30.8 5.4 %all-gather = f32[4,96,256]{2,1,0:T(8,128)S(1)} all-gather(f32[2,96,256]{2,1,0:T(8,128)S(1)} %pad_maximum_fusion), channel_id=2, replica_groups=mesh['y_lo'=4,'z'=8,'core'=2,'x'=4,'y_hi'=2] {'core'}, dimensions={0}, use_global_device_ids=true | all-gather | bytes 589824 | tf_op jit(solution)/shard_map/all_gather | solution.py:206
  36.9 2.4 %shard_map.59 = (bf16[1024,80]{1,0:T(8,128)(2,1)S(1)}, f32[64,512]{1,0:T(8,128)S(1)}, f32[64,512]{1,0:T(8,128)S(1)}, bf16[4,1024,256]{2,1,0:T(8,128)(2,1)S(1)}) custom-call(f32[1,32]{1,0:T(1,128)S(1)} %bitcast.61, f32[2,2,96,256]{3,2,1,0:T(8,128)S(1)} %bitcast.56, bf16[4,96,256]{2,1,0:T(8,128)(2,1)S(1)} %all-to-all-done.block_ref), custom_call_target="tpu_custom_call" | custom-call | tf_op jit(solution)/shard_map/pallas_call | solution.py:210
  39.3 2.2 %shard_map.60 = (f32[64,512]{1,0:T(8,128)S(1)}, f32[64,512]{1,0:T(8,128)S(1)}, bf16[4,1024,256]{2,1,0:T(8,128)(2,1)S(1)}) custom-call(bf16[1024,80]{1,0:T(8,128)(2,1)S(1)} %get-tuple-element.22.weights_ref, f32[64,512]{1,0:T(8,128)S(1)} %get-tuple-element.23.own_before, f32[64,512]{1,0:T(8,128)S(1)} %get-tuple-element.24.peer_before, ...), custom_call_target="tpu_custom_call" | custom-call | tf_op jit(solution)/shard_map/pallas_call | solution.py:223
  41.6 2.2 %shard_map.61 = (f32[64,512]{1,0:T(8,128)S(1)}, f32[64,512]{1,0:T(8,128)S(1)}, bf16[4,1024,256]{2,1,0:T(8,128)(2,1)S(1)}) custom-call(bf16[1024,80]{1,0:T(8,128)(2,1)S(1)} %get-tuple-element.22.weights_ref, f32[64,512]{1,0:T(8,128)S(1)} %get-tuple-element.25.own_before, f32[64,512]{1,0:T(8,128)S(1)} %get-tuple-element.26.peer_before, ...), custom_call_target="tpu_custom_call" | custom-call | tf_op jit(solution)/shard_map/pallas_call | solution.py:223
  45.1 2.0 %all-gather.1 = f32[128,512]{1,0:T(8,128)S(1)} all-gather(f32[64,512]{1,0:T(8,128)S(1)} %get-tuple-element.29), channel_id=3, replica_groups=mesh['y_lo'=4,'z'=8,'core'=2,'x'=4,'y_hi'=2] {'core'}, dimensions={0}, use_global_device_ids=true | all-gather | bytes 393216 | tf_op jit(solution)/shard_map/all_gather | solution.py:195
  47.1 4.8 %collective-permute-start.4 = (f32[64,256]{1,0:T(8,128)S(1)}, f32[64,256]{1,0:T(8,128)S(1)}, u32[]{:S(2)}, u32[]{:S(2)}) collective-permute-start(f32[64,256]{1,0:T(8,128)S(1)} %slice.59), channel_id=1, source_target_pairs={{0,1},{1,0},{2,3},{3,2},{4,5},{5,4},{6,7},{7,6},{8,9},{9,8},{10,11... | collective-permute-start | bytes 196616 | tf_op jit(solution)/shard_map/ppermute | solution.py:197
  51.9 4.2 %collective-permute-done.4 = f32[64,256]{1,0:T(8,128)S(1)} collective-permute-done((f32[64,256]{1,0:T(8,128)S(1)}, f32[64,256]{1,0:T(8,128)S(1)}, u32[]{:S(2)}, u32[]{:S(2)}) %collective-permute-start.4) | collective-permute-done | bytes 65568 | tf_op jit(solution)/shard_map/ppermute | solution.py:197
  56.1 10.0 %all_to_all.20.block_ref = bf16[4,64,256]{2,1,0:T(8,128)(2,1)S(1)} all-to-all(bf16[4,64,256]{2,1,0:T(8,128)(2,1)S(1)} %broadcast_in_dim.15), channel_id=1, replica_groups=mesh['y_lo'=4,'z'=8,'core'=2,'x'=4,'y_hi'=2] {'x'}, dimensions={0} | all-to-all | bytes 262144 | tf_op jit(solution)/shard_map/all_to_all | solution.py:176
  66.1 4.1 %collective-permute-start.5 = (f32[64,256]{1,0:T(8,128)S(1)}, f32[64,256]{1,0:T(8,128)S(1)}, u32[]{:S(2)}, u32[]{:S(2)}) collective-permute-start(f32[64,256]{1,0:T(8,128)S(1)} %get-tuple-element.30.image_ref), channel_id=1, source_target_pairs={{0,1},{1,0},{2,3},{3,2},{4,5},{5,4},{6,7},{7,6},{8,9},{9,8},{10,11... | collective-permute-start | bytes 196616 | tf_op jit(solution)/shard_map/ppermute | solution.py:232
  70.5 3.6 %collective-permute-start.6 = (bf16[4,64,256]{2,1,0:T(8,128)(2,1)S(1)}, bf16[4,64,256]{2,1,0:T(8,128)(2,1)S(1)}, u32[]{:S(2)}, u32[]{:S(2)}) collective-permute-start(bf16[4,64,256]{2,1,0:T(8,128)(2,1)S(1)} %all_to_all.20.block_ref), channel_id=1, source_target_pairs={{0,480},{8,40},{16,496},{24,56},{32,0},{40,72},{48,16},{56,88},{64... | collective-permute-start | bytes 393224 | tf_op jit(solution)/shard_map/ppermute | solution.py:183
  74.1 5.5 %collective-permute-start.7 = (bf16[4,64,256]{2,1,0:T(8,128)(2,1)S(1)}, bf16[4,64,256]{2,1,0:T(8,128)(2,1)S(1)}, u32[]{:S(2)}, u32[]{:S(2)}) collective-permute-start(bf16[4,64,256]{2,1,0:T(8,128)(2,1)S(1)} %all_to_all.20.block_ref), channel_id=1, source_target_pairs={{0,496},{8,504},{16,32},{24,40},{32,16},{40,24},{48,64},{56,72},{6... | collective-permute-start | bytes 393224 | tf_op jit(solution)/shard_map/ppermute | solution.py:183
  82.4 2.9 %all-gather.2 = f32[4,64,256]{2,1,0:T(8,128)S(1)} all-gather(f32[2,64,256]{2,1,0:T(8,128)S(1)} %pad_maximum_fusion.1), channel_id=4, replica_groups=mesh['y_lo'=4,'z'=8,'core'=2,'x'=4,'y_hi'=2] {'core'}, dimensions={0}, use_global_device_ids=true | all-gather | bytes 393216 | tf_op jit(solution)/shard_map/all_gather | solution.py:233
  88.3 5.0 %all-to-all-start.2 = ((f32[32,4,128]{2,1,0:T(4,128)}), f32[32,4,128]{2,1,0:T(4,128)S(1)}, u32[]{:S(2)}, u32[]{:S(2)}) async-start(f32[32,4,128]{2,1,0:T(4,128)} %broadcast_in_dim.16), calls=%async_computation.2 | async-start | bytes 131072 | tf_op jit(solution)/shard_map/all_to_all | solution.py:176
  93.3 5.0 %all-gather.3 = f32[128,512]{1,0:T(8,128)S(1)} all-gather(f32[64,512]{1,0:T(8,128)S(1)} %get-tuple-element.41.peer_ref), channel_id=5, replica_groups=mesh['y_lo'=4,'z'=8,'core'=2,'x'=4,'y_hi'=2] {'core'}, dimensions={0}, use_global_device_ids=true | all-gather | bytes 393216 | tf_op jit(solution)/shard_map/all_gather | solution.py:195
  98.2 3.9 %all-to-all-done.2 = f32[32,4,128]{2,1,0:T(4,128)S(1)} async-done(((f32[32,4,128]{2,1,0:T(4,128)}), f32[32,4,128]{2,1,0:T(4,128)S(1)}, u32[]{:S(2)}, u32[]{:S(2)}) %all-to-all-start.2) | async-done | bytes 65568 | tf_op jit(solution)/shard_map/all_to_all | solution.py:176
  102.8 8.0 %all-to-all-start.3 = ((f32[16,4,128]{2,1,0:T(4,128)}), f32[16,4,128]{2,1,0:T(4,128)S(1)}, u32[]{:S(2)}, u32[]{:S(2)}) async-start(f32[16,4,128]{2,1,0:T(4,128)} %broadcast_in_dim.17), calls=%async_computation.3 | async-start | bytes 65536 | tf_op jit(solution)/shard_map/all_to_all | solution.py:176
  110.9 2.6 %collective-permute-start.9 = (f32[64,256]{1,0:T(8,128)S(1)}, f32[64,256]{1,0:T(8,128)S(1)}, u32[]{:S(2)}, u32[]{:S(2)}) collective-permute-start(f32[64,256]{1,0:T(8,128)S(1)} %slice.63), channel_id=1, source_target_pairs={{0,1},{1,0},{2,3},{3,2},{4,5},{5,4},{6,7},{7,6},{8,9},{9,8},{10,11... | collective-permute-start | bytes 196616 | tf_op jit(solution)/shard_map/ppermute | solution.py:197
  113.5 4.7 %all-to-all-done.3 = f32[16,4,128]{2,1,0:T(4,128)S(1)} async-done(((f32[16,4,128]{2,1,0:T(4,128)}), f32[16,4,128]{2,1,0:T(4,128)S(1)}, u32[]{:S(2)}, u32[]{:S(2)}) %all-to-all-start.3) | async-done | bytes 32800 | tf_op jit(solution)/shard_map/all_to_all | solution.py:176
  118.4 2.1 %collective-permute-done.9 = f32[64,256]{1,0:T(8,128)S(1)} collective-permute-done((f32[64,256]{1,0:T(8,128)S(1)}, f32[64,256]{1,0:T(8,128)S(1)}, u32[]{:S(2)}, u32[]{:S(2)}) %collective-permute-start.9) | collective-permute-done | bytes 65568 | tf_op jit(solution)/shard_map/ppermute | solution.py:197
  (43 shorter events, 11.9 us)
Async XLA Ops:
  2.9 12.3 %all-to-all-start = ((bf16[4,96,256]{2,1,0:T(8,128)(2,1)}), bf16[4,96,256]{2,1,0:T(8,128)(2,1)S(1)}, u32[]{:S(2)}, u32[]{:S(2)}) async-start(bf16[4,96,256]{2,1,0:T(8,128)(2,1)} %broadcast_in_dim.13), calls=%async_computation | async-start | bytes 393216 | tf_op jit(solution)/shard_map/all_to_all | solution.py:176
  7.8 23.0 %collective-permute-start = (f32[96,256]{1,0:T(8,128)S(1)}, f32[96,256]{1,0:T(8,128)S(1)}, u32[]{:S(2)}, u32[]{:S(2)}) collective-permute-start(f32[96,256]{1,0:T(8,128)S(1)} %pad_maximum_fusion.2), channel_id=1, source_target_pairs={{0,1},{1,0},{2,3},{3,2},{4,5},{5,4},{6,7},{7,6},{8,9},{9,8},{10,11... | collective-permute-start | bytes 294920 | tf_op jit(solution)/shard_map/ppermute | solution.py:204
  15.2 24.1 %collective-permute-start.1 = (bf16[4,96,256]{2,1,0:T(8,128)(2,1)S(1)}, bf16[4,96,256]{2,1,0:T(8,128)(2,1)S(1)}, u32[]{:S(2)}, u32[]{:S(2)}) collective-permute-start(bf16[4,96,256]{2,1,0:T(8,128)(2,1)S(1)} %all-to-all-done.block_ref), channel_id=1, source_target_pairs={{0,16},{8,24},{16,0},{24,8},{32,48},{40,56},{48,32},{56,40},{64,80... | collective-permute-start | bytes 589832 | tf_op jit(solution)/shard_map/ppermute | solution.py:183
  19.2 22.3 %collective-permute-start.2 = (bf16[4,96,256]{2,1,0:T(8,128)(2,1)S(1)}, bf16[4,96,256]{2,1,0:T(8,128)(2,1)S(1)}, u32[]{:S(2)}, u32[]{:S(2)}) collective-permute-start(bf16[4,96,256]{2,1,0:T(8,128)(2,1)S(1)} %all-to-all-done.block_ref), channel_id=1, source_target_pairs={{0,496},{8,504},{16,32},{24,40},{32,16},{40,24},{48,64},{56,72},{6... | collective-permute-start | bytes 589832 | tf_op jit(solution)/shard_map/ppermute | solution.py:183
  28.8 14.9 %collective-permute-start.3 = (bf16[4,96,256]{2,1,0:T(8,128)(2,1)S(1)}, bf16[4,96,256]{2,1,0:T(8,128)(2,1)S(1)}, u32[]{:S(2)}, u32[]{:S(2)}) collective-permute-start(bf16[4,96,256]{2,1,0:T(8,128)(2,1)S(1)} %all-to-all-done.block_ref), channel_id=1, source_target_pairs={{0,480},{8,40},{16,496},{24,56},{32,0},{40,72},{48,16},{56,88},{64... | collective-permute-start | bytes 589832 | tf_op jit(solution)/shard_map/ppermute | solution.py:183
  30.8 25.2 %copy-start = (f32[64,256]{1,0:T(8,128)S(1)}, f32[64,256]{1,0:T(8,128)}, u32[]{:S(2)}) copy-start(f32[64,256]{1,0:T(8,128)} %first_ref.3) | copy-start | bytes 196612
  30.8 25.2 %copy-start.1 = (f32[256]{0:T(256)S(1)}, f32[256]{0:T(256)}, u32[]{:S(2)}) copy-start(f32[256]{0:T(256)} %param.6) | copy-start | bytes 3076
  36.3 0.7 copy-start.2
  47.1 8.9 %collective-permute-start.4 = (f32[64,256]{1,0:T(8,128)S(1)}, f32[64,256]{1,0:T(8,128)S(1)}, u32[]{:S(2)}, u32[]{:S(2)}) collective-permute-start(f32[64,256]{1,0:T(8,128)S(1)} %slice.59), channel_id=1, source_target_pairs={{0,1},{1,0},{2,3},{3,2},{4,5},{5,4},{6,7},{7,6},{8,9},{9,8},{10,11... | collective-permute-start | bytes 196616 | tf_op jit(solution)/shard_map/ppermute | solution.py:197
  66.1 16.3 %collective-permute-start.5 = (f32[64,256]{1,0:T(8,128)S(1)}, f32[64,256]{1,0:T(8,128)S(1)}, u32[]{:S(2)}, u32[]{:S(2)}) collective-permute-start(f32[64,256]{1,0:T(8,128)S(1)} %get-tuple-element.30.image_ref), channel_id=1, source_target_pairs={{0,1},{1,0},{2,3},{3,2},{4,5},{5,4},{6,7},{7,6},{8,9},{9,8},{10,11... | collective-permute-start | bytes 196616 | tf_op jit(solution)/shard_map/ppermute | solution.py:232
  70.5 14.8 %collective-permute-start.6 = (bf16[4,64,256]{2,1,0:T(8,128)(2,1)S(1)}, bf16[4,64,256]{2,1,0:T(8,128)(2,1)S(1)}, u32[]{:S(2)}, u32[]{:S(2)}) collective-permute-start(bf16[4,64,256]{2,1,0:T(8,128)(2,1)S(1)} %all_to_all.20.block_ref), channel_id=1, source_target_pairs={{0,480},{8,40},{16,496},{24,56},{32,0},{40,72},{48,16},{56,88},{64... | collective-permute-start | bytes 393224 | tf_op jit(solution)/shard_map/ppermute | solution.py:183
  74.1 11.6 %collective-permute-start.7 = (bf16[4,64,256]{2,1,0:T(8,128)(2,1)S(1)}, bf16[4,64,256]{2,1,0:T(8,128)(2,1)S(1)}, u32[]{:S(2)}, u32[]{:S(2)}) collective-permute-start(bf16[4,64,256]{2,1,0:T(8,128)(2,1)S(1)} %all_to_all.20.block_ref), channel_id=1, source_target_pairs={{0,496},{8,504},{16,32},{24,40},{32,16},{40,24},{48,64},{56,72},{6... | collective-permute-start | bytes 393224 | tf_op jit(solution)/shard_map/ppermute | solution.py:183
  79.7 6.8 %collective-permute-start.8 = (bf16[4,64,256]{2,1,0:T(8,128)(2,1)S(1)}, bf16[4,64,256]{2,1,0:T(8,128)(2,1)S(1)}, u32[]{:S(2)}, u32[]{:S(2)}) collective-permute-start(bf16[4,64,256]{2,1,0:T(8,128)(2,1)S(1)} %all_to_all.20.block_ref), channel_id=1, source_target_pairs={{0,16},{8,24},{16,0},{24,8},{32,48},{40,56},{48,32},{56,40},{64,80... | collective-permute-start | bytes 393224 | tf_op jit(solution)/shard_map/ppermute | solution.py:183
  88.3 13.8 %all-to-all-start.2 = ((f32[32,4,128]{2,1,0:T(4,128)}), f32[32,4,128]{2,1,0:T(4,128)S(1)}, u32[]{:S(2)}, u32[]{:S(2)}) async-start(f32[32,4,128]{2,1,0:T(4,128)} %broadcast_in_dim.16), calls=%async_computation.2 | async-start | bytes 131072 | tf_op jit(solution)/shard_map/all_to_all | solution.py:176
  102.8 15.4 %all-to-all-start.3 = ((f32[16,4,128]{2,1,0:T(4,128)}), f32[16,4,128]{2,1,0:T(4,128)S(1)}, u32[]{:S(2)}, u32[]{:S(2)}) async-start(f32[16,4,128]{2,1,0:T(4,128)} %broadcast_in_dim.17), calls=%async_computation.3 | async-start | bytes 65536 | tf_op jit(solution)/shard_map/all_to_all | solution.py:176
  110.9 9.7 %collective-permute-start.9 = (f32[64,256]{1,0:T(8,128)S(1)}, f32[64,256]{1,0:T(8,128)S(1)}, u32[]{:S(2)}, u32[]{:S(2)}) collective-permute-start(f32[64,256]{1,0:T(8,128)S(1)} %slice.63), channel_id=1, source_target_pairs={{0,1},{1,0},{2,3},{3,2},{4,5},{5,4},{6,7},{7,6},{8,9},{9,8},{10,11... | collective-permute-start | bytes 196616 | tf_op jit(solution)/shard_map/ppermute | solution.py:197

commit v10 on v9

--- a/solution.py
+++ b/solution.py
@@ -71,14 +71,11 @@
     return total
 
 
-def build_first(scale_ref, both_ref, block_ref, weights_ref, own_ref, peer_ref, kernel_ref, cols_ref, dist_ref):
+def build_first(both_ref, block_ref, weights_ref, own_ref, peer_ref, kernel_ref, cols_ref, dist_ref):
     core = lax.axis_index("core")
-    row = lax.broadcasted_iota(jnp.int32, (FEAT, FEAT), 0)
-    column = lax.broadcasted_iota(jnp.int32, (FEAT, FEAT), 1)
-    scale = GRID / jnp.sum(jnp.where(row == column, scale_ref[...], 0.0), axis=1, keepdims=True)
     for at, ref in enumerate(both_ref.at[which, peer] for which in (core, 1 - core) for peer in range(2)):
         rows = slice(at * WIDTH, (at + 1) * WIDTH)
-        coords = ref[:FEAT] * scale
+        coords = ref[:FEAT]
         scaled = coords * (-2.0 * SPAN**2)
         high = scaled.astype(BF16).astype(F32)
         stacked = jnp.concatenate([high, scaled - high, square_rows(coords, 3, 0)], axis=0)
@@ -203,7 +200,7 @@
     exact = known * scale[:, None]
     across = lax.ppermute(known, "y_hi", SWAP)
     block = gathered(exact.astype(BF16), ("x",))
-    both = lax.all_gather(jnp.stack([known, across]), "core")
+    both = lax.all_gather(jnp.stack([known, across]) * scale[:, None], "core")
     far, *pairs = halo(block)
 
     half = shape(RHS, ROWS)
@@ -211,7 +208,7 @@
         build_first,
         (shape(2 * ROWS, DEPTH, dtype=BF16), half, half, kernel_shape()),
         scratch_shapes=scratch(),
-    )(lengthscale[None], both, block)
+    )(both, block)
     kernels = {}
     for kind in "ABF":
         if kind == "F":
@@ -228,12 +225,12 @@
     first_total = summed(own, peer)
     image = noise * targets + first_total
     block = gathered((targets - SIGMA * image).astype(BF16), ("x",))
-    block, later = lax.optimization_barrier((block, image))
-    across = lax.ppermute(later, "y_hi", SWAP)
-    images = lax.all_gather(jnp.stack([image, across]), "core")
     far, *pairs = halo(block)
     early = call(early_sums, shape(2, 2 * RHS))(targets, image)
     own, peer = call(apply_first, (half, half))(kernel_own, block)
+    own, later = lax.optimization_barrier((own, image))
+    across = lax.ppermute(later, "y_hi", SWAP)
+    images = lax.all_gather(jnp.stack([image, across]), "core")
     for kind in "FBA":
         if kind == "F":
             peer = call(apply_far, half)(kernels[kind], peer, far)

time: 122 us -> 122 us (level)
  no operation moved by 1% of the time
where the time goes in v10:
time: 122 us; the launch traced here: 121 us
  starting transfers between devices  64 us (52%)
  blocking collectives  25.5 us (21%)
  waiting for transfers between devices  14.7 us (12%)
  Pallas kernels  11.3 us (9%)
  other arithmetic  2.74 us (2%)
  local copies, waits for them, and re-layouts  2 us (2%)
    ppermute x6, starting transfers between devices, halo(): lax.ppermute(block, BLK, route)  26.6 us
    all_to_all x3, starting transfers between devices, gathered(): lax.all_to_all(jnp.broadcast_to(value[None], (count,) + value.shape), axe...  18.5 us
    all_to_all x1, blocking collectives, gathered(): lax.all_to_all(jnp.broadcast_to(value[None], (count,) + value.shape), axe...  9.98 us
    all_to_all x3, waiting for transfers between devices, gathered(): lax.all_to_all(jnp.broadcast_to(value[None], (count,) + value.shape), axe...  8.59 us
    ppermute x1, starting transfers between devices, body(): across = lax.ppermute(known, 'y_hi', SWAP)  7.44 us
    ppermute x2, starting transfers between devices, summed(): return total[:, :WIDTH] + lax.ppermute(total[:, WIDTH:], 'y_hi', SWAP)  7.34 us
    all_gather x2, blocking collectives, summed(): lent = lax.all_gather(peer, 'core')  7.13 us
    ppermute x2, waiting for transfers between devices, summed(): return total[:, :WIDTH] + lax.ppermute(total[:, WIDTH:], 'y_hi', SWAP)  6.04 us
  transfers between devices with their start and end apart: 13, of which 4 were waited for; matrix products, arithmetic and copies ran while one was open for 0% of the time, Pallas kernels for 7%

profile of v10, /device:TPU:1, one launch (start us, length us, event | category | flops | bytes accessed | tf_op | source)
XLA Modules:
  0.0 121.1 jit_solution(13238765450025019779)
XLA Ops:
  2.9 4.8 %all-to-all-start = ((bf16[4,96,256]{2,1,0:T(8,128)(2,1)}), bf16[4,96,256]{2,1,0:T(8,128)(2,1)S(1)}, u32[]{:S(2)}, u32[]{:S(2)}) async-start(bf16[4,96,256]{2,1,0:T(8,128)(2,1)} %broadcast_in_dim.10), calls=%async_computation | async-start | bytes 393216 | tf_op jit(solution)/shard_map/all_to_all | solution.py:173
  7.8 7.4 %collective-permute-start = (f32[96,256]{1,0:T(8,128)S(1)}, f32[96,256]{1,0:T(8,128)S(1)}, u32[]{:S(2)}, u32[]{:S(2)}) collective-permute-start(f32[96,256]{1,0:T(8,128)S(1)} %pad_maximum_fusion.1), channel_id=1, source_target_pairs={{0,1},{1,0},{2,3},{3,2},{4,5},{5,4},{6,7},{7,6},{8,9},{9,8},{10,11... | collective-permute-start | bytes 294920 | tf_op jit(solution)/shard_map/ppermute | solution.py:201
  15.2 4.0 %collective-permute-start.1 = (bf16[4,96,256]{2,1,0:T(8,128)(2,1)S(1)}, bf16[4,96,256]{2,1,0:T(8,128)(2,1)S(1)}, u32[]{:S(2)}, u32[]{:S(2)}) collective-permute-start(bf16[4,96,256]{2,1,0:T(8,128)(2,1)S(1)} %all-to-all-done.block_ref), channel_id=1, source_target_pairs={{0,16},{8,24},{16,0},{24,8},{32,48},{40,56},{48,32},{56,40},{64,80... | collective-permute-start | bytes 589832 | tf_op jit(solution)/shard_map/ppermute | solution.py:180
  19.2 9.6 %collective-permute-start.2 = (bf16[4,96,256]{2,1,0:T(8,128)(2,1)S(1)}, bf16[4,96,256]{2,1,0:T(8,128)(2,1)S(1)}, u32[]{:S(2)}, u32[]{:S(2)}) collective-permute-start(bf16[4,96,256]{2,1,0:T(8,128)(2,1)S(1)} %all-to-all-done.block_ref), channel_id=1, source_target_pairs={{0,496},{8,504},{16,32},{24,40},{32,16},{40,24},{48,64},{56,72},{6... | collective-permute-start | bytes 589832 | tf_op jit(solution)/shard_map/ppermute | solution.py:180
  28.8 1.9 %collective-permute-start.3 = (bf16[4,96,256]{2,1,0:T(8,128)(2,1)S(1)}, bf16[4,96,256]{2,1,0:T(8,128)(2,1)S(1)}, u32[]{:S(2)}, u32[]{:S(2)}) collective-permute-start(bf16[4,96,256]{2,1,0:T(8,128)(2,1)S(1)} %all-to-all-done.block_ref), channel_id=1, source_target_pairs={{0,480},{8,40},{16,496},{24,56},{32,0},{40,72},{48,16},{56,88},{64... | collective-permute-start | bytes 589832 | tf_op jit(solution)/shard_map/ppermute | solution.py:180
  30.9 5.4 %all_gather.22.both_ref.firsts_ref = f32[2,2,96,256]{3,2,1,0:T(8,128)S(1)} all-gather(f32[1,2,96,256]{3,2,1,0:T(8,128)S(1)} %maximum_multiply_fusion), channel_id=1, replica_groups=mesh['y_lo'=4,'z'=8,'core'=2,'x'=4,'y_hi'=2] {'core'}, dimensions={0}, use_global_device_ids=true | all-gather | bytes 589824 | tf_op jit(solution)/shard_map/all_gather | solution.py:203
  36.3 2.3 %shard_map.59 = (bf16[1024,80]{1,0:T(8,128)(2,1)S(1)}, f32[64,512]{1,0:T(8,128)S(1)}, f32[64,512]{1,0:T(8,128)S(1)}, bf16[4,1024,256]{2,1,0:T(8,128)(2,1)S(1)}) custom-call(f32[2,2,96,256]{3,2,1,0:T(8,128)S(1)} %all_gather.22.both_ref.firsts_ref, bf16[4,96,256]{2,1,0:T(8,128)(2,1)S(1)} %all-to-all-done.block_ref), custom_call_target="tpu_custom_call" | custom-call | tf_op jit(solution)/shard_map/pallas_call | solution.py:207
  38.6 2.2 %shard_map.60 = (f32[64,512]{1,0:T(8,128)S(1)}, f32[64,512]{1,0:T(8,128)S(1)}, bf16[4,1024,256]{2,1,0:T(8,128)(2,1)S(1)}) custom-call(bf16[1024,80]{1,0:T(8,128)(2,1)S(1)} %get-tuple-element.22.weights_ref, f32[64,512]{1,0:T(8,128)S(1)} %get-tuple-element.23.own_before, f32[64,512]{1,0:T(8,128)S(1)} %get-tuple-element.24.peer_before, ...), custom_call_target="tpu_custom_call" | custom-call | tf_op jit(solution)/shard_map/pallas_call | solution.py:220
  40.9 2.2 %shard_map.61 = (f32[64,512]{1,0:T(8,128)S(1)}, f32[64,512]{1,0:T(8,128)S(1)}, bf16[4,1024,256]{2,1,0:T(8,128)(2,1)S(1)}) custom-call(bf16[1024,80]{1,0:T(8,128)(2,1)S(1)} %get-tuple-element.22.weights_ref, f32[64,512]{1,0:T(8,128)S(1)} %get-tuple-element.25.own_before, f32[64,512]{1,0:T(8,128)S(1)} %get-tuple-element.26.peer_before, ...), custom_call_target="tpu_custom_call" | custom-call | tf_op jit(solution)/shard_map/pallas_call | solution.py:220
  44.4 2.0 %all-gather = f32[128,512]{1,0:T(8,128)S(1)} all-gather(f32[64,512]{1,0:T(8,128)S(1)} %get-tuple-element.29), channel_id=2, replica_groups=mesh['y_lo'=4,'z'=8,'core'=2,'x'=4,'y_hi'=2] {'core'}, dimensions={0}, use_global_device_ids=true | all-gather | bytes 393216 | tf_op jit(solution)/shard_map/all_gather | solution.py:192
  46.5 4.8 %collective-permute-start.4 = (f32[64,256]{1,0:T(8,128)S(1)}, f32[64,256]{1,0:T(8,128)S(1)}, u32[]{:S(2)}, u32[]{:S(2)}) collective-permute-start(f32[64,256]{1,0:T(8,128)S(1)} %slice.59), channel_id=1, source_target_pairs={{0,1},{1,0},{2,3},{3,2},{4,5},{5,4},{6,7},{7,6},{8,9},{9,8},{10,11... | collective-permute-start | bytes 196616 | tf_op jit(solution)/shard_map/ppermute | solution.py:194
  51.2 4.2 %collective-permute-done.4 = f32[64,256]{1,0:T(8,128)S(1)} collective-permute-done((f32[64,256]{1,0:T(8,128)S(1)}, f32[64,256]{1,0:T(8,128)S(1)}, u32[]{:S(2)}, u32[]{:S(2)}) %collective-permute-start.4) | collective-permute-done | bytes 65568 | tf_op jit(solution)/shard_map/ppermute | solution.py:194
  55.4 10.0 %all_to_all.20.block_ref = bf16[4,64,256]{2,1,0:T(8,128)(2,1)S(1)} all-to-all(bf16[4,64,256]{2,1,0:T(8,128)(2,1)S(1)} %broadcast_in_dim.12), channel_id=1, replica_groups=mesh['y_lo'=4,'z'=8,'core'=2,'x'=4,'y_hi'=2] {'x'}, dimensions={0} | all-to-all | bytes 262144 | tf_op jit(solution)/shard_map/all_to_all | solution.py:173
  66.1 4.1 %collective-permute-start.5 = (f32[64,256]{1,0:T(8,128)S(1)}, f32[64,256]{1,0:T(8,128)S(1)}, u32[]{:S(2)}, u32[]{:S(2)}) collective-permute-start(f32[64,256]{1,0:T(8,128)S(1)} %get-tuple-element.32.image_ref), channel_id=1, source_target_pairs={{0,1},{1,0},{2,3},{3,2},{4,5},{5,4},{6,7},{7,6},{8,9},{9,8},{10,11... | collective-permute-start | bytes 196616 | tf_op jit(solution)/shard_map/ppermute | solution.py:232
  70.6 3.6 %collective-permute-start.6 = (bf16[4,64,256]{2,1,0:T(8,128)(2,1)S(1)}, bf16[4,64,256]{2,1,0:T(8,128)(2,1)S(1)}, u32[]{:S(2)}, u32[]{:S(2)}) collective-permute-start(bf16[4,64,256]{2,1,0:T(8,128)(2,1)S(1)} %all_to_all.20.block_ref), channel_id=1, source_target_pairs={{0,480},{8,40},{16,496},{24,56},{32,0},{40,72},{48,16},{56,88},{64... | collective-permute-start | bytes 393224 | tf_op jit(solution)/shard_map/ppermute | solution.py:180
  74.2 5.5 %collective-permute-start.7 = (bf16[4,64,256]{2,1,0:T(8,128)(2,1)S(1)}, bf16[4,64,256]{2,1,0:T(8,128)(2,1)S(1)}, u32[]{:S(2)}, u32[]{:S(2)}) collective-permute-start(bf16[4,64,256]{2,1,0:T(8,128)(2,1)S(1)} %all_to_all.20.block_ref), channel_id=1, source_target_pairs={{0,496},{8,504},{16,32},{24,40},{32,16},{40,24},{48,64},{56,72},{6... | collective-permute-start | bytes 393224 | tf_op jit(solution)/shard_map/ppermute | solution.py:180
  79.8 1.9 %collective-permute-start.8 = (bf16[4,64,256]{2,1,0:T(8,128)(2,1)S(1)}, bf16[4,64,256]{2,1,0:T(8,128)(2,1)S(1)}, u32[]{:S(2)}, u32[]{:S(2)}) collective-permute-start(bf16[4,64,256]{2,1,0:T(8,128)(2,1)S(1)} %all_to_all.20.block_ref), channel_id=1, source_target_pairs={{0,16},{8,24},{16,0},{24,8},{32,48},{40,56},{48,32},{56,40},{64,80... | collective-permute-start | bytes 393224 | tf_op jit(solution)/shard_map/ppermute | solution.py:180
  81.7 2.9 %all-gather.1 = f32[4,64,256]{2,1,0:T(8,128)S(1)} all-gather(f32[2,64,256]{2,1,0:T(8,128)S(1)} %pad_maximum_fusion), channel_id=3, replica_groups=mesh['y_lo'=4,'z'=8,'core'=2,'x'=4,'y_hi'=2] {'core'}, dimensions={0}, use_global_device_ids=true | all-gather | bytes 393216 | tf_op jit(solution)/shard_map/all_gather | solution.py:233
  87.6 5.7 %all-to-all-start.2 = ((f32[32,4,128]{2,1,0:T(4,128)}), f32[32,4,128]{2,1,0:T(4,128)S(1)}, u32[]{:S(2)}, u32[]{:S(2)}) async-start(f32[32,4,128]{2,1,0:T(4,128)} %broadcast_in_dim.13), calls=%async_computation.2 | async-start | bytes 131072 | tf_op jit(solution)/shard_map/all_to_all | solution.py:173
  93.3 5.1 %all-gather.2 = f32[128,512]{1,0:T(8,128)S(1)} all-gather(f32[64,512]{1,0:T(8,128)S(1)} %get-tuple-element.41.peer_ref), channel_id=4, replica_groups=mesh['y_lo'=4,'z'=8,'core'=2,'x'=4,'y_hi'=2] {'core'}, dimensions={0}, use_global_device_ids=true | all-gather | bytes 393216 | tf_op jit(solution)/shard_map/all_gather | solution.py:192
  98.5 3.8 %all-to-all-done.2 = f32[32,4,128]{2,1,0:T(4,128)S(1)} async-done(((f32[32,4,128]{2,1,0:T(4,128)}), f32[32,4,128]{2,1,0:T(4,128)S(1)}, u32[]{:S(2)}, u32[]{:S(2)}) %all-to-all-start.2) | async-done | bytes 65568 | tf_op jit(solution)/shard_map/all_to_all | solution.py:173
  102.9 7.9 %all-to-all-start.3 = ((f32[16,4,128]{2,1,0:T(4,128)}), f32[16,4,128]{2,1,0:T(4,128)S(1)}, u32[]{:S(2)}, u32[]{:S(2)}) async-start(f32[16,4,128]{2,1,0:T(4,128)} %broadcast_in_dim.14), calls=%async_computation.3 | async-start | bytes 65536 | tf_op jit(solution)/shard_map/all_to_all | solution.py:173
  110.8 2.6 %collective-permute-start.9 = (f32[64,256]{1,0:T(8,128)S(1)}, f32[64,256]{1,0:T(8,128)S(1)}, u32[]{:S(2)}, u32[]{:S(2)}) collective-permute-start(f32[64,256]{1,0:T(8,128)S(1)} %slice.63), channel_id=1, source_target_pairs={{0,1},{1,0},{2,3},{3,2},{4,5},{5,4},{6,7},{7,6},{8,9},{9,8},{10,11... | collective-permute-start | bytes 196616 | tf_op jit(solution)/shard_map/ppermute | solution.py:194
  113.4 4.8 %all-to-all-done.3 = f32[16,4,128]{2,1,0:T(4,128)S(1)} async-done(((f32[16,4,128]{2,1,0:T(4,128)}), f32[16,4,128]{2,1,0:T(4,128)S(1)}, u32[]{:S(2)}, u32[]{:S(2)}) %all-to-all-start.3) | async-done | bytes 32800 | tf_op jit(solution)/shard_map/all_to_all | solution.py:173
  (41 shorter events, 11.3 us)
Async XLA Ops:
  2.9 12.3 %all-to-all-start = ((bf16[4,96,256]{2,1,0:T(8,128)(2,1)}), bf16[4,96,256]{2,1,0:T(8,128)(2,1)S(1)}, u32[]{:S(2)}, u32[]{:S(2)}) async-start(bf16[4,96,256]{2,1,0:T(8,128)(2,1)} %broadcast_in_dim.10), calls=%async_computation | async-start | bytes 393216 | tf_op jit(solution)/shard_map/all_to_all | solution.py:173
  7.8 23.0 %collective-permute-start = (f32[96,256]{1,0:T(8,128)S(1)}, f32[96,256]{1,0:T(8,128)S(1)}, u32[]{:S(2)}, u32[]{:S(2)}) collective-permute-start(f32[96,256]{1,0:T(8,128)S(1)} %pad_maximum_fusion.1), channel_id=1, source_target_pairs={{0,1},{1,0},{2,3},{3,2},{4,5},{5,4},{6,7},{7,6},{8,9},{9,8},{10,11... | collective-permute-start | bytes 294920 | tf_op jit(solution)/shard_map/ppermute | solution.py:201
  15.2 23.4 %collective-permute-start.1 = (bf16[4,96,256]{2,1,0:T(8,128)(2,1)S(1)}, bf16[4,96,256]{2,1,0:T(8,128)(2,1)S(1)}, u32[]{:S(2)}, u32[]{:S(2)}) collective-permute-start(bf16[4,96,256]{2,1,0:T(8,128)(2,1)S(1)} %all-to-all-done.block_ref), channel_id=1, source_target_pairs={{0,16},{8,24},{16,0},{24,8},{32,48},{40,56},{48,32},{56,40},{64,80... | collective-permute-start | bytes 589832 | tf_op jit(solution)/shard_map/ppermute | solution.py:180
  19.2 21.6 %collective-permute-start.2 = (bf16[4,96,256]{2,1,0:T(8,128)(2,1)S(1)}, bf16[4,96,256]{2,1,0:T(8,128)(2,1)S(1)}, u32[]{:S(2)}, u32[]{:S(2)}) collective-permute-start(bf16[4,96,256]{2,1,0:T(8,128)(2,1)S(1)} %all-to-all-done.block_ref), channel_id=1, source_target_pairs={{0,496},{8,504},{16,32},{24,40},{32,16},{40,24},{48,64},{56,72},{6... | collective-permute-start | bytes 589832 | tf_op jit(solution)/shard_map/ppermute | solution.py:180
  28.8 14.3 %collective-permute-start.3 = (bf16[4,96,256]{2,1,0:T(8,128)(2,1)S(1)}, bf16[4,96,256]{2,1,0:T(8,128)(2,1)S(1)}, u32[]{:S(2)}, u32[]{:S(2)}) collective-permute-start(bf16[4,96,256]{2,1,0:T(8,128)(2,1)S(1)} %all-to-all-done.block_ref), channel_id=1, source_target_pairs={{0,480},{8,40},{16,496},{24,56},{32,0},{40,72},{48,16},{56,88},{64... | collective-permute-start | bytes 589832 | tf_op jit(solution)/shard_map/ppermute | solution.py:180
  30.9 24.5 %copy-start = (f32[64,256]{1,0:T(8,128)S(1)}, f32[64,256]{1,0:T(8,128)}, u32[]{:S(2)}) copy-start(f32[64,256]{1,0:T(8,128)} %first_ref.3) | copy-start | bytes 196612
  30.9 24.5 %copy-start.1 = (f32[256]{0:T(256)S(1)}, f32[256]{0:T(256)}, u32[]{:S(2)}) copy-start(f32[256]{0:T(256)} %param.6) | copy-start | bytes 3076
  46.5 8.9 %collective-permute-start.4 = (f32[64,256]{1,0:T(8,128)S(1)}, f32[64,256]{1,0:T(8,128)S(1)}, u32[]{:S(2)}, u32[]{:S(2)}) collective-permute-start(f32[64,256]{1,0:T(8,128)S(1)} %slice.59), channel_id=1, source_target_pairs={{0,1},{1,0},{2,3},{3,2},{4,5},{5,4},{6,7},{7,6},{8,9},{9,8},{10,11... | collective-permute-start | bytes 196616 | tf_op jit(solution)/shard_map/ppermute | solution.py:194
  66.1 15.6 %collective-permute-start.5 = (f32[64,256]{1,0:T(8,128)S(1)}, f32[64,256]{1,0:T(8,128)S(1)}, u32[]{:S(2)}, u32[]{:S(2)}) collective-permute-start(f32[64,256]{1,0:T(8,128)S(1)} %get-tuple-element.32.image_ref), channel_id=1, source_target_pairs={{0,1},{1,0},{2,3},{3,2},{4,5},{5,4},{6,7},{7,6},{8,9},{9,8},{10,11... | collective-permute-start | bytes 196616 | tf_op jit(solution)/shard_map/ppermute | solution.py:232
  70.6 14.1 %collective-permute-start.6 = (bf16[4,64,256]{2,1,0:T(8,128)(2,1)S(1)}, bf16[4,64,256]{2,1,0:T(8,128)(2,1)S(1)}, u32[]{:S(2)}, u32[]{:S(2)}) collective-permute-start(bf16[4,64,256]{2,1,0:T(8,128)(2,1)S(1)} %all_to_all.20.block_ref), channel_id=1, source_target_pairs={{0,480},{8,40},{16,496},{24,56},{32,0},{40,72},{48,16},{56,88},{64... | collective-permute-start | bytes 393224 | tf_op jit(solution)/shard_map/ppermute | solution.py:180
  74.2 10.9 %collective-permute-start.7 = (bf16[4,64,256]{2,1,0:T(8,128)(2,1)S(1)}, bf16[4,64,256]{2,1,0:T(8,128)(2,1)S(1)}, u32[]{:S(2)}, u32[]{:S(2)}) collective-permute-start(bf16[4,64,256]{2,1,0:T(8,128)(2,1)S(1)} %all_to_all.20.block_ref), channel_id=1, source_target_pairs={{0,496},{8,504},{16,32},{24,40},{32,16},{40,24},{48,64},{56,72},{6... | collective-permute-start | bytes 393224 | tf_op jit(solution)/shard_map/ppermute | solution.py:180
  79.8 6.1 %collective-permute-start.8 = (bf16[4,64,256]{2,1,0:T(8,128)(2,1)S(1)}, bf16[4,64,256]{2,1,0:T(8,128)(2,1)S(1)}, u32[]{:S(2)}, u32[]{:S(2)}) collective-permute-start(bf16[4,64,256]{2,1,0:T(8,128)(2,1)S(1)} %all_to_all.20.block_ref), channel_id=1, source_target_pairs={{0,16},{8,24},{16,0},{24,8},{32,48},{40,56},{48,32},{56,40},{64,80... | collective-permute-start | bytes 393224 | tf_op jit(solution)/shard_map/ppermute | solution.py:180
  87.6 14.6 %all-to-all-start.2 = ((f32[32,4,128]{2,1,0:T(4,128)}), f32[32,4,128]{2,1,0:T(4,128)S(1)}, u32[]{:S(2)}, u32[]{:S(2)}) async-start(f32[32,4,128]{2,1,0:T(4,128)} %broadcast_in_dim.13), calls=%async_computation.2 | async-start | bytes 131072 | tf_op jit(solution)/shard_map/all_to_all | solution.py:173
  102.9 15.4 %all-to-all-start.3 = ((f32[16,4,128]{2,1,0:T(4,128)}), f32[16,4,128]{2,1,0:T(4,128)S(1)}, u32[]{:S(2)}, u32[]{:S(2)}) async-start(f32[16,4,128]{2,1,0:T(4,128)} %broadcast_in_dim.14), calls=%async_computation.3 | async-start | bytes 65536 | tf_op jit(solution)/shard_map/all_to_all | solution.py:173
  110.8 9.5 %collective-permute-start.9 = (f32[64,256]{1,0:T(8,128)S(1)}, f32[64,256]{1,0:T(8,128)S(1)}, u32[]{:S(2)}, u32[]{:S(2)}) collective-permute-start(f32[64,256]{1,0:T(8,128)S(1)} %slice.63), channel_id=1, source_target_pairs={{0,1},{1,0},{2,3},{3,2},{4,5},{5,4},{6,7},{7,6},{8,9},{9,8},{10,11... | collective-permute-start | bytes 196616 | tf_op jit(solution)/shard_map/ppermute | solution.py:194

commit v11 on v10

--- a/solution.py
+++ b/solution.py
@@ -240,7 +240,7 @@
         early, noise, targets, image, first_total, both, images, own, peer
     )
     second = noise * image + (first_total - summed(own, peer)) * (1.0 / SIGMA)
-    for axes in (("x", "y_hi", "y_lo"), ("z", "core")):
+    for axes in (("z", "core"), ("x", "y_hi", "y_lo")):
         sums = jnp.sum(gathered(sums, axes), axis=0)
 
     (rr, rq), (qq, _), (rs, qs) = ((sums[i, :RHS], sums[i, RHS:]) for i in range(3))

time: 122 us -> 120 us (0.984)
  blocking collectives: 25.5 us -> 22.3 us
  waiting for transfers between devices: 14.7 us -> 11.6 us
  starting transfers between devices: 64 us -> 67 us
    ppermute x2, starting transfers between devices: 7.34 us -> 11.8 us  [summed(): return total[:, :WIDTH] + lax.ppermute(total[:, WIDTH:], 'y_hi', SWAP)]
    all_gather x2, blocking collectives: 7.13 us -> 3.99 us  [summed(): lent = lax.all_gather(peer, 'core')]
    ppermute x2, waiting for transfers between devices: 6.04 us -> 4.34 us  [summed(): return total[:, :WIDTH] + lax.ppermute(total[:, WIDTH:], 'y_hi', SWAP)]
    all_to_all x3, starting transfers between devices: 18.5 us -> 17.1 us  [gathered(): lax.all_to_all(jnp.broadcast_to(value[None], (count,) + value.shape), axe...]
    all_to_all x3, waiting for transfers between devices: 8.59 us -> 7.25 us  [gathered(): lax.all_to_all(jnp.broadcast_to(value[None], (count,) + value.shape), axe...]
where the time goes in v11:
time: 120 us; the launch traced here: 118 us
  starting transfers between devices  67 us (56%)
  blocking collectives  22.3 us (19%)
  waiting for transfers between devices  11.6 us (10%)
  Pallas kernels  11.3 us (9%)
  other arithmetic  2.74 us (2%)
  local copies, waits for them, and re-layouts  2 us (2%)
    ppermute x6, starting transfers between devices, halo(): lax.ppermute(block, BLK, route)  26.6 us
    all_to_all x3, starting transfers between devices, gathered(): lax.all_to_all(jnp.broadcast_to(value[None], (count,) + value.shape), axe...  17.1 us
    ppermute x2, starting transfers between devices, summed(): return total[:, :WIDTH] + lax.ppermute(total[:, WIDTH:], 'y_hi', SWAP)  11.8 us
    all_to_all x1, blocking collectives, gathered(): lax.all_to_all(jnp.broadcast_to(value[None], (count,) + value.shape), axe...  9.98 us
    ppermute x1, starting transfers between devices, body(): across = lax.ppermute(known, 'y_hi', SWAP)  7.44 us
    all_to_all x3, waiting for transfers between devices, gathered(): lax.all_to_all(jnp.broadcast_to(value[None], (count,) + value.shape), axe...  7.25 us
    all_gather x1, blocking collectives, body(): both = lax.all_gather(jnp.stack([known, across]) * scale[:, None], 'core')  5.42 us
    pallas_call x2, Pallas kernels, body(): call(functools.partial(build_pair, second), (half, half, kernel_shape()),...  4.43 us
  transfers between devices with their start and end apart: 13, of which 4 were waited for; matrix products, arithmetic and copies ran while one was open for 0% of the time, Pallas kernels for 7%

profile of v11, /device:TPU:1, one launch (start us, length us, event | category | flops | bytes accessed | tf_op | source)
XLA Modules:
  0.0 118.0 jit_solution(6481587292158822681)
XLA Ops:
  2.9 4.8 %all-to-all-start = ((bf16[4,96,256]{2,1,0:T(8,128)(2,1)}), bf16[4,96,256]{2,1,0:T(8,128)(2,1)S(1)}, u32[]{:S(2)}, u32[]{:S(2)}) async-start(bf16[4,96,256]{2,1,0:T(8,128)(2,1)} %broadcast_in_dim.10), calls=%async_computation | async-start | bytes 393216 | tf_op jit(solution)/shard_map/all_to_all | solution.py:173
  7.8 7.4 %collective-permute-start = (f32[96,256]{1,0:T(8,128)S(1)}, f32[96,256]{1,0:T(8,128)S(1)}, u32[]{:S(2)}, u32[]{:S(2)}) collective-permute-start(f32[96,256]{1,0:T(8,128)S(1)} %pad_maximum_fusion.1), channel_id=1, source_target_pairs={{0,1},{1,0},{2,3},{3,2},{4,5},{5,4},{6,7},{7,6},{8,9},{9,8},{10,11... | collective-permute-start | bytes 294920 | tf_op jit(solution)/shard_map/ppermute | solution.py:201
  15.2 4.0 %collective-permute-start.1 = (bf16[4,96,256]{2,1,0:T(8,128)(2,1)S(1)}, bf16[4,96,256]{2,1,0:T(8,128)(2,1)S(1)}, u32[]{:S(2)}, u32[]{:S(2)}) collective-permute-start(bf16[4,96,256]{2,1,0:T(8,128)(2,1)S(1)} %all-to-all-done.block_ref), channel_id=1, source_target_pairs={{0,16},{8,24},{16,0},{24,8},{32,48},{40,56},{48,32},{56,40},{64,80... | collective-permute-start | bytes 589832 | tf_op jit(solution)/shard_map/ppermute | solution.py:180
  19.2 9.6 %collective-permute-start.2 = (bf16[4,96,256]{2,1,0:T(8,128)(2,1)S(1)}, bf16[4,96,256]{2,1,0:T(8,128)(2,1)S(1)}, u32[]{:S(2)}, u32[]{:S(2)}) collective-permute-start(bf16[4,96,256]{2,1,0:T(8,128)(2,1)S(1)} %all-to-all-done.block_ref), channel_id=1, source_target_pairs={{0,496},{8,504},{16,32},{24,40},{32,16},{40,24},{48,64},{56,72},{6... | collective-permute-start | bytes 589832 | tf_op jit(solution)/shard_map/ppermute | solution.py:180
  28.8 1.9 %collective-permute-start.3 = (bf16[4,96,256]{2,1,0:T(8,128)(2,1)S(1)}, bf16[4,96,256]{2,1,0:T(8,128)(2,1)S(1)}, u32[]{:S(2)}, u32[]{:S(2)}) collective-permute-start(bf16[4,96,256]{2,1,0:T(8,128)(2,1)S(1)} %all-to-all-done.block_ref), channel_id=1, source_target_pairs={{0,480},{8,40},{16,496},{24,56},{32,0},{40,72},{48,16},{56,88},{64... | collective-permute-start | bytes 589832 | tf_op jit(solution)/shard_map/ppermute | solution.py:180
  30.9 5.4 %all_gather.22.both_ref.firsts_ref = f32[2,2,96,256]{3,2,1,0:T(8,128)S(1)} all-gather(f32[1,2,96,256]{3,2,1,0:T(8,128)S(1)} %maximum_multiply_fusion), channel_id=1, replica_groups=mesh['y_lo'=4,'z'=8,'core'=2,'x'=4,'y_hi'=2] {'core'}, dimensions={0}, use_global_device_ids=true | all-gather | bytes 589824 | tf_op jit(solution)/shard_map/all_gather | solution.py:203
  36.3 2.3 %shard_map.59 = (bf16[1024,80]{1,0:T(8,128)(2,1)S(1)}, f32[64,512]{1,0:T(8,128)S(1)}, f32[64,512]{1,0:T(8,128)S(1)}, bf16[4,1024,256]{2,1,0:T(8,128)(2,1)S(1)}) custom-call(f32[2,2,96,256]{3,2,1,0:T(8,128)S(1)} %all_gather.22.both_ref.firsts_ref, bf16[4,96,256]{2,1,0:T(8,128)(2,1)S(1)} %all-to-all-done.block_ref), custom_call_target="tpu_custom_call" | custom-call | tf_op jit(solution)/shard_map/pallas_call | solution.py:207
  38.6 2.2 %shard_map.60 = (f32[64,512]{1,0:T(8,128)S(1)}, f32[64,512]{1,0:T(8,128)S(1)}, bf16[4,1024,256]{2,1,0:T(8,128)(2,1)S(1)}) custom-call(bf16[1024,80]{1,0:T(8,128)(2,1)S(1)} %get-tuple-element.22.weights_ref, f32[64,512]{1,0:T(8,128)S(1)} %get-tuple-element.23.own_before, f32[64,512]{1,0:T(8,128)S(1)} %get-tuple-element.24.peer_before, ...), custom_call_target="tpu_custom_call" | custom-call | tf_op jit(solution)/shard_map/pallas_call | solution.py:220
  40.9 2.2 %shard_map.61 = (f32[64,512]{1,0:T(8,128)S(1)}, f32[64,512]{1,0:T(8,128)S(1)}, bf16[4,1024,256]{2,1,0:T(8,128)(2,1)S(1)}) custom-call(bf16[1024,80]{1,0:T(8,128)(2,1)S(1)} %get-tuple-element.22.weights_ref, f32[64,512]{1,0:T(8,128)S(1)} %get-tuple-element.25.own_before, f32[64,512]{1,0:T(8,128)S(1)} %get-tuple-element.26.peer_before, ...), custom_call_target="tpu_custom_call" | custom-call | tf_op jit(solution)/shard_map/pallas_call | solution.py:220
  44.4 2.0 %all-gather = f32[128,512]{1,0:T(8,128)S(1)} all-gather(f32[64,512]{1,0:T(8,128)S(1)} %get-tuple-element.29), channel_id=2, replica_groups=mesh['y_lo'=4,'z'=8,'core'=2,'x'=4,'y_hi'=2] {'core'}, dimensions={0}, use_global_device_ids=true | all-gather | bytes 393216 | tf_op jit(solution)/shard_map/all_gather | solution.py:192
  46.5 4.8 %collective-permute-start.4 = (f32[64,256]{1,0:T(8,128)S(1)}, f32[64,256]{1,0:T(8,128)S(1)}, u32[]{:S(2)}, u32[]{:S(2)}) collective-permute-start(f32[64,256]{1,0:T(8,128)S(1)} %slice.59), channel_id=1, source_target_pairs={{0,1},{1,0},{2,3},{3,2},{4,5},{5,4},{6,7},{7,6},{8,9},{9,8},{10,11... | collective-permute-start | bytes 196616 | tf_op jit(solution)/shard_map/ppermute | solution.py:194
  51.2 4.2 %collective-permute-done.4 = f32[64,256]{1,0:T(8,128)S(1)} collective-permute-done((f32[64,256]{1,0:T(8,128)S(1)}, f32[64,256]{1,0:T(8,128)S(1)}, u32[]{:S(2)}, u32[]{:S(2)}) %collective-permute-start.4) | collective-permute-done | bytes 65568 | tf_op jit(solution)/shard_map/ppermute | solution.py:194
  55.4 10.0 %all_to_all.20.block_ref = bf16[4,64,256]{2,1,0:T(8,128)(2,1)S(1)} all-to-all(bf16[4,64,256]{2,1,0:T(8,128)(2,1)S(1)} %broadcast_in_dim.12), channel_id=1, replica_groups=mesh['y_lo'=4,'z'=8,'core'=2,'x'=4,'y_hi'=2] {'x'}, dimensions={0} | all-to-all | bytes 262144 | tf_op jit(solution)/shard_map/all_to_all | solution.py:173
  66.1 4.1 %collective-permute-start.5 = (f32[64,256]{1,0:T(8,128)S(1)}, f32[64,256]{1,0:T(8,128)S(1)}, u32[]{:S(2)}, u32[]{:S(2)}) collective-permute-start(f32[64,256]{1,0:T(8,128)S(1)} %get-tuple-element.32.image_ref), channel_id=1, source_target_pairs={{0,1},{1,0},{2,3},{3,2},{4,5},{5,4},{6,7},{7,6},{8,9},{9,8},{10,11... | collective-permute-start | bytes 196616 | tf_op jit(solution)/shard_map/ppermute | solution.py:232
  70.6 3.6 %collective-permute-start.6 = (bf16[4,64,256]{2,1,0:T(8,128)(2,1)S(1)}, bf16[4,64,256]{2,1,0:T(8,128)(2,1)S(1)}, u32[]{:S(2)}, u32[]{:S(2)}) collective-permute-start(bf16[4,64,256]{2,1,0:T(8,128)(2,1)S(1)} %all_to_all.20.block_ref), channel_id=1, source_target_pairs={{0,480},{8,40},{16,496},{24,56},{32,0},{40,72},{48,16},{56,88},{64... | collective-permute-start | bytes 393224 | tf_op jit(solution)/shard_map/ppermute | solution.py:180
  74.2 5.5 %collective-permute-start.7 = (bf16[4,64,256]{2,1,0:T(8,128)(2,1)S(1)}, bf16[4,64,256]{2,1,0:T(8,128)(2,1)S(1)}, u32[]{:S(2)}, u32[]{:S(2)}) collective-permute-start(bf16[4,64,256]{2,1,0:T(8,128)(2,1)S(1)} %all_to_all.20.block_ref), channel_id=1, source_target_pairs={{0,496},{8,504},{16,32},{24,40},{32,16},{40,24},{48,64},{56,72},{6... | collective-permute-start | bytes 393224 | tf_op jit(solution)/shard_map/ppermute | solution.py:180
  79.8 1.9 %collective-permute-start.8 = (bf16[4,64,256]{2,1,0:T(8,128)(2,1)S(1)}, bf16[4,64,256]{2,1,0:T(8,128)(2,1)S(1)}, u32[]{:S(2)}, u32[]{:S(2)}) collective-permute-start(bf16[4,64,256]{2,1,0:T(8,128)(2,1)S(1)} %all_to_all.20.block_ref), channel_id=1, source_target_pairs={{0,16},{8,24},{16,0},{24,8},{32,48},{40,56},{48,32},{56,40},{64,80... | collective-permute-start | bytes 393224 | tf_op jit(solution)/shard_map/ppermute | solution.py:180
  81.7 2.9 %all-gather.1 = f32[4,64,256]{2,1,0:T(8,128)S(1)} all-gather(f32[2,64,256]{2,1,0:T(8,128)S(1)} %pad_maximum_fusion), channel_id=3, replica_groups=mesh['y_lo'=4,'z'=8,'core'=2,'x'=4,'y_hi'=2] {'core'}, dimensions={0}, use_global_device_ids=true | all-gather | bytes 393216 | tf_op jit(solution)/shard_map/all_gather | solution.py:233
  87.6 8.1 %all-to-all-start.2 = ((f32[16,4,128]{2,1,0:T(4,128)}), f32[16,4,128]{2,1,0:T(4,128)S(1)}, u32[]{:S(2)}, u32[]{:S(2)}) async-start(f32[16,4,128]{2,1,0:T(4,128)} %broadcast_in_dim.13), calls=%async_computation.2 | async-start | bytes 65536 | tf_op jit(solution)/shard_map/all_to_all | solution.py:173
  95.7 2.0 %all-gather.2 = f32[128,512]{1,0:T(8,128)S(1)} all-gather(f32[64,512]{1,0:T(8,128)S(1)} %get-tuple-element.41.peer_ref), channel_id=4, replica_groups=mesh['y_lo'=4,'z'=8,'core'=2,'x'=4,'y_hi'=2] {'core'}, dimensions={0}, use_global_device_ids=true | all-gather | bytes 393216 | tf_op jit(solution)/shard_map/all_gather | solution.py:192
  97.7 5.5 %all-to-all-done.2 = f32[16,4,128]{2,1,0:T(4,128)S(1)} async-done(((f32[16,4,128]{2,1,0:T(4,128)}), f32[16,4,128]{2,1,0:T(4,128)S(1)}, u32[]{:S(2)}, u32[]{:S(2)}) %all-to-all-start.2) | async-done | bytes 32800 | tf_op jit(solution)/shard_map/all_to_all | solution.py:173
  103.8 4.1 %all-to-all-start.3 = ((f32[32,4,128]{2,1,0:T(4,128)}), f32[32,4,128]{2,1,0:T(4,128)S(1)}, u32[]{:S(2)}, u32[]{:S(2)}) async-start(f32[32,4,128]{2,1,0:T(4,128)} %broadcast_in_dim.14), calls=%async_computation.3 | async-start | bytes 131072 | tf_op jit(solution)/shard_map/all_to_all | solution.py:173
  108.0 7.0 %collective-permute-start.9 = (f32[64,256]{1,0:T(8,128)S(1)}, f32[64,256]{1,0:T(8,128)S(1)}, u32[]{:S(2)}, u32[]{:S(2)}) collective-permute-start(f32[64,256]{1,0:T(8,128)S(1)} %slice.63), channel_id=1, source_target_pairs={{0,1},{1,0},{2,3},{3,2},{4,5},{5,4},{6,7},{7,6},{8,9},{9,8},{10,11... | collective-permute-start | bytes 196616 | tf_op jit(solution)/shard_map/ppermute | solution.py:194
  115.1 1.8 %all-to-all-done.3 = f32[32,4,128]{2,1,0:T(4,128)S(1)} async-done(((f32[32,4,128]{2,1,0:T(4,128)}), f32[32,4,128]{2,1,0:T(4,128)S(1)}, u32[]{:S(2)}, u32[]{:S(2)}) %all-to-all-start.3) | async-done | bytes 65568 | tf_op jit(solution)/shard_map/all_to_all | solution.py:173
  (41 shorter events, 9.6 us)
Async XLA Ops:
  2.9 12.3 %all-to-all-start = ((bf16[4,96,256]{2,1,0:T(8,128)(2,1)}), bf16[4,96,256]{2,1,0:T(8,128)(2,1)S(1)}, u32[]{:S(2)}, u32[]{:S(2)}) async-start(bf16[4,96,256]{2,1,0:T(8,128)(2,1)} %broadcast_in_dim.10), calls=%async_computation | async-start | bytes 393216 | tf_op jit(solution)/shard_map/all_to_all | solution.py:173
  7.8 23.0 %collective-permute-start = (f32[96,256]{1,0:T(8,128)S(1)}, f32[96,256]{1,0:T(8,128)S(1)}, u32[]{:S(2)}, u32[]{:S(2)}) collective-permute-start(f32[96,256]{1,0:T(8,128)S(1)} %pad_maximum_fusion.1), channel_id=1, source_target_pairs={{0,1},{1,0},{2,3},{3,2},{4,5},{5,4},{6,7},{7,6},{8,9},{9,8},{10,11... | collective-permute-start | bytes 294920 | tf_op jit(solution)/shard_map/ppermute | solution.py:201
  15.2 23.4 %collective-permute-start.1 = (bf16[4,96,256]{2,1,0:T(8,128)(2,1)S(1)}, bf16[4,96,256]{2,1,0:T(8,128)(2,1)S(1)}, u32[]{:S(2)}, u32[]{:S(2)}) collective-permute-start(bf16[4,96,256]{2,1,0:T(8,128)(2,1)S(1)} %all-to-all-done.block_ref), channel_id=1, source_target_pairs={{0,16},{8,24},{16,0},{24,8},{32,48},{40,56},{48,32},{56,40},{64,80... | collective-permute-start | bytes 589832 | tf_op jit(solution)/shard_map/ppermute | solution.py:180
  19.2 21.6 %collective-permute-start.2 = (bf16[4,96,256]{2,1,0:T(8,128)(2,1)S(1)}, bf16[4,96,256]{2,1,0:T(8,128)(2,1)S(1)}, u32[]{:S(2)}, u32[]{:S(2)}) collective-permute-start(bf16[4,96,256]{2,1,0:T(8,128)(2,1)S(1)} %all-to-all-done.block_ref), channel_id=1, source_target_pairs={{0,496},{8,504},{16,32},{24,40},{32,16},{40,24},{48,64},{56,72},{6... | collective-permute-start | bytes 589832 | tf_op jit(solution)/shard_map/ppermute | solution.py:180
  28.8 14.3 %collective-permute-start.3 = (bf16[4,96,256]{2,1,0:T(8,128)(2,1)S(1)}, bf16[4,96,256]{2,1,0:T(8,128)(2,1)S(1)}, u32[]{:S(2)}, u32[]{:S(2)}) collective-permute-start(bf16[4,96,256]{2,1,0:T(8,128)(2,1)S(1)} %all-to-all-done.block_ref), channel_id=1, source_target_pairs={{0,480},{8,40},{16,496},{24,56},{32,0},{40,72},{48,16},{56,88},{64... | collective-permute-start | bytes 589832 | tf_op jit(solution)/shard_map/ppermute | solution.py:180
  30.9 24.5 %copy-start = (f32[64,256]{1,0:T(8,128)S(1)}, f32[64,256]{1,0:T(8,128)}, u32[]{:S(2)}) copy-start(f32[64,256]{1,0:T(8,128)} %first_ref.3) | copy-start | bytes 196612
  30.9 24.5 %copy-start.1 = (f32[256]{0:T(256)S(1)}, f32[256]{0:T(256)}, u32[]{:S(2)}) copy-start(f32[256]{0:T(256)} %param.6) | copy-start | bytes 3076
  46.5 8.9 %collective-permute-start.4 = (f32[64,256]{1,0:T(8,128)S(1)}, f32[64,256]{1,0:T(8,128)S(1)}, u32[]{:S(2)}, u32[]{:S(2)}) collective-permute-start(f32[64,256]{1,0:T(8,128)S(1)} %slice.59), channel_id=1, source_target_pairs={{0,1},{1,0},{2,3},{3,2},{4,5},{5,4},{6,7},{7,6},{8,9},{9,8},{10,11... | collective-permute-start | bytes 196616 | tf_op jit(solution)/shard_map/ppermute | solution.py:194
  66.1 15.6 %collective-permute-start.5 = (f32[64,256]{1,0:T(8,128)S(1)}, f32[64,256]{1,0:T(8,128)S(1)}, u32[]{:S(2)}, u32[]{:S(2)}) collective-permute-start(f32[64,256]{1,0:T(8,128)S(1)} %get-tuple-element.32.image_ref), channel_id=1, source_target_pairs={{0,1},{1,0},{2,3},{3,2},{4,5},{5,4},{6,7},{7,6},{8,9},{9,8},{10,11... | collective-permute-start | bytes 196616 | tf_op jit(solution)/shard_map/ppermute | solution.py:232
  70.6 14.1 %collective-permute-start.6 = (bf16[4,64,256]{2,1,0:T(8,128)(2,1)S(1)}, bf16[4,64,256]{2,1,0:T(8,128)(2,1)S(1)}, u32[]{:S(2)}, u32[]{:S(2)}) collective-permute-start(bf16[4,64,256]{2,1,0:T(8,128)(2,1)S(1)} %all_to_all.20.block_ref), channel_id=1, source_target_pairs={{0,480},{8,40},{16,496},{24,56},{32,0},{40,72},{48,16},{56,88},{64... | collective-permute-start | bytes 393224 | tf_op jit(solution)/shard_map/ppermute | solution.py:180
  74.2 10.9 %collective-permute-start.7 = (bf16[4,64,256]{2,1,0:T(8,128)(2,1)S(1)}, bf16[4,64,256]{2,1,0:T(8,128)(2,1)S(1)}, u32[]{:S(2)}, u32[]{:S(2)}) collective-permute-start(bf16[4,64,256]{2,1,0:T(8,128)(2,1)S(1)} %all_to_all.20.block_ref), channel_id=1, source_target_pairs={{0,496},{8,504},{16,32},{24,40},{32,16},{40,24},{48,64},{56,72},{6... | collective-permute-start | bytes 393224 | tf_op jit(solution)/shard_map/ppermute | solution.py:180
  79.8 6.1 %collective-permute-start.8 = (bf16[4,64,256]{2,1,0:T(8,128)(2,1)S(1)}, bf16[4,64,256]{2,1,0:T(8,128)(2,1)S(1)}, u32[]{:S(2)}, u32[]{:S(2)}) collective-permute-start(bf16[4,64,256]{2,1,0:T(8,128)(2,1)S(1)} %all_to_all.20.block_ref), channel_id=1, source_target_pairs={{0,16},{8,24},{16,0},{24,8},{32,48},{40,56},{48,32},{56,40},{64,80... | collective-permute-start | bytes 393224 | tf_op jit(solution)/shard_map/ppermute | solution.py:180
  87.6 15.6 %all-to-all-start.2 = ((f32[16,4,128]{2,1,0:T(4,128)}), f32[16,4,128]{2,1,0:T(4,128)S(1)}, u32[]{:S(2)}, u32[]{:S(2)}) async-start(f32[16,4,128]{2,1,0:T(4,128)} %broadcast_in_dim.13), calls=%async_computation.2 | async-start | bytes 65536 | tf_op jit(solution)/shard_map/all_to_all | solution.py:173
  103.8 13.0 %all-to-all-start.3 = ((f32[32,4,128]{2,1,0:T(4,128)}), f32[32,4,128]{2,1,0:T(4,128)S(1)}, u32[]{:S(2)}, u32[]{:S(2)}) async-start(f32[32,4,128]{2,1,0:T(4,128)} %broadcast_in_dim.14), calls=%async_computation.3 | async-start | bytes 131072 | tf_op jit(solution)/shard_map/all_to_all | solution.py:173
  108.0 9.2 %collective-permute-start.9 = (f32[64,256]{1,0:T(8,128)S(1)}, f32[64,256]{1,0:T(8,128)S(1)}, u32[]{:S(2)}, u32[]{:S(2)}) collective-permute-start(f32[64,256]{1,0:T(8,128)S(1)} %slice.63), channel_id=1, source_target_pairs={{0,1},{1,0},{2,3},{3,2},{4,5},{5,4},{6,7},{7,6},{8,9},{9,8},{10,11... | collective-permute-start | bytes 196616 | tf_op jit(solution)/shard_map/ppermute | solution.py:194

commit v12 on v11

--- a/solution.py
+++ b/solution.py
@@ -33,6 +33,17 @@
 ROWS = 2 * WIDTH
 SIGMA = 0.5
 NT = (((1,), (1,)), ((), ()))
+
+
+def prepare(known_ref, scale_ref, exact_ref, message_ref):
+    row = lax.broadcasted_iota(jnp.int32, (FEAT, FEAT), 0)
+    column = lax.broadcasted_iota(jnp.int32, (FEAT, FEAT), 1)
+    scale = jnp.sum(jnp.where(row == column, scale_ref[...], 0.0), axis=1, keepdims=True)
+    exact_ref[:FEAT] = known_ref[:FEAT] * (GRID / scale)
+    exact_ref[FEAT:] = known_ref[FEAT:]
+    message = exact_ref[...].astype(BF16)
+    for i in range(SHARDS):
+        message_ref[i] = message
 
 
 def square_rows(coords, first, second):
@@ -195,12 +206,13 @@
 
 
 def body(points, lengthscale, noise_var, targets):
-    scale = GRID / jnp.pad(lengthscale, (0, RHS), constant_values=GRID)
-    known = lax.optimization_barrier(jnp.concatenate([points, targets], axis=0))
-    exact = known * scale[:, None]
-    across = lax.ppermute(known, "y_hi", SWAP)
-    block = gathered(exact.astype(BF16), ("x",))
-    both = lax.all_gather(jnp.stack([known, across]) * scale[:, None], "core")
+    known = jnp.concatenate([points, targets], axis=0)
+    exact, message = call(
+        prepare, (shape(FEAT + RHS, WIDTH), shape(SHARDS, FEAT + RHS, WIDTH, dtype=BF16))
+    )(known, lengthscale[None])
+    across = lax.ppermute(exact, "y_hi", SWAP)
+    block = lax.all_to_all(message, ("x",), 0, 0)
+    both = lax.all_gather(jnp.stack([exact, across]), "core")
     far, *pairs = halo(block)
 
     half = shape(RHS, ROWS)

time: 120 us -> 120 us (level)
    all_to_all x3 -> x2, starting transfers between devices: 17.1 us -> 12.2 us  [gathered(): lax.all_to_all(jnp.broadcast_to(value[None], (count,) + value.shape), axe...]
    all_to_all x0 -> x1, starting transfers between devices: none -> 4.84 us  [body(): block = lax.all_to_all(message, ('x',), 0, 0)]
    all_to_all x3 -> x2, waiting for transfers between devices: 7.25 us -> 7.25 us  [gathered(): lax.all_to_all(jnp.broadcast_to(value[None], (count,) + value.shape), axe...]
where the time goes in v12:
time: 120 us; the launch traced here: 118 us
  starting transfers between devices  67 us (56%)
  blocking collectives  22.3 us (19%)
  Pallas kernels  12.1 us (10%)
  waiting for transfers between devices  11.6 us (10%)
  local copies, waits for them, and re-layouts  1.97 us (2%)
  other arithmetic  1.93 us (2%)
    ppermute x6, starting transfers between devices, halo(): lax.ppermute(block, BLK, route)  26.6 us
    all_to_all x2, starting transfers between devices, gathered(): lax.all_to_all(jnp.broadcast_to(value[None], (count,) + value.shape), axe...  12.2 us
    ppermute x2, starting transfers between devices, summed(): return total[:, :WIDTH] + lax.ppermute(total[:, WIDTH:], 'y_hi', SWAP)  11.8 us
    all_to_all x1, blocking collectives, gathered(): lax.all_to_all(jnp.broadcast_to(value[None], (count,) + value.shape), axe...  9.98 us
    ppermute x1, starting transfers between devices, body(): across = lax.ppermute(exact, 'y_hi', SWAP)  7.44 us
    all_to_all x2, waiting for transfers between devices, gathered(): lax.all_to_all(jnp.broadcast_to(value[None], (count,) + value.shape), axe...  7.25 us
    all_gather x1, blocking collectives, body(): both = lax.all_gather(jnp.stack([exact, across]), 'core')  5.42 us
    all_to_all x1, starting transfers between devices, body(): block = lax.all_to_all(message, ('x',), 0, 0)  4.84 us
  transfers between devices with their start and end apart: 13, of which 4 were waited for; matrix products, arithmetic and copies ran while one was open for 0% of the time, Pallas kernels for 7%

profile of v12, /device:TPU:1, one launch (start us, length us, event | category | flops | bytes accessed | tf_op | source)
XLA Modules:
  0.0 117.9 jit_solution(12282892493514973880)
XLA Ops:
  2.9 4.8 %all-to-all-start = ((bf16[4,96,256]{2,1,0:T(8,128)(2,1)}), bf16[4,96,256]{2,1,0:T(8,128)(2,1)S(1)}, u32[]{:S(2)}, u32[]{:S(2)}) async-start(bf16[4,96,256]{2,1,0:T(8,128)(2,1)} %get-tuple-element.25), calls=%async_computation | async-start | bytes 393216 | tf_op jit(solution)/shard_map/all_to_all | solution.py:214
  7.7 7.4 %collective-permute-start = (f32[96,256]{1,0:T(8,128)S(1)}, f32[96,256]{1,0:T(8,128)S(1)}, u32[]{:S(2)}, u32[]{:S(2)}) collective-permute-start(f32[96,256]{1,0:T(8,128)S(1)} %get-tuple-element.24), channel_id=1, source_target_pairs={{0,1},{1,0},{2,3},{3,2},{4,5},{5,4},{6,7},{7,6},{8,9},{9,8},{10,11... | collective-permute-start | bytes 294920 | tf_op jit(solution)/shard_map/ppermute | solution.py:213
  15.2 4.0 %collective-permute-start.1 = (bf16[4,96,256]{2,1,0:T(8,128)(2,1)S(1)}, bf16[4,96,256]{2,1,0:T(8,128)(2,1)S(1)}, u32[]{:S(2)}, u32[]{:S(2)}) collective-permute-start(bf16[4,96,256]{2,1,0:T(8,128)(2,1)S(1)} %all-to-all-done.block_ref), channel_id=1, source_target_pairs={{0,16},{8,24},{16,0},{24,8},{32,48},{40,56},{48,32},{56,40},{64,80... | collective-permute-start | bytes 589832 | tf_op jit(solution)/shard_map/ppermute | solution.py:191
  19.2 9.6 %collective-permute-start.2 = (bf16[4,96,256]{2,1,0:T(8,128)(2,1)S(1)}, bf16[4,96,256]{2,1,0:T(8,128)(2,1)S(1)}, u32[]{:S(2)}, u32[]{:S(2)}) collective-permute-start(bf16[4,96,256]{2,1,0:T(8,128)(2,1)S(1)} %all-to-all-done.block_ref), channel_id=1, source_target_pairs={{0,496},{8,504},{16,32},{24,40},{32,16},{40,24},{48,64},{56,72},{6... | collective-permute-start | bytes 589832 | tf_op jit(solution)/shard_map/ppermute | solution.py:191
  28.8 1.9 %collective-permute-start.3 = (bf16[4,96,256]{2,1,0:T(8,128)(2,1)S(1)}, bf16[4,96,256]{2,1,0:T(8,128)(2,1)S(1)}, u32[]{:S(2)}, u32[]{:S(2)}) collective-permute-start(bf16[4,96,256]{2,1,0:T(8,128)(2,1)S(1)} %all-to-all-done.block_ref), channel_id=1, source_target_pairs={{0,480},{8,40},{16,496},{24,56},{32,0},{40,72},{48,16},{56,88},{64... | collective-permute-start | bytes 589832 | tf_op jit(solution)/shard_map/ppermute | solution.py:191
  30.8 5.4 %all-gather = f32[4,96,256]{2,1,0:T(8,128)S(1)} all-gather(f32[2,96,256]{2,1,0:T(8,128)S(1)} %pad_maximum_fusion), channel_id=2, replica_groups=mesh['y_lo'=4,'z'=8,'core'=2,'x'=4,'y_hi'=2] {'core'}, dimensions={0}, use_global_device_ids=true | all-gather | bytes 589824 | tf_op jit(solution)/shard_map/all_gather | solution.py:215
  36.2 2.3 %shard_map.60 = (bf16[1024,80]{1,0:T(8,128)(2,1)S(1)}, f32[64,512]{1,0:T(8,128)S(1)}, f32[64,512]{1,0:T(8,128)S(1)}, bf16[4,1024,256]{2,1,0:T(8,128)(2,1)S(1)}) custom-call(f32[2,2,96,256]{3,2,1,0:T(8,128)S(1)} %bitcast.56, bf16[4,96,256]{2,1,0:T(8,128)(2,1)S(1)} %all-to-all-done.block_ref), custom_call_target="tpu_custom_call" | custom-call | tf_op jit(solution)/shard_map/pallas_call | solution.py:219
  38.6 2.2 %shard_map.61 = (f32[64,512]{1,0:T(8,128)S(1)}, f32[64,512]{1,0:T(8,128)S(1)}, bf16[4,1024,256]{2,1,0:T(8,128)(2,1)S(1)}) custom-call(bf16[1024,80]{1,0:T(8,128)(2,1)S(1)} %get-tuple-element.26.weights_ref, f32[64,512]{1,0:T(8,128)S(1)} %get-tuple-element.27.own_before, f32[64,512]{1,0:T(8,128)S(1)} %get-tuple-element.28.peer_before, ...), custom_call_target="tpu_custom_call" | custom-call | tf_op jit(solution)/shard_map/pallas_call | solution.py:232
  40.8 2.2 %shard_map.62 = (f32[64,512]{1,0:T(8,128)S(1)}, f32[64,512]{1,0:T(8,128)S(1)}, bf16[4,1024,256]{2,1,0:T(8,128)(2,1)S(1)}) custom-call(bf16[1024,80]{1,0:T(8,128)(2,1)S(1)} %get-tuple-element.26.weights_ref, f32[64,512]{1,0:T(8,128)S(1)} %get-tuple-element.29.own_before, f32[64,512]{1,0:T(8,128)S(1)} %get-tuple-element.30.peer_before, ...), custom_call_target="tpu_custom_call" | custom-call | tf_op jit(solution)/shard_map/pallas_call | solution.py:232
  44.3 2.0 %all-gather.1 = f32[128,512]{1,0:T(8,128)S(1)} all-gather(f32[64,512]{1,0:T(8,128)S(1)} %get-tuple-element.33), channel_id=3, replica_groups=mesh['y_lo'=4,'z'=8,'core'=2,'x'=4,'y_hi'=2] {'core'}, dimensions={0}, use_global_device_ids=true | all-gather | bytes 393216 | tf_op jit(solution)/shard_map/all_gather | solution.py:203
  46.4 4.8 %collective-permute-start.4 = (f32[64,256]{1,0:T(8,128)S(1)}, f32[64,256]{1,0:T(8,128)S(1)}, u32[]{:S(2)}, u32[]{:S(2)}) collective-permute-start(f32[64,256]{1,0:T(8,128)S(1)} %slice.59), channel_id=1, source_target_pairs={{0,1},{1,0},{2,3},{3,2},{4,5},{5,4},{6,7},{7,6},{8,9},{9,8},{10,11... | collective-permute-start | bytes 196616 | tf_op jit(solution)/shard_map/ppermute | solution.py:205
  51.1 4.2 %collective-permute-done.4 = f32[64,256]{1,0:T(8,128)S(1)} collective-permute-done((f32[64,256]{1,0:T(8,128)S(1)}, f32[64,256]{1,0:T(8,128)S(1)}, u32[]{:S(2)}, u32[]{:S(2)}) %collective-permute-start.4) | collective-permute-done | bytes 65568 | tf_op jit(solution)/shard_map/ppermute | solution.py:205
  55.3 10.0 %all_to_all.20.block_ref = bf16[4,64,256]{2,1,0:T(8,128)(2,1)S(1)} all-to-all(bf16[4,64,256]{2,1,0:T(8,128)(2,1)S(1)} %broadcast_in_dim.12), channel_id=1, replica_groups=mesh['y_lo'=4,'z'=8,'core'=2,'x'=4,'y_hi'=2] {'x'}, dimensions={0} | all-to-all | bytes 262144 | tf_op jit(solution)/shard_map/all_to_all | solution.py:184
  66.1 4.1 %collective-permute-start.5 = (f32[64,256]{1,0:T(8,128)S(1)}, f32[64,256]{1,0:T(8,128)S(1)}, u32[]{:S(2)}, u32[]{:S(2)}) collective-permute-start(f32[64,256]{1,0:T(8,128)S(1)} %get-tuple-element.36.image_ref), channel_id=1, source_target_pairs={{0,1},{1,0},{2,3},{3,2},{4,5},{5,4},{6,7},{7,6},{8,9},{9,8},{10,11... | collective-permute-start | bytes 196616 | tf_op jit(solution)/shard_map/ppermute | solution.py:244
  70.5 3.6 %collective-permute-start.6 = (bf16[4,64,256]{2,1,0:T(8,128)(2,1)S(1)}, bf16[4,64,256]{2,1,0:T(8,128)(2,1)S(1)}, u32[]{:S(2)}, u32[]{:S(2)}) collective-permute-start(bf16[4,64,256]{2,1,0:T(8,128)(2,1)S(1)} %all_to_all.20.block_ref), channel_id=1, source_target_pairs={{0,480},{8,40},{16,496},{24,56},{32,0},{40,72},{48,16},{56,88},{64... | collective-permute-start | bytes 393224 | tf_op jit(solution)/shard_map/ppermute | solution.py:191
  74.2 5.5 %collective-permute-start.7 = (bf16[4,64,256]{2,1,0:T(8,128)(2,1)S(1)}, bf16[4,64,256]{2,1,0:T(8,128)(2,1)S(1)}, u32[]{:S(2)}, u32[]{:S(2)}) collective-permute-start(bf16[4,64,256]{2,1,0:T(8,128)(2,1)S(1)} %all_to_all.20.block_ref), channel_id=1, source_target_pairs={{0,496},{8,504},{16,32},{24,40},{32,16},{40,24},{48,64},{56,72},{6... | collective-permute-start | bytes 393224 | tf_op jit(solution)/shard_map/ppermute | solution.py:191
  79.7 1.9 %collective-permute-start.8 = (bf16[4,64,256]{2,1,0:T(8,128)(2,1)S(1)}, bf16[4,64,256]{2,1,0:T(8,128)(2,1)S(1)}, u32[]{:S(2)}, u32[]{:S(2)}) collective-permute-start(bf16[4,64,256]{2,1,0:T(8,128)(2,1)S(1)} %all_to_all.20.block_ref), channel_id=1, source_target_pairs={{0,16},{8,24},{16,0},{24,8},{32,48},{40,56},{48,32},{56,40},{64,80... | collective-permute-start | bytes 393224 | tf_op jit(solution)/shard_map/ppermute | solution.py:191
  81.7 2.9 %all-gather.2 = f32[4,64,256]{2,1,0:T(8,128)S(1)} all-gather(f32[2,64,256]{2,1,0:T(8,128)S(1)} %pad_maximum_fusion.1), channel_id=4, replica_groups=mesh['y_lo'=4,'z'=8,'core'=2,'x'=4,'y_hi'=2] {'core'}, dimensions={0}, use_global_device_ids=true | all-gather | bytes 393216 | tf_op jit(solution)/shard_map/all_gather | solution.py:245
  87.5 8.1 %all-to-all-start.2 = ((f32[16,4,128]{2,1,0:T(4,128)}), f32[16,4,128]{2,1,0:T(4,128)S(1)}, u32[]{:S(2)}, u32[]{:S(2)}) async-start(f32[16,4,128]{2,1,0:T(4,128)} %broadcast_in_dim.13), calls=%async_computation.2 | async-start | bytes 65536 | tf_op jit(solution)/shard_map/all_to_all | solution.py:184
  95.6 2.0 %all-gather.3 = f32[128,512]{1,0:T(8,128)S(1)} all-gather(f32[64,512]{1,0:T(8,128)S(1)} %get-tuple-element.45.peer_ref), channel_id=5, replica_groups=mesh['y_lo'=4,'z'=8,'core'=2,'x'=4,'y_hi'=2] {'core'}, dimensions={0}, use_global_device_ids=true | all-gather | bytes 393216 | tf_op jit(solution)/shard_map/all_gather | solution.py:203
  97.6 5.5 %all-to-all-done.2 = f32[16,4,128]{2,1,0:T(4,128)S(1)} async-done(((f32[16,4,128]{2,1,0:T(4,128)}), f32[16,4,128]{2,1,0:T(4,128)S(1)}, u32[]{:S(2)}, u32[]{:S(2)}) %all-to-all-start.2) | async-done | bytes 32800 | tf_op jit(solution)/shard_map/all_to_all | solution.py:184
  103.8 4.1 %all-to-all-start.3 = ((f32[32,4,128]{2,1,0:T(4,128)}), f32[32,4,128]{2,1,0:T(4,128)S(1)}, u32[]{:S(2)}, u32[]{:S(2)}) async-start(f32[32,4,128]{2,1,0:T(4,128)} %broadcast_in_dim.14), calls=%async_computation.3 | async-start | bytes 131072 | tf_op jit(solution)/shard_map/all_to_all | solution.py:184
  107.9 7.0 %collective-permute-start.9 = (f32[64,256]{1,0:T(8,128)S(1)}, f32[64,256]{1,0:T(8,128)S(1)}, u32[]{:S(2)}, u32[]{:S(2)}) collective-permute-start(f32[64,256]{1,0:T(8,128)S(1)} %slice.63), channel_id=1, source_target_pairs={{0,1},{1,0},{2,3},{3,2},{4,5},{5,4},{6,7},{7,6},{8,9},{9,8},{10,11... | collective-permute-start | bytes 196616 | tf_op jit(solution)/shard_map/ppermute | solution.py:205
  115.0 1.8 %all-to-all-done.3 = f32[32,4,128]{2,1,0:T(4,128)S(1)} async-done(((f32[32,4,128]{2,1,0:T(4,128)}), f32[32,4,128]{2,1,0:T(4,128)S(1)}, u32[]{:S(2)}, u32[]{:S(2)}) %all-to-all-start.3) | async-done | bytes 65568 | tf_op jit(solution)/shard_map/all_to_all | solution.py:184
  (41 shorter events, 9.5 us)
Async XLA Ops:
  1.5 0.7 copy-start.2
  2.9 12.3 %all-to-all-start = ((bf16[4,96,256]{2,1,0:T(8,128)(2,1)}), bf16[4,96,256]{2,1,0:T(8,128)(2,1)S(1)}, u32[]{:S(2)}, u32[]{:S(2)}) async-start(bf16[4,96,256]{2,1,0:T(8,128)(2,1)} %get-tuple-element.25), calls=%async_computation | async-start | bytes 393216 | tf_op jit(solution)/shard_map/all_to_all | solution.py:214
  7.7 23.0 %collective-permute-start = (f32[96,256]{1,0:T(8,128)S(1)}, f32[96,256]{1,0:T(8,128)S(1)}, u32[]{:S(2)}, u32[]{:S(2)}) collective-permute-start(f32[96,256]{1,0:T(8,128)S(1)} %get-tuple-element.24), channel_id=1, source_target_pairs={{0,1},{1,0},{2,3},{3,2},{4,5},{5,4},{6,7},{7,6},{8,9},{9,8},{10,11... | collective-permute-start | bytes 294920 | tf_op jit(solution)/shard_map/ppermute | solution.py:213
  15.2 23.3 %collective-permute-start.1 = (bf16[4,96,256]{2,1,0:T(8,128)(2,1)S(1)}, bf16[4,96,256]{2,1,0:T(8,128)(2,1)S(1)}, u32[]{:S(2)}, u32[]{:S(2)}) collective-permute-start(bf16[4,96,256]{2,1,0:T(8,128)(2,1)S(1)} %all-to-all-done.block_ref), channel_id=1, source_target_pairs={{0,16},{8,24},{16,0},{24,8},{32,48},{40,56},{48,32},{56,40},{64,80... | collective-permute-start | bytes 589832 | tf_op jit(solution)/shard_map/ppermute | solution.py:191
  19.2 21.6 %collective-permute-start.2 = (bf16[4,96,256]{2,1,0:T(8,128)(2,1)S(1)}, bf16[4,96,256]{2,1,0:T(8,128)(2,1)S(1)}, u32[]{:S(2)}, u32[]{:S(2)}) collective-permute-start(bf16[4,96,256]{2,1,0:T(8,128)(2,1)S(1)} %all-to-all-done.block_ref), channel_id=1, source_target_pairs={{0,496},{8,504},{16,32},{24,40},{32,16},{40,24},{48,64},{56,72},{6... | collective-permute-start | bytes 589832 | tf_op jit(solution)/shard_map/ppermute | solution.py:191
  28.8 14.2 %collective-permute-start.3 = (bf16[4,96,256]{2,1,0:T(8,128)(2,1)S(1)}, bf16[4,96,256]{2,1,0:T(8,128)(2,1)S(1)}, u32[]{:S(2)}, u32[]{:S(2)}) collective-permute-start(bf16[4,96,256]{2,1,0:T(8,128)(2,1)S(1)} %all-to-all-done.block_ref), channel_id=1, source_target_pairs={{0,480},{8,40},{16,496},{24,56},{32,0},{40,72},{48,16},{56,88},{64... | collective-permute-start | bytes 589832 | tf_op jit(solution)/shard_map/ppermute | solution.py:191
  30.8 24.5 %copy-start = (f32[64,256]{1,0:T(8,128)S(1)}, f32[64,256]{1,0:T(8,128)}, u32[]{:S(2)}) copy-start(f32[64,256]{1,0:T(8,128)} %first_ref.3) | copy-start | bytes 196612
  30.8 24.5 %copy-start.1 = (f32[256]{0:T(256)S(1)}, f32[256]{0:T(256)}, u32[]{:S(2)}) copy-start(f32[256]{0:T(256)} %param.6) | copy-start | bytes 3076
  46.4 8.9 %collective-permute-start.4 = (f32[64,256]{1,0:T(8,128)S(1)}, f32[64,256]{1,0:T(8,128)S(1)}, u32[]{:S(2)}, u32[]{:S(2)}) collective-permute-start(f32[64,256]{1,0:T(8,128)S(1)} %slice.59), channel_id=1, source_target_pairs={{0,1},{1,0},{2,3},{3,2},{4,5},{5,4},{6,7},{7,6},{8,9},{9,8},{10,11... | collective-permute-start | bytes 196616 | tf_op jit(solution)/shard_map/ppermute | solution.py:205
  66.1 15.6 %collective-permute-start.5 = (f32[64,256]{1,0:T(8,128)S(1)}, f32[64,256]{1,0:T(8,128)S(1)}, u32[]{:S(2)}, u32[]{:S(2)}) collective-permute-start(f32[64,256]{1,0:T(8,128)S(1)} %get-tuple-element.36.image_ref), channel_id=1, source_target_pairs={{0,1},{1,0},{2,3},{3,2},{4,5},{5,4},{6,7},{7,6},{8,9},{9,8},{10,11... | collective-permute-start | bytes 196616 | tf_op jit(solution)/shard_map/ppermute | solution.py:244
  70.5 14.1 %collective-permute-start.6 = (bf16[4,64,256]{2,1,0:T(8,128)(2,1)S(1)}, bf16[4,64,256]{2,1,0:T(8,128)(2,1)S(1)}, u32[]{:S(2)}, u32[]{:S(2)}) collective-permute-start(bf16[4,64,256]{2,1,0:T(8,128)(2,1)S(1)} %all_to_all.20.block_ref), channel_id=1, source_target_pairs={{0,480},{8,40},{16,496},{24,56},{32,0},{40,72},{48,16},{56,88},{64... | collective-permute-start | bytes 393224 | tf_op jit(solution)/shard_map/ppermute | solution.py:191
  74.2 10.9 %collective-permute-start.7 = (bf16[4,64,256]{2,1,0:T(8,128)(2,1)S(1)}, bf16[4,64,256]{2,1,0:T(8,128)(2,1)S(1)}, u32[]{:S(2)}, u32[]{:S(2)}) collective-permute-start(bf16[4,64,256]{2,1,0:T(8,128)(2,1)S(1)} %all_to_all.20.block_ref), channel_id=1, source_target_pairs={{0,496},{8,504},{16,32},{24,40},{32,16},{40,24},{48,64},{56,72},{6... | collective-permute-start | bytes 393224 | tf_op jit(solution)/shard_map/ppermute | solution.py:191
  79.7 6.1 %collective-permute-start.8 = (bf16[4,64,256]{2,1,0:T(8,128)(2,1)S(1)}, bf16[4,64,256]{2,1,0:T(8,128)(2,1)S(1)}, u32[]{:S(2)}, u32[]{:S(2)}) collective-permute-start(bf16[4,64,256]{2,1,0:T(8,128)(2,1)S(1)} %all_to_all.20.block_ref), channel_id=1, source_target_pairs={{0,16},{8,24},{16,0},{24,8},{32,48},{40,56},{48,32},{56,40},{64,80... | collective-permute-start | bytes 393224 | tf_op jit(solution)/shard_map/ppermute | solution.py:191
  87.5 15.6 %all-to-all-start.2 = ((f32[16,4,128]{2,1,0:T(4,128)}), f32[16,4,128]{2,1,0:T(4,128)S(1)}, u32[]{:S(2)}, u32[]{:S(2)}) async-start(f32[16,4,128]{2,1,0:T(4,128)} %broadcast_in_dim.13), calls=%async_computation.2 | async-start | bytes 65536 | tf_op jit(solution)/shard_map/all_to_all | solution.py:184
  103.8 13.0 %all-to-all-start.3 = ((f32[32,4,128]{2,1,0:T(4,128)}), f32[32,4,128]{2,1,0:T(4,128)S(1)}, u32[]{:S(2)}, u32[]{:S(2)}) async-start(f32[32,4,128]{2,1,0:T(4,128)} %broadcast_in_dim.14), calls=%async_computation.3 | async-start | bytes 131072 | tf_op jit(solution)/shard_map/all_to_all | solution.py:184
  107.9 9.2 %collective-permute-start.9 = (f32[64,256]{1,0:T(8,128)S(1)}, f32[64,256]{1,0:T(8,128)S(1)}, u32[]{:S(2)}, u32[]{:S(2)}) collective-permute-start(f32[64,256]{1,0:T(8,128)S(1)} %slice.63), channel_id=1, source_target_pairs={{0,1},{1,0},{2,3},{3,2},{4,5},{5,4},{6,7},{7,6},{8,9},{9,8},{10,11... | collective-permute-start | bytes 196616 | tf_op jit(solution)/shard_map/ppermute | solution.py:205
